TPU v7x, 32 devices: a whole 2x2x4 slice. The times are simulated.
32 devices in a mesh: lat: 4 (over x, core), items: 8 (over z, y).
Axes of the slice: x: 2, y: 2, z: 4, core: 2. Of those that a mesh axis runs over, the one named last changes fastest.
Arguments:
- tokens: bfloat16 [24, 2, 8, 16, 512], P('items', None, 'lat'), may hold values from -6 to 6
- norm1_gain: bfloat16 [512], replicated, may hold values from 0.5 to 1.5
- norm1_bias: bfloat16 [512], replicated, may hold values from -1 to 1
- qkv_weight: bfloat16 [512, 1536], replicated, may hold values from -0.25 to 0.25
- qv_bias: bfloat16 [2, 512], replicated, may hold values from -1 to 1
- proj_weight: bfloat16 [512, 512], replicated, may hold values from -0.75 to 0.75
- proj_bias: bfloat16 [512], replicated, may hold values from -1 to 1
- norm2_gain: bfloat16 [512], replicated, may hold values from 0.5 to 1.5
- norm2_bias: bfloat16 [512], replicated, may hold values from -1 to 1
- fc1_weight: bfloat16 [512, 2048], replicated, may hold values from -0.25 to 0.25
- fc1_bias: bfloat16 [2048], replicated, may hold values from -1 to 1
- fc2_weight: bfloat16 [2048, 512], replicated, may hold values from -0.125 to 0.125
- fc2_bias: bfloat16 [512], replicated, may hold values from -1 to 1
- cotangent: bfloat16 [24, 2, 8, 16, 512], P('items', None, 'lat'), may hold values from -6 to 6
Outputs:
- mixed: bfloat16 [24, 2, 8, 16, 512], P('items', None, 'lat')
- tokens_grad: bfloat16 [24, 2, 8, 16, 512], P('items', None, 'lat')
- norm1_gain_grad: float32 [512], replicated
- norm1_bias_grad: float32 [512], replicated
- qkv_weight_grad: float32 [512, 1536], replicated
- qv_bias_grad: float32 [2, 512], replicated
- proj_weight_grad: float32 [512, 512], replicated
- proj_bias_grad: float32 [512], replicated
- norm2_gain_grad: float32 [512], replicated
- norm2_bias_grad: float32 [512], replicated
- fc1_weight_grad: float32 [512, 2048], replicated
- fc1_bias_grad: float32 [2048], replicated
- fc2_weight_grad: float32 [2048, 512], replicated
- fc2_bias_grad: float32 [512], replicated
All inputs are finite; a program needn't handle non-finite values.
Results may differ from a plain program's by a relative error of at most 0.012.
Values may be sent and summed in bfloat16 or wider, within the bound.
No kernel may reach another device: no remote copies, remote signals or barrier semaphores. Data moves between devices by JAX's collectives and lax.ppermute only.
A program may use at most 128 MiB of HBM per device.

v0:
```python
import jax
import jax.numpy as jnp
from jax import lax
from jax.sharding import PartitionSpec as P

HEADS = 16
HEAD_DIM = 32
STEPS = 2
LON = 16
ROW_REACH = 1
COL_REACH = 2


epsilon = 1e-06


def padded(block, sides, width):
    for axis, dim in sides:
        count = lax.axis_size(axis)
        forward = [(i, i + 1) for i in range(count - 1)]
        backward = [(target, source) for source, target in forward]
        low = lax.ppermute(
            lax.slice_in_dim(block, block.shape[dim] - width, None, axis=dim), axis, forward
        )
        high = lax.ppermute(lax.slice_in_dim(block, 0, width, axis=dim), axis, backward)
        block = jnp.concatenate([low, block, high], axis=dim)
    return block


def shifted_2(block, axis, distance):
    devices = range(lax.axis_size(axis))
    route = [(i - distance, i) for i in devices if i - distance in devices]
    return lax.ppermute(block, axis, route)


def layer_norm(values, gain_vec, shift_vec):
    average = jnp.mean(values, axis=-1, keepdims=True)
    centred = values - average
    spread = jnp.mean(centred * centred, axis=-1, keepdims=True)
    return centred * lax.rsqrt(spread + epsilon) * gain_vec + shift_vec


def gelu_exact(values):
    return jax.nn.gelu(values, approximate=False)


def contract_rows(left, right):
    return lax.dot_general(
        left, right, (((0,), (0,)), ((), ())), preferred_element_type=jnp.float32
    )


def times_transpose(left, right):
    return lax.dot_general(
        left, right, (((1,), (1,)), ((), ())), preferred_element_type=jnp.float32
    )


def band_mask(lat_index, lat_dev, lat_total):
    wide_rows = lat_dev + 2 * ROW_REACH
    query_pos = jnp.arange(STEPS * lat_dev * LON)
    key_pos = jnp.arange(STEPS * wide_rows * LON)
    query_row = lat_index * lat_dev + query_pos // LON % lat_dev
    key_row = lat_index * lat_dev + key_pos // LON % wide_rows - ROW_REACH
    col_gap = jnp.abs((query_pos % LON)[:, None] - (key_pos % LON)[None, :])
    col_gap = jnp.minimum(col_gap, LON - col_gap)
    inside = (key_row >= 0) & (key_row < lat_total)
    row_gap = jnp.abs(query_row[:, None] - key_row[None, :])
    return inside[None, :] & (row_gap <= ROW_REACH) & (col_gap <= COL_REACH)


def body(
    tokens,
    norm1_gain,
    norm1_bias,
    qkv_weight,
    qv_bias,
    proj_weight,
    proj_bias,
    norm2_gain,
    norm2_bias,
    fc1_weight,
    fc1_bias,
    fc2_weight,
    fc2_bias,
    cotangent,
):
    items_dev, steps, lat_dev, lon_count, width = tokens.shape
    row_count = items_dev * steps * lat_dev * lon_count
    block_count = 1
    wide_rows = lat_dev + 2 * ROW_REACH
    query_len = steps * lat_dev * lon_count
    key_len = steps * wide_rows * lon_count
    score_scale = HEAD_DIM ** (-0.5)
    window = band_mask(lax.axis_index("lat"), lat_dev, lat_dev * lax.axis_size("lat"))
    band_shape = (items_dev, steps, lat_dev, lon_count, width)
    wide_shape = (items_dev, steps, wide_rows, lon_count, width)

    def masked_scores(query_blk, key_blk):
        scores = (
            jnp.einsum("bqhd,bkhd->bhqk", query_blk, key_blk, preferred_element_type=jnp.float32)
            * score_scale
        )
        return jnp.where(window, scores, -1e30)

    def forward_block(inputs):
        query_blk, key_blk, value_blk = inputs
        scores = masked_scores(query_blk, key_blk)
        row_max = jnp.max(scores, axis=-1, keepdims=True)
        shifted = jnp.exp(scores - row_max)
        exp_total = jnp.sum(shifted, axis=-1, keepdims=True)
        soft_low = (shifted / exp_total).astype(jnp.bfloat16)
        result = jnp.einsum(
            "bhqk,bkhd->bqhd", soft_low, value_blk, preferred_element_type=jnp.float32
        )
        return (result.astype(jnp.bfloat16), (row_max + jnp.log(exp_total))[..., 0])

    def backward_block(inputs):
        query_blk, key_blk, value_blk, grad_blk, log_blk = inputs
        soft_weights = jnp.exp(masked_scores(query_blk, key_blk) - log_blk[..., None])
        grad_soft = jnp.einsum(
            "bqhd,bkhd->bhqk", grad_blk, value_blk, preferred_element_type=jnp.float32
        )
        inner_sum = jnp.sum(soft_weights * grad_soft, axis=-1, keepdims=True)
        grad_scores = (soft_weights * (grad_soft - inner_sum)).astype(jnp.bfloat16)
        grad_query = (
            jnp.einsum("bhqk,bkhd->bqhd", grad_scores, key_blk, preferred_element_type=jnp.float32)
            * score_scale
        )
        grad_key = (
            jnp.einsum(
                "bhqk,bqhd->bkhd", grad_scores, query_blk, preferred_element_type=jnp.float32
            )
            * score_scale
        )
        grad_value = jnp.einsum(
            "bhqk,bqhd->bkhd",
            soft_weights.astype(jnp.bfloat16),
            grad_blk,
            preferred_element_type=jnp.float32,
        )
        return (grad_query, grad_key, grad_value)

    flat_tokens = tokens.reshape(row_count, width).astype(jnp.float32)
    normed_one, norm_one_back = jax.vjp(
        layer_norm, flat_tokens, norm1_gain.astype(jnp.float32), norm1_bias.astype(jnp.float32)
    )
    normed_low = normed_one.astype(jnp.bfloat16)
    joined_qkv = jnp.dot(normed_low, qkv_weight, preferred_element_type=jnp.float32)
    query_low = (joined_qkv[:, :width] + qv_bias[0].astype(jnp.float32)).astype(jnp.bfloat16)
    key_low = joined_qkv[:, width : 2 * width].astype(jnp.bfloat16)
    value_low = (joined_qkv[:, 2 * width :] + qv_bias[1].astype(jnp.float32)).astype(jnp.bfloat16)
    pair_kv = jnp.stack([key_low.reshape(band_shape), value_low.reshape(band_shape)])
    wide_kv = padded(pair_kv, (("lat", 3),), ROW_REACH)
    query_blocks = query_low.reshape(block_count, items_dev, query_len, HEADS, HEAD_DIM)
    wide_fwd = wide_kv.reshape(2, block_count, items_dev, key_len, HEADS, HEAD_DIM)
    attended_blocks, log_totals = lax.map(forward_block, (query_blocks, wide_fwd[0], wide_fwd[1]))
    attended_low = attended_blocks.reshape(row_count, width)
    branch = jnp.dot(
        attended_low, proj_weight, preferred_element_type=jnp.float32
    ) + proj_bias.astype(jnp.float32)
    middle = flat_tokens + branch
    normed_two, norm_two_back = jax.vjp(
        layer_norm, middle, norm2_gain.astype(jnp.float32), norm2_bias.astype(jnp.float32)
    )
    normed_two_low = normed_two.astype(jnp.bfloat16)
    hidden_pre = jnp.dot(
        normed_two_low, fc1_weight, preferred_element_type=jnp.float32
    ) + fc1_bias.astype(jnp.float32)
    hidden_act, gelu_back = jax.vjp(gelu_exact, hidden_pre)
    hidden_low = hidden_act.astype(jnp.bfloat16)
    branch_two = jnp.dot(
        hidden_low, fc2_weight, preferred_element_type=jnp.float32
    ) + fc2_bias.astype(jnp.float32)
    mixed = (middle + branch_two).astype(jnp.bfloat16).reshape(band_shape)
    cot_flat = cotangent.reshape(row_count, width)
    grad_fc2 = contract_rows(hidden_low, cot_flat)
    grad_fc2_bias = jnp.sum(cot_flat.astype(jnp.float32), axis=0)
    grad_hidden = times_transpose(cot_flat, fc2_weight)
    (grad_pre,) = gelu_back(grad_hidden)
    grad_pre_low = grad_pre.astype(jnp.bfloat16)
    grad_fc1 = contract_rows(normed_two_low, grad_pre_low)
    grad_fc1_bias = jnp.sum(grad_pre_low.astype(jnp.float32), axis=0)
    grad_normed_two = times_transpose(grad_pre_low, fc1_weight)
    grad_mid_norm, grad_gain_two, grad_bias_two = norm_two_back(grad_normed_two)
    grad_middle = cot_flat.astype(jnp.float32) + grad_mid_norm
    mlp_terms = (grad_gain_two, grad_bias_two, grad_fc1, grad_fc1_bias, grad_fc2, grad_fc2_bias)
    mlp_terms = lax.psum(
        (mlp_terms[0], mlp_terms[1], mlp_terms[2], mlp_terms[3], mlp_terms[4], mlp_terms[5]),
        ("lat", "items"),
    )
    grad_branch_low = grad_middle.astype(jnp.bfloat16)
    grad_proj = contract_rows(attended_low, grad_branch_low)
    grad_proj_bias = jnp.sum(grad_branch_low.astype(jnp.float32), axis=0)
    grad_attended_low = times_transpose(grad_branch_low, proj_weight).astype(jnp.bfloat16)
    grad_blocks = grad_attended_low.reshape(block_count, items_dev, query_len, HEADS, HEAD_DIM)
    grad_q_blocks, grad_k_blocks, grad_v_blocks = lax.map(
        backward_block, (query_blocks, wide_fwd[0], wide_fwd[1], grad_blocks, log_totals)
    )
    kv_grads = jnp.stack([grad_k_blocks.reshape(wide_shape), grad_v_blocks.reshape(wide_shape)])
    to_lower = kv_grads[:, :, :, :ROW_REACH]
    to_upper = kv_grads[:, :, :, wide_rows - ROW_REACH :]
    from_above = shifted_2(to_lower.astype(jnp.bfloat16), "lat", -1).astype(to_lower.dtype)
    from_below = shifted_2(to_upper.astype(jnp.bfloat16), "lat", 1).astype(to_upper.dtype)
    own_grads = kv_grads[:, :, :, ROW_REACH : ROW_REACH + lat_dev]
    own_grads = own_grads.at[:, :, :, :ROW_REACH].add(from_below)
    own_grads = own_grads.at[:, :, :, lat_dev - ROW_REACH :].add(from_above)
    query_grad_low = grad_q_blocks.reshape(row_count, width).astype(jnp.bfloat16)
    key_grad_low = own_grads[0].reshape(row_count, width).astype(jnp.bfloat16)
    value_grad_low = own_grads[1].reshape(row_count, width).astype(jnp.bfloat16)
    grad_joined_low = jnp.concatenate([query_grad_low, key_grad_low, value_grad_low], axis=1)
    grad_qkv = contract_rows(normed_low, grad_joined_low)
    grad_qv_bias = jnp.stack(
        [
            jnp.sum(query_grad_low.astype(jnp.float32), axis=0),
            jnp.sum(value_grad_low.astype(jnp.float32), axis=0),
        ]
    )
    grad_normed_one = times_transpose(grad_joined_low, qkv_weight)
    grad_in_norm, grad_gain_one, grad_bias_one = norm_one_back(grad_normed_one)
    tokens_grad = (grad_middle + grad_in_norm).astype(jnp.bfloat16).reshape(band_shape)
    attn_terms = (grad_gain_one, grad_bias_one, grad_qkv, grad_qv_bias, grad_proj, grad_proj_bias)
    attn_terms = lax.psum(
        (attn_terms[0], attn_terms[1], attn_terms[2], attn_terms[3], attn_terms[4], attn_terms[5]),
        ("lat", "items"),
    )
    return (
        mixed,
        tokens_grad,
        attn_terms[0],
        attn_terms[1],
        attn_terms[2],
        attn_terms[3],
        attn_terms[4],
        attn_terms[5],
        mlp_terms[0],
        mlp_terms[1],
        mlp_terms[2],
        mlp_terms[3],
        mlp_terms[4],
        mlp_terms[5],
    )


def solution(mesh):
    placed = (
        P("items", None, "lat", None, None),
        P(),
        P(),
        P(),
        P(),
        P(),
        P(),
        P(),
        P(),
        P(),
        P(),
        P(),
        P(),
        P("items", None, "lat", None, None),
    )
    return jax.shard_map(
        body,
        mesh=mesh,
        in_specs=placed,
        out_specs=(
            P("items", None, "lat", None, None),
            P("items", None, "lat", None, None),
            P(),
            P(),
            P(),
            P(),
            P(),
            P(),
            P(),
            P(),
            P(),
            P(),
            P(),
            P(),
        ),
        check_vma=False,
    )
```

profile of v0, /device:TPU:0, one launch (start us, length us, event | category | flops | bytes accessed | tf_op | source)
XLA Modules:
  0.0 365.5 jit_solution(4617219332563700692)
XLA Ops:
  7.2 1.2 convert_reduce_fusion.5
  8.5 1.1 multiply_reduce_fusion.6
  11.9 1.1 add_convert_fusion.3
  13.0 2.0 fusion.43
  16.6 3.0 collective-permute-start
  19.6 1.3 collective-permute-start.1
  22.3 2.4 collective-permute-done.1
  24.7 1.2 pad_maximum_fusion
  26.0 2.0 squeeze.37
  28.0 1.9 copy.36
  29.9 2.0 squeeze.35
  31.9 1.9 copy.37
  35.6 1.2 fusion.9
  36.9 1.1 copy.38
  38.0 1.5 reshape.330
  39.5 1.5 fusion.42
  41.3 2.3 convolution_add_fusion
  43.6 5.1 %convert_reduce_fusion = (f32[2048]{0:T(1024)S(1)}, bf16[192,2048]{1,0:T(8,128)(2,1)S(1)}, f32[192,2048]{1,0:T(8,128)}) fusion(f32[192,2048]{1,0:T(8,128)S(1)} %convolution_add_fusion, bf16[192,512]{1,0:T(8,128)(2,1)S(1)} %bitcast.70, bf16[2048,512]{1,0:T(8,128)(2,1)S(1)} %copy-done), kind=kOutput, calls=%fused_computation.3 | convolution fusion | flops 431749120 | bytes 6234112 | tf_op jit(solution)/shard_map/dot_general | solution.py:54
  51.8 2.3 reshape.338
  54.1 2.5 copy.40
  56.6 3.2 convolution_bitcast_fusion
  59.7 1.5 multiply_reduce_fusion
  62.2 1.3 convert_reduce_fusion.1
  63.5 1.2 fusion.7
  64.7 3.1 copy.45
  67.9 2.7 stack_reshape.14
  71.5 3.1 copy.47
  74.6 2.7 stack_reshape.15
  78.2 2.6 convert.14
  81.7 2.9 fusion.35
  85.6 1.1 copy.43
  86.7 2.1 convert_element_type.163
  88.8 1.0 fusion.39
  89.9 1.3 collective-permute-start.3
  91.2 6.8 %collective-permute-start.2 = (bf16[2,3,2,1,16,512]{5,4,3,2,1,0:T(8,128)(2,1)S(1)}, bf16[2,3,2,1,16,512]{5,4,3,2,1,0:T(8,128)(2,1)S(1)}, u32[]{:S(2)}, u32[]{:S(2)}) collective-permute-start(bf16[2,3,2,1,16,512]{5,4,3,2,1,0:T(8,128)(2,1)S(1)} %get-tuple-element.119), channel_id=1, source_target_pairs={{0,8},{8,16},{16,24},{1,9},{9,17},{17,25},{2,10},{10,18},{18,26},{... | collective-permute-start | bytes 589832 | tf_op jit(solution)/shard_map/ppermute | solution.py:33
  98.0 3.7 %fusion.45 = f32[2048,512]{1,0:T(8,128)} fusion(bf16[192,2048]{1,0:T(8,128)(2,1)S(1)} %multiply_convert_fusion.1, bf16[192,512]{1,0:T(8,128)(2,1)} %bitcast.69), kind=kOutput, calls=%fused_computation.130 | convolution fusion | flops 402653184 | bytes 5177344 | tf_op jit(solution)/shard_map/dot_general | solution.py:48
  101.7 1.3 fusion.44
  103.0 1.1 fusion.17
  105.6 1.8 copy.48
  107.4 1.8 copy.49
  109.1 3.5 fusion.20
  114.4 1.3 fusion.13
  117.2 43.1 %all-reduce = (f32[512]{0:T(512)}, f32[512]{0:T(512)}, f32[2,512]{1,0:T(2,128)}, f32[512]{0:T(512)}, f32[512]{0:T(512)}, /*index=5*/f32[512]{0:T(512)}, f32[2048]{0:T(1024)}, f32[512]{0:T(512)}) all-reduce(f32[512]{0:T(512)S(1)} %get-tuple-element.91, ...), channel_id=1, replica_groups=mesh['lat'=4,'items'=8] {'lat','items'}, use_global_device_ids=true, to_apply=%region_12.13 | all-reduce | flops 6144 | bytes 49152 | tf_op jit(solution)/shard_map/psum | solution.py:223
  161.1 186.9 %all-reduce.4.cloned.1.call-done = (f32[512,1536]{1,0:T(8,128)}, f32[512,512]{1,0:T(8,128)}, f32[512,2048]{1,0:T(8,128)}, f32[2048,512]{1,0:T(8,128)}) async-done(((f32[512,1536]{1,0:T(8,128)}, f32[512,512]{1,0:T(8,128)}, f32[512,2048]{1,0:T(8,128)}, f32[2048,512]{1,0:T(8,128)}), (f32[512,1536]{1,0:T(8,128)}, f32[512,512]{1,0:T(8,128)}, f32[512,2048]{1,0:T(8,128)}, ...) | async-done | bytes 12582928 | tf_op jit(solution)/shard_map/psum | solution.py:223
  348.0 3.9 %copy.61 = f32[512,1536]{1,0:T(8,128)} copy(f32[512,1536]{1,0:T(8,128)} %get-tuple-element.144) | data formatting | bytes 6291456
  352.9 2.1 copy.63
  355.1 1.6 copy-done.7
  356.6 2.0 copy.64
  (139 shorter events, 21.7 us)
Async XLA Ops:
  7.2 36.4 %copy-start = (bf16[2048,512]{1,0:T(8,128)(2,1)S(1)}, bf16[2048,512]{1,0:T(8,128)(2,1)}, u32[]{:S(2)}) copy-start(bf16[2048,512]{1,0:T(8,128)(2,1)} %param.29) | copy-start | bytes 6291460
  7.2 340.8 %all-reduce.4.cloned.1.call-start = ((), (), s32[]{:S(2)}) async-start(), calls=%async_computation | async-start | bytes 25165824 | tf_op jit(solution)/shard_map/psum | solution.py:223
  13.0 2.1 copy-start.21
  14.9 6.0 %copy-start.37 = (bf16[512]{0:T(512)(128)(2,1)S(1)}, bf16[512]{0:T(512)(128)(2,1)}, u32[]{:S(2)}) copy-start(bf16[512]{0:T(512)(128)(2,1)} %param.25) | copy-start | bytes 3076
  15.0 6.0 %copy-start.38 = (bf16[512]{0:T(512)(128)(2,1)S(1)}, bf16[512]{0:T(512)(128)(2,1)}, u32[]{:S(2)}) copy-start(bf16[512]{0:T(512)(128)(2,1)} %param.26) | copy-start | bytes 3076
  15.0 6.0 %copy-start.39 = (bf16[512]{0:T(512)(128)(2,1)S(1)}, bf16[512]{0:T(512)(128)(2,1)}, u32[]{:S(2)}) copy-start(bf16[512]{0:T(512)(128)(2,1)} %param.24) | copy-start | bytes 3076
  15.0 6.1 %copy-start.36 = (bf16[2048]{0:T(1024)(128)(2,1)S(1)}, bf16[2048]{0:T(1024)(128)(2,1)}, u32[]{:S(2)}) copy-start(bf16[2048]{0:T(1024)(128)(2,1)} %param.28) | copy-start | bytes 12292
  15.1 0.7 copy-start.22
  16.6 5.7 %collective-permute-start = (bf16[2,3,2,1,16,512]{5,4,3,2,1,0:T(8,128)(2,1)}, bf16[2,3,2,1,16,512]{5,4,3,2,1,0:T(8,128)(2,1)}, u32[]{:S(2)}, u32[]{:S(2)}) collective-permute-start(bf16[2,3,2,1,16,512]{5,4,3,2,1,0:T(8,128)(2,1)} %get-tuple-element.122), channel_id=1, source_target_pairs={{0,8},{8,16},{16,24},{1,9},{9,17},{17,25},{2,10},{10,18},{18,26},{... | collective-permute-start | bytes 589832 | tf_op jit(solution)/shard_map/ppermute | solution.py:22
  19.6 5.1 %collective-permute-start.1 = (bf16[2,3,2,1,16,512]{5,4,3,2,1,0:T(8,128)(2,1)}, bf16[2,3,2,1,16,512]{5,4,3,2,1,0:T(8,128)(2,1)}, u32[]{:S(2)}, u32[]{:S(2)}) collective-permute-start(bf16[2,3,2,1,16,512]{5,4,3,2,1,0:T(8,128)(2,1)} %get-tuple-element.123), channel_id=1, source_target_pairs={{8,0},{16,8},{24,16},{9,1},{17,9},{25,17},{10,2},{18,10},{26,18},{... | collective-permute-start | bytes 589832 | tf_op jit(solution)/shard_map/ppermute | solution.py:25
  29.9 3.9 %copy-start.11 = (bf16[3,128,16,32]{1,3,2,0:T(8,128)(2,1)}, bf16[3,128,16,32]{1,3,2,0:T(8,128)(2,1)S(1)}, u32[]{:S(2)}) copy-start(bf16[3,128,16,32]{1,3,2,0:T(8,128)(2,1)S(1)} %copy.36) | copy-start | bytes 1179652
  33.9 1.7 copy-start.28
  34.7 2.2 copy-start.1
  36.8 2.7 copy-start.6
  39.5 4.1 %copy-start.17 = (bf16[192,512]{0,1:T(8,128)(2,1)}, bf16[192,512]{0,1:T(8,128)(2,1)S(1)}, u32[]{:S(2)}) copy-start(bf16[192,512]{0,1:T(8,128)(2,1)S(1)} %reshape.330) | copy-start | bytes 589828
  41.3 2.3 copy-start.14
  43.6 5.1 %copy-start.4 = (f32[192,2048]{1,0:T(8,128)}, f32[192,2048]{1,0:T(8,128)S(1)}, u32[]{:S(2)}) copy-start(f32[192,2048]{1,0:T(8,128)S(1)} %convolution_add_fusion) | copy-start | bytes 4718596
  43.6 5.1 %copy-start.20 = (bf16[512,2048]{1,0:T(8,128)(2,1)S(1)}, bf16[512,2048]{1,0:T(8,128)(2,1)}, u32[]{:S(2)}) copy-start(bf16[512,2048]{1,0:T(8,128)(2,1)} %param.27) | copy-start | bytes 6291460
  48.7 1.0 copy-start.34
  49.7 1.1 copy-start.19
  50.0 6.6 %copy-start.9 = (f32[192,512]{1,0:T(8,128)}, f32[192,512]{1,0:T(8,128)S(1)}, u32[]{:S(2)}) copy-start(f32[192,512]{1,0:T(8,128)S(1)} %get-tuple-element.115) | copy-start | bytes 1179652
  50.1 0.7 copy-start.23
  56.6 3.2 copy-start.2
  56.6 3.2 copy-start.13
  56.6 3.2 copy-start.29
  61.2 1.0 copy-start.12
  78.2 2.6 copy-start.3
  78.2 3.5 copy-start.35
  81.7 2.9 copy-start.5
  81.7 2.9 copy-start.27
  84.6 1.0 copy-start.26
  89.9 14.2 %collective-permute-start.3 = (bf16[2,3,2,1,16,512]{5,4,3,2,1,0:T(8,128)(2,1)S(1)}, bf16[2,3,2,1,16,512]{5,4,3,2,1,0:T(8,128)(2,1)S(1)}, u32[]{:S(2)}, u32[]{:S(2)}) collective-permute-start(bf16[2,3,2,1,16,512]{5,4,3,2,1,0:T(8,128)(2,1)S(1)} %get-tuple-element.118), channel_id=1, source_target_pairs={{8,0},{16,8},{24,16},{9,1},{17,9},{25,17},{10,2},{18,10},{26,18},{... | collective-permute-start | bytes 589832 | tf_op jit(solution)/shard_map/ppermute | solution.py:33
  91.2 10.5 %copy-start.18 = (bf16[192,512]{0,1:T(8,128)(2,1)S(1)}, bf16[192,512]{0,1:T(8,128)(2,1)}, u32[]{:S(2)}) copy-start(bf16[192,512]{0,1:T(8,128)(2,1)} %copy-done.17) | copy-start | bytes 589828
  91.2 10.5 %copy-start.24 = (bf16[192,512]{1,0:T(8,128)(2,1)S(1)}, bf16[192,512]{1,0:T(8,128)(2,1)}, u32[]{:S(2)}) copy-start(bf16[192,512]{1,0:T(8,128)(2,1)} %copy-done.23) | copy-start | bytes 589828
  91.2 11.8 %copy-start.16 = (f32[2,3,2,2,16,512]{5,4,3,2,1,0:T(8,128)S(1)}, f32[2,3,2,2,16,512]{5,4,3,2,1,0:T(8,128)}, u32[]{:S(2)}) copy-start(f32[2,3,2,2,16,512]{5,4,3,2,1,0:T(8,128)} %slice.152) | copy-start | bytes 2359300
  91.2 11.8 %collective-permute-start.2 = (bf16[2,3,2,1,16,512]{5,4,3,2,1,0:T(8,128)(2,1)S(1)}, bf16[2,3,2,1,16,512]{5,4,3,2,1,0:T(8,128)(2,1)S(1)}, u32[]{:S(2)}, u32[]{:S(2)}) collective-permute-start(bf16[2,3,2,1,16,512]{5,4,3,2,1,0:T(8,128)(2,1)S(1)} %get-tuple-element.119), channel_id=1, source_target_pairs={{0,8},{8,16},{16,24},{1,9},{9,17},{17,25},{2,10},{10,18},{18,26},{... | collective-permute-start | bytes 589832 | tf_op jit(solution)/shard_map/ppermute | solution.py:33
  112.6 0.7 copy-start.40
  114.4 1.4 copy-start.25
  114.4 1.4 copy-start.30
  114.4 1.5 copy-start.31
  114.4 1.6 copy-start.32
  116.8 43.4 %copy-start.10 = (f32[192,512]{1,0:T(8,128)S(1)}, f32[192,512]{1,0:T(8,128)}, u32[]{:S(2)}) copy-start(f32[192,512]{1,0:T(8,128)} %copy-done.9) | copy-start | bytes 1179652
  116.8 43.4 %copy-start.15 = (bf16[3,2,2,16,512]{4,3,2,1,0:T(8,128)(2,1)S(1)}, bf16[3,2,2,16,512]{4,3,2,1,0:T(8,128)(2,1)}, u32[]{:S(2)}) copy-start(bf16[3,2,2,16,512]{4,3,2,1,0:T(8,128)(2,1)} %param.31) | copy-start | bytes 589828
  348.0 3.9 %copy-start.33 = (f32[512,512]{1,0:T(8,128)S(1)}, f32[512,512]{1,0:T(8,128)}, u32[]{:S(2)}) copy-start(f32[512,512]{1,0:T(8,128)} %get-tuple-element.146) | copy-start | bytes 3145732
  348.0 4.9 %copy-start.8 = (f32[512,2048]{1,0:T(8,128)S(1)}, f32[512,2048]{1,0:T(8,128)}, u32[]{:S(2)}) copy-start(f32[512,2048]{1,0:T(8,128)} %get-tuple-element.150) | copy-start | bytes 12582916
  352.9 3.7 %copy-start.7 = (f32[2048,512]{1,0:T(8,128)S(1)}, f32[2048,512]{1,0:T(8,128)}, u32[]{:S(2)}) copy-start(f32[2048,512]{1,0:T(8,128)} %get-tuple-element.152) | copy-start | bytes 12582916
Sparse Core Ops, SparseCore 0:
  112.8 235.1 all-reduce.3
where the time goes:
time: 367 us; the launch traced here: 365 us
  waiting for transfers between devices  189 us (51%)
  local copies, waits for them, and re-layouts  53.5 us (15%)
  blocking collectives  43.1 us (12%)
  matrix products  35.3 us (10%)
  other arithmetic  17 us (5%)
  between operations  14.7 us (4%)
  starting transfers between devices  12.5 us (3%)
    psum x1, waiting for transfers between devices, body(): lax.psum((attn_terms[0], attn_terms[1], attn_terms[2], attn_terms[3], att...  187 us
    psum x1, blocking collectives, body(): lax.psum((attn_terms[0], attn_terms[1], attn_terms[2], attn_terms[3], att...  43.1 us
    unnamed x87, local copies, waits for them, and re-layouts  14.9 us
    squeeze x8, local copies, waits for them, and re-layouts, body(): lax.map(forward_block, (query_blocks, wide_fwd[0], wide_fwd[1]))  13.6 us
    dot_general x4, matrix products, contract_rows(): lax.dot_general(left, right, (((0,), (0,)), ((), ())), preferred_element_...  11.3 us
    ppermute x2, starting transfers between devices, shifted_2(): return lax.ppermute(block, axis, route)  8.09 us
    dot_general x4, matrix products, times_transpose(): lax.dot_general(left, right, (((1,), (1,)), ((), ())), preferred_element_...  7.89 us
  transfers between devices with their start and end apart: 5, of which 2 were waited for; matrix products, arithmetic and copies ran while one was open for 3% of the time, Pallas kernels for 0%

commit v1 on v0

v1 whole, which is shorter than its diff:
```python
import functools
import math

import jax
import jax.numpy as jnp
from jax import lax
from jax.experimental import pallas as pl
from jax.experimental.pallas import tpu as pltpu
from jax.sharding import PartitionSpec as P

HEAD_DIM = 32
ROW_REACH = 1
COL_REACH = 2
GROUP = 128 // HEAD_DIM
EPSILON = 1e-06
SCALE = HEAD_DIM ** (-0.5)
SQRT_HALF = 0.5**0.5
PHI_SCALE = (2.0 * math.pi) ** (-0.5)
NEGATIVE = -1e30

f32 = jnp.float32
bf16 = jnp.bfloat16
MIB = 1024 * 1024


def dot_nn(left, right):
    return lax.dot_general(left, right, (((1,), (0,)), ((), ())), preferred_element_type=f32)


def dot_nt(left, right):
    return lax.dot_general(left, right, (((1,), (1,)), ((), ())), preferred_element_type=f32)


def dot_tn(left, right):
    return lax.dot_general(left, right, (((0,), (0,)), ((), ())), preferred_element_type=f32)


def normed(values):
    mean = jnp.mean(values, axis=-1, keepdims=True)
    centred = values - mean
    spread = jnp.mean(centred * centred, axis=-1, keepdims=True)
    scale = lax.rsqrt(spread + EPSILON)
    return centred * scale, scale


def norm_back(grad, gain, unit, scale):
    scaled = grad * gain
    first = jnp.mean(scaled, axis=-1, keepdims=True)
    second = jnp.mean(scaled * unit, axis=-1, keepdims=True)
    return scale * (scaled - first - unit * second)


def stack_heads(block, lane_head):
    zero = jnp.zeros_like(block)
    return jnp.concatenate(
        [jnp.where(lane_head == head, block, zero) for head in range(GROUP)], axis=0
    )


def fold_heads(stacked, lane_head, rows):
    total = jnp.where(lane_head == 0, stacked[:rows], 0.0)
    for head in range(1, GROUP):
        total = jnp.where(lane_head == head, stacked[head * rows : (head + 1) * rows], total)
    return total


def block_kernel(
    items,
    tok,
    low,
    high,
    cot,
    vecs,
    wqkv,
    wproj,
    w1,
    w2,
    mask,
    mixed_out,
    a_out,
    o_out,
    c_out,
    g_out,
    du_out,
    dy_out,
    dx1_out,
    dq_out,
    dk_out,
    dv_out,
    to_low,
    to_high,
    small_out,
    kv_ref,
    q_ref,
    p_ref,
    do_ref,
):
    rows, width = tok.shape
    hidden = w1.shape[1]
    side = low.shape[0]
    band = rows // items
    edge = side // items
    groups = width // 128
    lane_head = lax.broadcasted_iota(jnp.int32, (1, 128), 1) // HEAD_DIM

    def vec(index):
        return vecs[index : index + 1, :]

    x = tok[...].astype(f32)
    unit, _ = normed(x)
    a_own = (unit * vec(0) + vec(1)).astype(bf16)
    a_out[...] = a_own
    wide = jnp.concatenate([low[...], high[...]], axis=0).astype(f32)
    unit_wide, _ = normed(wide)
    a_wide = (unit_wide * vec(0) + vec(1)).astype(bf16)
    a_all = jnp.concatenate([a_own, a_wide], axis=0)
    q_ref[...] = (dot_nn(a_own, wqkv[:, :width]) + vec(2)).astype(bf16)
    kv_ref[0] = dot_nn(a_all, wqkv[:, width : 2 * width]).astype(bf16)
    kv_ref[1] = (dot_nn(a_all, wqkv[:, 2 * width :]) + vec(3)).astype(bf16)

    window = jnp.concatenate([mask[...]] * GROUP, axis=0)

    def keys_of(which, item, lanes):
        return jnp.concatenate(
            [
                kv_ref[which, item * band : (item + 1) * band, lanes],
                kv_ref[which, rows + item * edge : rows + (item + 1) * edge, lanes],
                kv_ref[which, rows + side + item * edge : rows + side + (item + 1) * edge, lanes],
            ],
            axis=0,
        )

    for item in range(items):
        for group in range(groups):
            lanes = slice(group * 128, (group + 1) * 128)
            own = slice(item * band, (item + 1) * band)
            queries = stack_heads(q_ref[own, lanes], lane_head)
            scores = dot_nt(queries, keys_of(0, item, lanes)) * SCALE + window
            top = jnp.max(scores, axis=-1, keepdims=True)
            weights = jnp.exp(scores - top)
            total = jnp.sum(weights, axis=-1, keepdims=True)
            soft = weights * (1.0 / total)
            p_ref[item * groups + group] = soft
            mixed_heads = dot_nn(soft.astype(bf16), keys_of(1, item, lanes))
            o_out[own, lanes] = fold_heads(mixed_heads, lane_head, band).astype(bf16)

    x1 = x + dot_nn(o_out[...], wproj[...]) + vec(4)
    unit2, scale2 = normed(x1)
    c_low = (unit2 * vec(5) + vec(6)).astype(bf16)
    c_out[...] = c_low
    cot_low = cot[...]
    branch = jnp.zeros((rows, width), f32)
    dc = jnp.zeros((rows, width), f32)
    for part in range(hidden // width):
        cols = slice(part * width, (part + 1) * width)
        u = dot_nn(c_low, w1[:, cols]) + vec(8 + part)
        cdf = 0.5 + 0.5 * lax.erf(u * SQRT_HALF)
        slope = cdf + u * (jnp.exp(u * u * -0.5) * PHI_SCALE)
        act = (u * cdf).astype(bf16)
        g_out[:, cols] = act
        branch = branch + dot_nn(act, w2[cols, :])
        dh = dot_nt(cot_low, w2[cols, :])
        du_low = (dh * slope).astype(bf16)
        du_out[:, cols] = du_low
        small_out[4 + part : 5 + part, :] = jnp.sum(du_low.astype(f32), axis=0, keepdims=True)
        dc = dc + dot_nt(du_low, w1[:, cols])
    mixed_out[...] = (x1 + branch + vec(7)).astype(bf16)
    cot_wide = cot_low.astype(f32)
    small_out[0:1, :] = jnp.sum(dc * unit2, axis=0, keepdims=True)
    small_out[1:2, :] = jnp.sum(dc, axis=0, keepdims=True)
    small_out[2:3, :] = jnp.sum(cot_wide, axis=0, keepdims=True)
    dx1 = cot_wide + norm_back(dc, vec(5), unit2, scale2)
    dx1_out[...] = dx1
    dy = dx1.astype(bf16)
    dy_out[...] = dy
    small_out[3:4, :] = jnp.sum(dy.astype(f32), axis=0, keepdims=True)
    do_ref[...] = dot_nt(dy, wproj[...]).astype(bf16)

    for item in range(items):
        for group in range(groups):
            lanes = slice(group * 128, (group + 1) * 128)
            own = slice(item * band, (item + 1) * band)
            ends = slice(item * edge, (item + 1) * edge)
            grads = stack_heads(do_ref[own, lanes], lane_head)
            queries = stack_heads(q_ref[own, lanes], lane_head)
            soft = p_ref[item * groups + group]
            dp = dot_nt(grads, keys_of(1, item, lanes))
            inner = jnp.sum(soft * dp, axis=-1, keepdims=True)
            ds = (soft * (dp - inner)).astype(bf16)
            dq = fold_heads(dot_nn(ds, keys_of(0, item, lanes)), lane_head, band) * SCALE
            dq_out[own, lanes] = dq.astype(bf16)
            dk = dot_tn(ds, queries) * SCALE
            dv = dot_tn(soft.astype(bf16), grads)
            dk_out[own, lanes] = dk[:band]
            dv_out[own, lanes] = dv[:band]
            to_low[0, ends, lanes] = dk[band : band + edge].astype(bf16)
            to_low[1, ends, lanes] = dv[band : band + edge].astype(bf16)
            to_high[0, ends, lanes] = dk[band + edge :].astype(bf16)
            to_high[1, ends, lanes] = dv[band + edge :].astype(bf16)


def grad_halves(place, slot_index, shards, left, right, keep, send, lanes=slice(None)):
    half = left.shape[1] // 2
    per = half // shards
    step = min(half, 256)
    core = place[0]
    slot = place[slot_index]
    values = right[...]
    for ref, owner in ((keep, core), (send, 1 - core)):
        for start in range(0, half, step):
            columns = pl.ds(pl.multiple_of(owner * half + start, 128), step)
            product = dot_tn(left[:, columns], values)
            for index in range(step // per):
                spot = pl.multiple_of(((start // per + index) ^ slot) * per, per)
                ref[pl.ds(spot, per), lanes] = product[index * per : (index + 1) * per].astype(bf16)


def mlp_grad_kernel(shards, place, g, cot, c, du, o, dy, keep1, send1, keep2, send2):
    hidden = du.shape[1]
    grad_halves(place, 1, shards, g, cot, keep1, send1)
    grad_halves(place, 2, shards, c, du, keep2, send2, slice(0, hidden))
    grad_halves(place, 2, shards, o, dy, keep2, send2, slice(hidden, hidden + dy.shape[1]))


def qkv_grad_kernel(
    shards,
    lat_dev,
    lon,
    place,
    dq,
    dk,
    dv,
    from_below,
    from_above,
    a_low,
    tok,
    vecs,
    dx1,
    wqkv,
    small_in,
    keep,
    send,
    tokens_out,
    small_out,
    joined,
):
    rows, width = tok.shape
    joined[:, :width] = dq[...]
    for which, grads in ((0, dk), (1, dv)):
        columns = slice((1 + which) * width, (2 + which) * width)
        for strip in range(rows // (lat_dev * lon)):
            edge = slice(strip * lon, (strip + 1) * lon)
            for row in range(lat_dev):
                start = (strip * lat_dev + row) * lon
                value = grads[start : start + lon, :]
                if row == 0:
                    value = value + from_below[which, edge, :].astype(f32)
                if row == lat_dev - 1:
                    value = value + from_above[which, edge, :].astype(f32)
                joined[start : start + lon, columns] = value.astype(bf16)
    grad_halves(place, 3, shards, a_low, joined, keep, send)
    da = dot_nt(joined[...], wqkv[...])
    unit, scale = normed(tok[...].astype(f32))
    grad = dx1[...] + norm_back(da, vecs[0:1, :], unit, scale)
    tokens_out[...] = grad.astype(bf16)
    sums = [
        jnp.sum(da * unit, axis=0, keepdims=True),
        jnp.sum(da, axis=0, keepdims=True),
        jnp.sum(joined[:, :width].astype(f32), axis=0, keepdims=True),
        jnp.sum(joined[:, 2 * width :].astype(f32), axis=0, keepdims=True),
    ] + [small_in[index : index + 1, :] for index in range(small_in.shape[0])]
    for index, row in enumerate(sums):
        place_of = slice(index % 3 * width, (index % 3 + 1) * width)
        small_out[index // 3 : index // 3 + 1, place_of] = row.astype(bf16)


def spread_kernel(slot_index, shards, splits, place, own, other, *outs):
    half = own.shape[0]
    per = half // shards
    core = place[0]
    slot = place[slot_index]
    for ref, owner in ((own, core), (other, 1 - core)):
        for index in range(shards):
            spot = pl.multiple_of(owner * half + (index ^ slot) * per, per)
            first = 0
            for out, count in zip(outs, splits):
                out[pl.ds(spot, per), :] = ref[
                    index * per : (index + 1) * per, first : first + count
                ].astype(f32)
                first += count


def on_device(kernel, outs, scratch=(), scalars=0, args=0, vmem=24):
    return pl.pallas_call(
        kernel,
        out_shape=[jax.ShapeDtypeStruct(shape, dtype) for shape, dtype in outs],
        in_specs=[pl.BlockSpec(memory_space=pltpu.SMEM)] * scalars
        + [pl.BlockSpec(memory_space=pltpu.VMEM)] * args,
        out_specs=[pl.BlockSpec(memory_space=pltpu.VMEM)] * len(outs),
        scratch_shapes=list(scratch),
        compiler_params=pltpu.CompilerParams(vmem_limit_bytes=vmem * MIB),
    )


class Axes:
    def __init__(self, mesh):
        self.sizes = dict(mesh.shape)
        bits = self.sizes["items"].bit_length() - 1
        self.core = ("lat", 1)
        chips = ("lat", 2)
        first = ("items", 1)
        second = ("items", 2)
        self.doubled = [("items", 1 << bit) for bit in range(2, bits)]
        self.orders = (
            (chips, first, second),
            (first, second, chips),
            (second, chips, first),
        )

    def bit(self, dim):
        axis, value = dim
        return (lax.axis_index(axis) // value) % 2

    def slot(self, order):
        total = 0
        for dim in order:
            total = total * 2 + self.bit(dim)
        return total

    def exchange(self, value, dim):
        axis, bit = dim
        pairs = [(index, index ^ bit) for index in range(self.sizes[axis])]
        return lax.ppermute(value, axis, pairs)


def add_rows(terms, low, high):
    total = terms[0][low:high].astype(f32)
    for term in terms[1:]:
        total = total + term[low:high].astype(f32)
    return total


def reduce_stream(axes, keep, send, order, small=None):
    terms = [keep, axes.exchange(send, axes.core)]
    if small is not None:
        small = small.astype(f32) + axes.exchange(small, axes.core).astype(f32)
    rows = keep.shape[0]
    extra = 0 if small is None else small.shape[0]

    def swap(value, dim, small):
        if small is None:
            return axes.exchange(value, dim), None
        small_low = small.astype(bf16)
        count = value.shape[0]
        got = axes.exchange(jnp.concatenate([value, small_low], axis=0), dim)
        return got[:count], small_low.astype(f32) + got[count : count + extra].astype(f32)

    for dim in order:
        rows //= 2
        got, small = swap(add_rows(terms, rows, 2 * rows).astype(bf16), dim, small)
        terms.append(got)
    piece = add_rows(terms, 0, rows).astype(bf16)
    for dim in axes.doubled:
        got, small = swap(piece, dim, small)
        piece = (piece.astype(f32) + got.astype(f32)).astype(bf16)
    return piece, small


def gather_stream(axes, piece, order):
    for dim in reversed(order):
        piece = jnp.concatenate([piece, axes.exchange(piece, dim)], axis=0)
    return piece, axes.exchange(piece, axes.core)


def window_mask(lat_index, lat_total, lat_dev, steps, lon):
    query = jnp.arange(steps * lat_dev * lon)
    query_row = query // lon % lat_dev
    query_col = query % lon
    side = jnp.arange(steps * lon)
    key_row = jnp.concatenate(
        [query_row, jnp.full_like(side, -1), jnp.full_like(side, lat_dev)]
    )
    key_col = jnp.concatenate([query_col, side % lon, side % lon])
    gap = jnp.abs(query_col[:, None] - key_col[None, :])
    gap = jnp.minimum(gap, lon - gap)
    near = jnp.abs(query_row[:, None] - key_row[None, :]) <= ROW_REACH
    world_row = lat_index * lat_dev + key_row
    inside = (world_row >= 0) & (world_row < lat_total * lat_dev)
    return jnp.where(near & (gap <= COL_REACH) & inside[None, :], 0.0, NEGATIVE).astype(f32)


def body(
    axes,
    tokens,
    norm1_gain,
    norm1_bias,
    qkv_weight,
    qv_bias,
    proj_weight,
    proj_bias,
    norm2_gain,
    norm2_bias,
    fc1_weight,
    fc1_bias,
    fc2_weight,
    fc2_bias,
    cotangent,
):
    items, steps, lat_dev, lon, width = tokens.shape
    hidden = fc1_weight.shape[1]
    rows = items * steps * lat_dev * lon
    side = items * steps * lon
    lat_total = axes.sizes["lat"]
    shards = 8
    upward = [(index, index + 1) for index in range(lat_total - 1)]
    downward = [(index + 1, index) for index in range(lat_total - 1)]
    low = lax.ppermute(tokens[:, :, lat_dev - 1].reshape(side, width), "lat", upward)
    high = lax.ppermute(tokens[:, :, 0].reshape(side, width), "lat", downward)
    vecs = (
        jnp.concatenate(
            [
                norm1_gain,
                norm1_bias,
                qv_bias.reshape(2 * width),
                proj_bias,
                norm2_gain,
                norm2_bias,
                fc2_bias,
                fc1_bias,
            ]
        )
        .astype(f32)
        .reshape(8 + hidden // width, width)
    )
    mask = window_mask(lax.axis_index("lat"), lat_total, lat_dev, steps, lon)
    place = jnp.stack([axes.bit(axes.core)] + [axes.slot(order) for order in axes.orders])
    flat_tokens = tokens.reshape(rows, width)
    flat_cot = cotangent.reshape(rows, width)
    band = rows // items
    keys = band + 2 * side // items
    groups = width // 128

    (mixed, a_low, o_low, c_low, g_low, du_low, dy_low, dx1, dq, dk, dv, to_low, to_high, small) = on_device(
        functools.partial(block_kernel, items),
        [
            ((rows, width), bf16),
            ((rows, width), bf16),
            ((rows, width), bf16),
            ((rows, width), bf16),
            ((rows, hidden), bf16),
            ((rows, hidden), bf16),
            ((rows, width), bf16),
            ((rows, width), f32),
            ((rows, width), bf16),
            ((rows, width), f32),
            ((rows, width), f32),
            ((2, side, width), bf16),
            ((2, side, width), bf16),
            ((4 + hidden // width, width), f32),
        ],
        scratch=[
            pltpu.VMEM((2, rows + 2 * side, width), bf16),
            pltpu.VMEM((rows, width), bf16),
            pltpu.VMEM((items * groups, GROUP * band, keys), f32),
            pltpu.VMEM((rows, width), bf16),
        ],
        args=10,
        vmem=40,
    )(flat_tokens, low, high, flat_cot, vecs, qkv_weight, proj_weight, fc1_weight, fc2_weight, mask)

    from_above = lax.ppermute(to_low, "lat", downward)
    from_below = lax.ppermute(to_high, "lat", upward)

    both = hidden + width
    keep1, send1, keep2, send2 = on_device(
        functools.partial(mlp_grad_kernel, shards),
        [((hidden // 2, width), bf16)] * 2 + [((width // 2, both), bf16)] * 2,
        scalars=1,
        args=6,
    )(place, g_low, flat_cot, c_low, du_low, o_low, dy_low)

    keep3, send3, tokens_grad, small = on_device(
        functools.partial(qkv_grad_kernel, shards, lat_dev, lon),
        [
            ((width // 2, 3 * width), bf16),
            ((width // 2, 3 * width), bf16),
            ((rows, width), bf16),
            (((8 + hidden // width) // 3, 3 * width), bf16),
        ],
        scratch=[pltpu.VMEM((rows, 3 * width), bf16)],
        scalars=1,
        args=11,
    )(place, dq, dk, dv, from_below, from_above, a_low, flat_tokens, vecs, dx1, qkv_weight, small)

    piece1, _ = reduce_stream(axes, keep1, send1, axes.orders[0])
    piece2, _ = reduce_stream(axes, keep2, send2, axes.orders[1])
    piece3, small = reduce_stream(axes, keep3, send3, axes.orders[2], small)
    halves1 = gather_stream(axes, piece1, axes.orders[0])
    halves2 = gather_stream(axes, piece2, axes.orders[1])
    halves3 = gather_stream(axes, piece3, axes.orders[2])

    def spread(index, halves, splits):
        return on_device(
            functools.partial(spread_kernel, index, shards, splits),
            [((2 * halves[0].shape[0], count), f32) for count in splits],
            scalars=1,
            args=2,
        )(place, *halves)

    (grad_fc2,) = spread(1, halves1, (width,))
    grad_fc1, grad_proj = spread(2, halves2, (hidden, width))
    (grad_qkv,) = spread(3, halves3, (3 * width,))
    small = small.reshape(8 + hidden // width, width)
    return (
        mixed.reshape(tokens.shape),
        tokens_grad.reshape(tokens.shape),
        small[0],
        small[1],
        grad_qkv,
        small[2:4],
        grad_proj,
        small[7],
        small[4],
        small[5],
        grad_fc1,
        small[8:].reshape(hidden),
        grad_fc2,
        small[6],
    )


def solution(mesh):
    split = P("items", None, "lat", None, None)
    whole = P()
    return jax.shard_map(
        functools.partial(body, Axes(mesh)),
        mesh=mesh,
        in_specs=(split,) + (whole,) * 12 + (split,),
        out_specs=(split, split) + (whole,) * 12,
        check_vma=False,
    )
```

time: 367 us -> 162 us (0.44)
  waiting for transfers between devices: 189 us -> 65.7 us
  blocking collectives: 43.1 us -> 0 us
  matrix products: 35.3 us -> 0 us
  Pallas kernels: 0 us -> 25.7 us
  starting transfers between devices: 12.5 us -> 37.8 us
  local copies, waits for them, and re-layouts: 53.5 us -> 28.9 us
  other arithmetic: 17 us -> 2.11 us
  between operations: 14.7 us -> 1.09 us
    psum x1 -> x0, waiting for transfers between devices: 187 us -> none  [body(): lax.psum((attn_terms[0], attn_terms[1], attn_terms[2], attn_terms[3], att...]
    ppermute x4 -> x32, waiting for transfers between devices: 2.46 us -> 65.7 us  [the longest x28 63.1 us: exchange(): return lax.ppermute(value, axis, pairs)]
    psum x1 -> x0, blocking collectives: 43.1 us -> none  [body(): lax.psum((attn_terms[0], attn_terms[1], attn_terms[2], attn_terms[3], att...]
    dot_general x18 -> x0, matrix products: 35.3 us -> none  [the longest x4 11.3 us: contract_rows(): lax.dot_general(left, right, (((0,), (0,)), ((), ())), preferred_element_...]
    pallas_call x0 -> x6, Pallas kernels: none -> 25.7 us  [the longest x3 10.6 us: spread(): on_device(functools.partial(spread_kernel, index, shards, splits), [((2 *...]
    ppermute x4 -> x32, starting transfers between devices: 12.4 us -> 37.8 us  [the longest x28 26.9 us: exchange(): return lax.ppermute(value, axis, pairs)]
    squeeze x8 -> x0, local copies, waits for them, and re-layouts: 13.6 us -> none  [body(): lax.map(forward_block, (query_blocks, wide_fwd[0], wide_fwd[1]))]
    unnamed x87 -> x64, local copies, waits for them, and re-layouts: 14.9 us -> 26 us
  transfers between devices with their start and end apart: 5 -> 32, of which waited for: 2 -> 17; matrix products, arithmetic and copies ran while one was open for 3% -> 7% of each run, Pallas kernels for 0% -> 5%
where the time goes in v1:
time: 162 us; the launch traced here: 161 us
  waiting for transfers between devices  65.7 us (41%)
  starting transfers between devices  37.8 us (23%)
  local copies, waits for them, and re-layouts  28.9 us (18%)
  Pallas kernels  25.7 us (16%)
  other arithmetic  2.11 us (1%)
    ppermute x28, waiting for transfers between devices, exchange(): return lax.ppermute(value, axis, pairs)  63.1 us
    ppermute x28, starting transfers between devices, exchange(): return lax.ppermute(value, axis, pairs)  26.9 us
    unnamed x64, local copies, waits for them, and re-layouts  26 us
    pallas_call x3, Pallas kernels, spread(): on_device(functools.partial(spread_kernel, index, shards, splits), [((2 *...  10.6 us
    pallas_call x1, Pallas kernels, body(): on_device(functools.partial(block_kernel, items), [((rows, width), bf16),...  10.1 us
    ppermute x1, starting transfers between devices, body(): from_below = lax.ppermute(to_high, 'lat', upward)  5.85 us
  transfers between devices with their start and end apart: 32, of which 17 were waited for; matrix products, arithmetic and copies ran while one was open for 7% of the time, Pallas kernels for 5%

profile of v1, /device:TPU:0, one launch (start us, length us, event | category | flops | bytes accessed | tf_op | source)
XLA Modules:
  0.0 161.3 jit_solution(15241166692509346720)
XLA Ops:
  0.6 1.0 fusion.5
  1.6 2.4 %collective-permute-start = (bf16[96,512]{1,0:T(8,128)(2,1)S(1)}, bf16[96,512]{1,0:T(8,128)(2,1)S(1)}, u32[]{:S(2)}, u32[]{:S(2)}) collective-permute-start(bf16[96,512]{1,0:T(8,128)(2,1)S(1)} %bitcast.26), channel_id=1, source_target_pairs={{0,8},{8,16},{16,24},{1,9},{9,17},{17,25},{2,10},{10,18},{18,26},{... | collective-permute-start | bytes 294920 | tf_op jit(solution)/shard_map/ppermute | solution.py:417
  4.0 1.3 collective-permute-start.1
  12.8 1.4 copy-done
  14.2 1.6 copy-done.2
  15.8 1.6 copy-done.3
  17.4 0.9 copy-done.4
  18.3 0.9 copy-done.6
  19.3 1.0 copy-done.8
  21.2 10.1 %shard_map.245 = (bf16[192,512]{1,0:T(8,128)(2,1)}, bf16[192,512]{1,0:T(8,128)(2,1)S(1)}, bf16[192,512]{1,0:T(8,128)(2,1)S(1)}, bf16[192,512]{1,0:T(8,128)(2,1)S...) custom-call(bf16[192,512]{1,0:T(8,128)(2,1)S(1)} %bitcast.21, ...), custom_call_target="tpu_custom_call" | custom-call | tf_op jit(solution)/shard_map/pallas_call | solution.py:443
  37.0 5.9 %collective-permute-start.2 = (bf16[2,96,512]{2,1,0:T(8,128)(2,1)}, bf16[2,96,512]{2,1,0:T(8,128)(2,1)}, u32[]{:S(2)}, u32[]{:S(2)}) collective-permute-start(bf16[2,96,512]{2,1,0:T(8,128)(2,1)} %get-tuple-element.42), channel_id=1, source_target_pairs={{0,8},{8,16},{16,24},{1,9},{9,17},{17,25},{2,10},{10,18},{18,26},{... | collective-permute-start | bytes 589832 | tf_op jit(solution)/shard_map/ppermute | solution.py:472
  42.8 1.5 collective-permute-start.3
  44.4 2.6 %collective-permute-done.3.from_above = bf16[2,96,512]{2,1,0:T(8,128)(2,1)} collective-permute-done((bf16[2,96,512]{2,1,0:T(8,128)(2,1)}, bf16[2,96,512]{2,1,0:T(8,128)(2,1)}, u32[]{:S(2)}, u32[]{:S(2)}) %collective-permute-start.3) | collective-permute-done | bytes 196640 | tf_op jit(solution)/shard_map/ppermute | solution.py:471
  47.0 1.0 copy-done.10
  48.0 1.0 copy-done.12
  49.0 1.0 copy-done.14
  51.9 3.0 %shard_map.246 = (bf16[256,1536]{1,0:T(8,128)(2,1)S(1)}, bf16[256,1536]{1,0:T(8,128)(2,1)S(1)}, bf16[192,512]{1,0:T(8,128)(2,1)}, bf16[4,1536]{1,0:T(4,128)(2,1)S(1)}) custom-call(s32[4]{0:T(128)S(1)} %pad_add_fusion.2.place, bf16[192,512]{1,0:T(8,128)(2,1)S(1)} %copy-done.18, f32[192,512]{1,0:T(8,128)S(1)} %copy-done.12, f32[192,512]{1,0:T(8,128)S(1)} %copy-done.14, ...), custom_call_target="tpu_custom_call" | custom-call | tf_op jit(solution)/shard_map/pallas_call | solution.py:482
  54.9 4.1 %collective-permute-start.5 = (bf16[256,1536]{1,0:T(8,128)(2,1)S(1)}, bf16[256,1536]{1,0:T(8,128)(2,1)S(1)}, u32[]{:S(2)}, u32[]{:S(2)}) collective-permute-start(bf16[256,1536]{1,0:T(8,128)(2,1)S(1)} %get-tuple-element.50), channel_id=1, source_target_pairs={{0,8},{8,0},{16,24},{24,16},{1,9},{9,1},{17,25},{25,17},{2,10},{10... | collective-permute-start | bytes 2359304 | tf_op jit(solution)/shard_map/ppermute | solution.py:333
  59.1 2.0 %shard_map.248 = (bf16[1024,512]{1,0:T(8,128)(2,1)S(1)}, bf16[1024,512]{1,0:T(8,128)(2,1)S(1)}, bf16[256,2560]{1,0:T(8,128)(2,1)S(1)}, bf16[256,2560]{1,0:T(8,128)(2,1)S(1)}) custom-call(s32[4]{0:T(128)S(1)} %pad_add_fusion.2.place, bf16[192,2048]{1,0:T(8,128)(2,1)S(1)} %get-tuple-element.51.g, bf16[192,512]{1,0:T(8,128)(2,1)S(1)} %bitcast.24, ...), custom_call_target="tpu_custom_call" | custom-call | tf_op jit(solution)/shard_map/pallas_call | solution.py:475
  61.8 1.6 %collective-permute-start.6 = (bf16[132,1536]{1,0:T(8,128)(2,1)S(1)}, bf16[132,1536]{1,0:T(8,128)(2,1)S(1)}, u32[]{:S(2)}, u32[]{:S(2)}) collective-permute-start(bf16[132,1536]{1,0:T(8,128)(2,1)S(1)} %pad_maximum_fusion.5), channel_id=1, source_target_pairs={{0,2},{1,3},{2,0},{3,1},{4,6},{5,7},{6,4},{7,5},{8,10},{9,11},{10,... | collective-permute-start | bytes 1216520 | tf_op jit(solution)/shard_map/ppermute | solution.py:333
  64.3 9.2 %collective-permute-done.6 = bf16[132,1536]{1,0:T(8,128)(2,1)S(1)} collective-permute-done((bf16[132,1536]{1,0:T(8,128)(2,1)S(1)}, bf16[132,1536]{1,0:T(8,128)(2,1)S(1)}, u32[]{:S(2)}, u32[]{:S(2)}) %collective-permute-start.6) | collective-permute-done | bytes 405536 | tf_op jit(solution)/shard_map/ppermute | solution.py:333
  74.0 1.6 collective-permute-start.15
  75.6 7.5 %collective-permute-done.7 = bf16[68,1536]{1,0:T(8,128)(2,1)S(1)} collective-permute-done((bf16[68,1536]{1,0:T(8,128)(2,1)S(1)}, bf16[68,1536]{1,0:T(8,128)(2,1)S(1)}, u32[]{:S(2)}, u32[]{:S(2)}) %collective-permute-start.7) | collective-permute-done | bytes 208928 | tf_op jit(solution)/shard_map/ppermute | solution.py:333
  83.2 1.6 collective-permute-start.8
  85.5 8.9 %collective-permute-done.8 = bf16[36,1536]{1,0:T(8,128)(2,1)S(1)} collective-permute-done((bf16[36,1536]{1,0:T(8,128)(2,1)S(1)}, bf16[36,1536]{1,0:T(8,128)(2,1)S(1)}, u32[]{:S(2)}, u32[]{:S(2)}) %collective-permute-start.8) | collective-permute-done | bytes 110624 | tf_op jit(solution)/shard_map/ppermute | solution.py:333
  94.6 1.6 %collective-permute-start.16 = (bf16[64,2560]{1,0:T(8,128)(2,1)S(1)}, bf16[64,2560]{1,0:T(8,128)(2,1)S(1)}, u32[]{:S(2)}, u32[]{:S(2)}) collective-permute-start(bf16[64,2560]{1,0:T(8,128)(2,1)S(1)} %add_convert_fusion.3), channel_id=1, source_target_pairs={{0,2},{1,3},{2,0},{3,1},{4,6},{5,7},{6,4},{7,5},{8,10},{9,11},{10,... | collective-permute-start | bytes 983048 | tf_op jit(solution)/shard_map/ppermute | solution.py:333
  96.3 2.7 %collective-permute-start.9 = (bf16[36,1536]{1,0:T(8,128)(2,1)S(1)}, bf16[36,1536]{1,0:T(8,128)(2,1)S(1)}, u32[]{:S(2)}, u32[]{:S(2)}) collective-permute-start(bf16[36,1536]{1,0:T(8,128)(2,1)S(1)} %pad_maximum_fusion.12), channel_id=1, source_target_pairs={{0,4},{1,5},{2,6},{3,7},{4,0},{5,1},{6,2},{7,3},{8,12},{9,13},{10,... | collective-permute-start | bytes 331784 | tf_op jit(solution)/shard_map/ppermute | solution.py:333
  99.0 5.9 %collective-permute-done.16 = bf16[64,2560]{1,0:T(8,128)(2,1)S(1)} collective-permute-done((bf16[64,2560]{1,0:T(8,128)(2,1)S(1)}, bf16[64,2560]{1,0:T(8,128)(2,1)S(1)}, u32[]{:S(2)}, u32[]{:S(2)}) %collective-permute-start.16) | collective-permute-done | bytes 327712 | tf_op jit(solution)/shard_map/ppermute | solution.py:333
  105.8 4.6 %collective-permute-done.17 = bf16[32,2560]{1,0:T(8,128)(2,1)S(1)} collective-permute-done((bf16[32,2560]{1,0:T(8,128)(2,1)S(1)}, bf16[32,2560]{1,0:T(8,128)(2,1)S(1)}, u32[]{:S(2)}, u32[]{:S(2)}) %collective-permute-start.17) | collective-permute-done | bytes 163872 | tf_op jit(solution)/shard_map/ppermute | solution.py:333
  110.5 1.8 %collective-permute-start.18 = (bf16[32,2560]{1,0:T(8,128)(2,1)S(1)}, bf16[32,2560]{1,0:T(8,128)(2,1)S(1)}, u32[]{:S(2)}, u32[]{:S(2)}) collective-permute-start(bf16[32,2560]{1,0:T(8,128)(2,1)S(1)} %add_convert_fusion.7), channel_id=1, source_target_pairs={{0,4},{1,5},{2,6},{3,7},{4,0},{5,1},{6,2},{7,3},{8,12},{9,13},{10,... | collective-permute-start | bytes 491528 | tf_op jit(solution)/shard_map/ppermute | solution.py:333
  112.3 1.4 collective-permute-start.27
  113.7 4.9 %collective-permute-done.18 = bf16[32,2560]{1,0:T(8,128)(2,1)S(1)} collective-permute-done((bf16[32,2560]{1,0:T(8,128)(2,1)S(1)}, bf16[32,2560]{1,0:T(8,128)(2,1)S(1)}, u32[]{:S(2)}, u32[]{:S(2)}) %collective-permute-start.18) | collective-permute-done | bytes 163872 | tf_op jit(solution)/shard_map/ppermute | solution.py:333
  119.1 2.3 %collective-permute-done.27 = bf16[128,512]{1,0:T(8,128)(2,1)S(1)} collective-permute-done((bf16[128,512]{1,0:T(8,128)(2,1)S(1)}, bf16[128,512]{1,0:T(8,128)(2,1)S(1)}, u32[]{:S(2)}, u32[]{:S(2)}) %collective-permute-start.27) | collective-permute-done | bytes 131104 | tf_op jit(solution)/shard_map/ppermute | solution.py:333
  121.6 2.5 %collective-permute-done.19 = bf16[32,2560]{1,0:T(8,128)(2,1)S(1)} collective-permute-done((bf16[32,2560]{1,0:T(8,128)(2,1)S(1)}, bf16[32,2560]{1,0:T(8,128)(2,1)S(1)}, u32[]{:S(2)}, u32[]{:S(2)}) %collective-permute-start.19) | collective-permute-done | bytes 163872 | tf_op jit(solution)/shard_map/ppermute | solution.py:333
  124.1 1.2 collective-permute-start.20
  125.3 1.6 collective-permute-start.10
  126.9 1.3 collective-permute-start.29
  128.1 3.1 %collective-permute-done.20 = bf16[64,2560]{1,0:T(8,128)(2,1)S(1)} collective-permute-done((bf16[64,2560]{1,0:T(8,128)(2,1)S(1)}, bf16[64,2560]{1,0:T(8,128)(2,1)S(1)}, u32[]{:S(2)}, u32[]{:S(2)}) %collective-permute-start.20) | collective-permute-done | bytes 327712 | tf_op jit(solution)/shard_map/ppermute | solution.py:333
  131.2 1.6 collective-permute-start.21
  133.3 3.4 %collective-permute-done.29 = bf16[256,512]{1,0:T(8,128)(2,1)S(1)} collective-permute-done((bf16[256,512]{1,0:T(8,128)(2,1)S(1)}, bf16[256,512]{1,0:T(8,128)(2,1)S(1)}, u32[]{:S(2)}, u32[]{:S(2)}) %collective-permute-start.29) | collective-permute-done | bytes 262176 | tf_op jit(solution)/shard_map/ppermute | solution.py:333
  136.8 1.8 %collective-permute-done.11 = bf16[64,1536]{1,0:T(8,128)(2,1)S(1)} collective-permute-done((bf16[64,1536]{1,0:T(8,128)(2,1)S(1)}, bf16[64,1536]{1,0:T(8,128)(2,1)S(1)}, u32[]{:S(2)}, u32[]{:S(2)}) %collective-permute-start.11) | collective-permute-done | bytes 196640 | tf_op jit(solution)/shard_map/ppermute | solution.py:333
  138.6 1.2 collective-permute-start.12
  139.8 5.0 %collective-permute-done.21 = bf16[128,2560]{1,0:T(8,128)(2,1)S(1)} collective-permute-done((bf16[128,2560]{1,0:T(8,128)(2,1)S(1)}, bf16[128,2560]{1,0:T(8,128)(2,1)S(1)}, u32[]{:S(2)}, u32[]{:S(2)}) %collective-permute-start.21) | collective-permute-done | bytes 655392 | tf_op jit(solution)/shard_map/ppermute | solution.py:333
  144.9 1.0 collective-permute-done.30
  148.6 2.1 %collective-permute-done.13.other = bf16[256,1536]{1,0:T(8,128)(2,1)} collective-permute-done((bf16[256,1536]{1,0:T(8,128)(2,1)S(1)}, bf16[256,1536]{1,0:T(8,128)(2,1)}, u32[]{:S(2)}, u32[]{:S(2)}) %collective-permute-start.13) | collective-permute-done | bytes 786464 | tf_op jit(solution)/shard_map/ppermute | solution.py:333
  150.7 3.0 %shard_map.247 = f32[512,1536]{1,0:T(8,128)} custom-call(s32[4]{0:T(128)S(1)} %pad_add_fusion.2.place, bf16[256,1536]{1,0:T(8,128)(2,1)S(1)} %pad_maximum_fusion.2.own, bf16[256,1536]{1,0:T(8,128)(2,1)} %collective-permute-done.13.other), custom_call_target="tpu_custom_call" | custom-call | tf_op jit(solution)/shard_map/pallas_call | solution.py:503
  153.7 3.5 %shard_map.250 = f32[2048,512]{1,0:T(8,128)} custom-call(s32[4]{0:T(128)S(1)} %pad_add_fusion.2.place, bf16[1024,512]{1,0:T(8,128)(2,1)S(1)} %pad_maximum_fusion.1.own, bf16[1024,512]{1,0:T(8,128)(2,1)} %collective-permute-done.31.other), custom_call_target="tpu_custom_call" | custom-call | tf_op jit(solution)/shard_map/pallas_call | solution.py:503
  157.3 4.0 %shard_map.249 = (f32[512,2048]{1,0:T(8,128)}, f32[512,512]{1,0:T(8,128)}) custom-call(s32[4]{0:T(128)S(1)} %pad_add_fusion.2.place, bf16[256,2560]{1,0:T(8,128)(2,1)S(1)} %pad_maximum_fusion.own, bf16[256,2560]{1,0:T(8,128)(2,1)} %collective-permute-done.22.other), custom_call_target="tpu_custom_call" | custom-call | tf_op jit(solution)/shard_map/pallas_call | solution.py:503
  (134 shorter events, 24.2 us)
Async XLA Ops:
  1.6 10.6 %collective-permute-start = (bf16[96,512]{1,0:T(8,128)(2,1)S(1)}, bf16[96,512]{1,0:T(8,128)(2,1)S(1)}, u32[]{:S(2)}, u32[]{:S(2)}) collective-permute-start(bf16[96,512]{1,0:T(8,128)(2,1)S(1)} %bitcast.26), channel_id=1, source_target_pairs={{0,8},{8,16},{16,24},{1,9},{9,17},{17,25},{2,10},{10,18},{18,26},{... | collective-permute-start | bytes 294920 | tf_op jit(solution)/shard_map/ppermute | solution.py:417
  4.0 8.2 %collective-permute-start.1 = (bf16[96,512]{1,0:T(8,128)(2,1)S(1)}, bf16[96,512]{1,0:T(8,128)(2,1)S(1)}, u32[]{:S(2)}, u32[]{:S(2)}) collective-permute-start(bf16[96,512]{1,0:T(8,128)(2,1)S(1)} %bitcast.25), channel_id=1, source_target_pairs={{8,0},{16,8},{24,16},{9,1},{17,9},{25,17},{10,2},{18,10},{26,18},{... | collective-permute-start | bytes 294920 | tf_op jit(solution)/shard_map/ppermute | solution.py:418
  12.8 1.4 copy-start
  14.2 1.6 copy-start.2
  15.8 1.6 copy-start.3
  17.4 0.9 copy-start.4
  18.3 0.9 copy-start.6
  19.3 1.0 copy-start.8
  21.2 25.8 %copy-start.1 = (bf16[512,1536]{1,0:T(8,128)(2,1)S(1)}, bf16[512,1536]{1,0:T(8,128)(2,1)}, u32[]{:S(2)}) copy-start(bf16[512,1536]{1,0:T(8,128)(2,1)} %wqkv.3) | copy-start | bytes 4718596
  21.2 25.8 %copy-start.5 = (bf16[3,2,2,16,512]{4,3,2,1,0:T(8,128)(2,1)S(1)}, bf16[3,2,2,16,512]{4,3,2,1,0:T(8,128)(2,1)}, u32[]{:S(2)}) copy-start(bf16[3,2,2,16,512]{4,3,2,1,0:T(8,128)(2,1)} %param.14) | copy-start | bytes 589828
  37.0 7.5 %collective-permute-start.2 = (bf16[2,96,512]{2,1,0:T(8,128)(2,1)}, bf16[2,96,512]{2,1,0:T(8,128)(2,1)}, u32[]{:S(2)}, u32[]{:S(2)}) collective-permute-start(bf16[2,96,512]{2,1,0:T(8,128)(2,1)} %get-tuple-element.42), channel_id=1, source_target_pairs={{0,8},{8,16},{16,24},{1,9},{9,17},{17,25},{2,10},{10,18},{18,26},{... | collective-permute-start | bytes 589832 | tf_op jit(solution)/shard_map/ppermute | solution.py:472
  42.8 4.2 %collective-permute-start.3 = (bf16[2,96,512]{2,1,0:T(8,128)(2,1)}, bf16[2,96,512]{2,1,0:T(8,128)(2,1)}, u32[]{:S(2)}, u32[]{:S(2)}) collective-permute-start(bf16[2,96,512]{2,1,0:T(8,128)(2,1)} %get-tuple-element.43), channel_id=1, source_target_pairs={{8,0},{16,8},{24,16},{9,1},{17,9},{25,17},{10,2},{18,10},{26,18},{... | collective-permute-start | bytes 589832 | tf_op jit(solution)/shard_map/ppermute | solution.py:471
  47.0 1.0 copy-start.10
  48.0 1.0 copy-start.12
  49.0 1.0 copy-start.14
  51.0 0.9 copy-start.18
  51.9 7.2 %copy-start.7 = (bf16[3,2,2,16,512]{4,3,2,1,0:T(8,128)(2,1)S(1)}, bf16[3,2,2,16,512]{4,3,2,1,0:T(8,128)(2,1)}, u32[]{:S(2)}) copy-start(bf16[3,2,2,16,512]{4,3,2,1,0:T(8,128)(2,1)} %param.27) | copy-start | bytes 589828
  51.9 7.2 %copy-start.20 = (bf16[192,512]{1,0:T(8,128)(2,1)S(1)}, bf16[192,512]{1,0:T(8,128)(2,1)}, u32[]{:S(2)}) copy-start(bf16[192,512]{1,0:T(8,128)(2,1)} %copy-done.19) | copy-start | bytes 589828
  51.9 7.2 %copy-start.22 = (bf16[192,512]{1,0:T(8,128)(2,1)S(1)}, bf16[192,512]{1,0:T(8,128)(2,1)}, u32[]{:S(2)}) copy-start(bf16[192,512]{1,0:T(8,128)(2,1)} %copy-done.21) | copy-start | bytes 589828
  51.9 7.2 %copy-start.24 = (bf16[192,512]{1,0:T(8,128)(2,1)S(1)}, bf16[192,512]{1,0:T(8,128)(2,1)}, u32[]{:S(2)}) copy-start(bf16[192,512]{1,0:T(8,128)(2,1)} %copy-done.23) | copy-start | bytes 589828
  54.9 6.8 %collective-permute-start.5 = (bf16[256,1536]{1,0:T(8,128)(2,1)S(1)}, bf16[256,1536]{1,0:T(8,128)(2,1)S(1)}, u32[]{:S(2)}, u32[]{:S(2)}) collective-permute-start(bf16[256,1536]{1,0:T(8,128)(2,1)S(1)} %get-tuple-element.50), channel_id=1, source_target_pairs={{0,8},{8,0},{16,24},{24,16},{1,9},{9,1},{17,25},{25,17},{2,10},{10... | collective-permute-start | bytes 2359304 | tf_op jit(solution)/shard_map/ppermute | solution.py:333
  59.1 2.6 %collective-permute-start.4 = (bf16[4,1536]{1,0:T(4,128)(2,1)S(1)}, bf16[4,1536]{1,0:T(4,128)(2,1)S(1)}, u32[]{:S(2)}, u32[]{:S(2)}) collective-permute-start(bf16[4,1536]{1,0:T(4,128)(2,1)S(1)} %get-tuple-element.48), channel_id=1, source_target_pairs={{0,8},{8,0},{16,24},{24,16},{1,9},{9,1},{17,25},{25,17},{2,10},{10... | collective-permute-start | bytes 36872 | tf_op jit(solution)/shard_map/ppermute | solution.py:333
  61.1 2.8 %collective-permute-start.23 = (bf16[1024,512]{1,0:T(8,128)(2,1)S(1)}, bf16[1024,512]{1,0:T(8,128)(2,1)S(1)}, u32[]{:S(2)}, u32[]{:S(2)}) collective-permute-start(bf16[1024,512]{1,0:T(8,128)(2,1)S(1)} %get-tuple-element.61), channel_id=1, source_target_pairs={{0,8},{8,0},{16,24},{24,16},{1,9},{9,1},{17,25},{25,17},{2,10},{10... | collective-permute-start | bytes 3145736 | tf_op jit(solution)/shard_map/ppermute | solution.py:333
  61.8 11.6 %collective-permute-start.6 = (bf16[132,1536]{1,0:T(8,128)(2,1)S(1)}, bf16[132,1536]{1,0:T(8,128)(2,1)S(1)}, u32[]{:S(2)}, u32[]{:S(2)}) collective-permute-start(bf16[132,1536]{1,0:T(8,128)(2,1)S(1)} %pad_maximum_fusion.5), channel_id=1, source_target_pairs={{0,2},{1,3},{2,0},{3,1},{4,6},{5,7},{6,4},{7,5},{8,10},{9,11},{10,... | collective-permute-start | bytes 1216520 | tf_op jit(solution)/shard_map/ppermute | solution.py:333
  63.5 10.4 %collective-permute-start.14 = (bf16[256,2560]{1,0:T(8,128)(2,1)S(1)}, bf16[256,2560]{1,0:T(8,128)(2,1)S(1)}, u32[]{:S(2)}, u32[]{:S(2)}) collective-permute-start(bf16[256,2560]{1,0:T(8,128)(2,1)S(1)} %get-tuple-element.57), channel_id=1, source_target_pairs={{0,8},{8,0},{16,24},{24,16},{1,9},{9,1},{17,25},{25,17},{2,10},{10... | collective-permute-start | bytes 3932168 | tf_op jit(solution)/shard_map/ppermute | solution.py:333
  64.1 20.7 %collective-permute-start.24 = (bf16[512,512]{1,0:T(8,128)(2,1)S(1)}, bf16[512,512]{1,0:T(8,128)(2,1)S(1)}, u32[]{:S(2)}, u32[]{:S(2)}) collective-permute-start(bf16[512,512]{1,0:T(8,128)(2,1)S(1)} %add_convert_fusion.1), channel_id=1, source_target_pairs={{0,16},{8,24},{16,0},{24,8},{1,17},{9,25},{17,1},{25,9},{2,18},{10... | collective-permute-start | bytes 1572872 | tf_op jit(solution)/shard_map/ppermute | solution.py:333
  73.6 9.5 %collective-permute-start.7 = (bf16[68,1536]{1,0:T(8,128)(2,1)S(1)}, bf16[68,1536]{1,0:T(8,128)(2,1)S(1)}, u32[]{:S(2)}, u32[]{:S(2)}) collective-permute-start(bf16[68,1536]{1,0:T(8,128)(2,1)S(1)} %pad_maximum_fusion.9), channel_id=1, source_target_pairs={{0,16},{8,24},{16,0},{24,8},{1,17},{9,25},{17,1},{25,9},{2,18},{10... | collective-permute-start | bytes 626696 | tf_op jit(solution)/shard_map/ppermute | solution.py:333
  74.0 20.4 %collective-permute-start.15 = (bf16[128,2560]{1,0:T(8,128)(2,1)S(1)}, bf16[128,2560]{1,0:T(8,128)(2,1)S(1)}, u32[]{:S(2)}, u32[]{:S(2)}) collective-permute-start(bf16[128,2560]{1,0:T(8,128)(2,1)S(1)} %add_convert_fusion), channel_id=1, source_target_pairs={{0,1},{1,0},{2,3},{3,2},{4,5},{5,4},{6,7},{7,6},{8,9},{9,8},{10,11... | collective-permute-start | bytes 1966088 | tf_op jit(solution)/shard_map/ppermute | solution.py:333
  83.2 11.2 %collective-permute-start.8 = (bf16[36,1536]{1,0:T(8,128)(2,1)S(1)}, bf16[36,1536]{1,0:T(8,128)(2,1)S(1)}, u32[]{:S(2)}, u32[]{:S(2)}) collective-permute-start(bf16[36,1536]{1,0:T(8,128)(2,1)S(1)} %pad_maximum_fusion.11), channel_id=1, source_target_pairs={{0,1},{1,0},{2,3},{3,2},{4,5},{5,4},{6,7},{7,6},{8,9},{9,8},{10,11... | collective-permute-start | bytes 331784 | tf_op jit(solution)/shard_map/ppermute | solution.py:333
  84.9 20.5 %collective-permute-start.25 = (bf16[256,512]{1,0:T(8,128)(2,1)S(1)}, bf16[256,512]{1,0:T(8,128)(2,1)S(1)}, u32[]{:S(2)}, u32[]{:S(2)}) collective-permute-start(bf16[256,512]{1,0:T(8,128)(2,1)S(1)} %add_convert_fusion.4), channel_id=1, source_target_pairs={{0,1},{1,0},{2,3},{3,2},{4,5},{5,4},{6,7},{7,6},{8,9},{9,8},{10,11... | collective-permute-start | bytes 786440 | tf_op jit(solution)/shard_map/ppermute | solution.py:333
  94.6 10.3 %collective-permute-start.16 = (bf16[64,2560]{1,0:T(8,128)(2,1)S(1)}, bf16[64,2560]{1,0:T(8,128)(2,1)S(1)}, u32[]{:S(2)}, u32[]{:S(2)}) collective-permute-start(bf16[64,2560]{1,0:T(8,128)(2,1)S(1)} %add_convert_fusion.3), channel_id=1, source_target_pairs={{0,2},{1,3},{2,0},{3,1},{4,6},{5,7},{6,4},{7,5},{8,10},{9,11},{10,... | collective-permute-start | bytes 983048 | tf_op jit(solution)/shard_map/ppermute | solution.py:333
  96.3 28.9 %collective-permute-start.9 = (bf16[36,1536]{1,0:T(8,128)(2,1)S(1)}, bf16[36,1536]{1,0:T(8,128)(2,1)S(1)}, u32[]{:S(2)}, u32[]{:S(2)}) collective-permute-start(bf16[36,1536]{1,0:T(8,128)(2,1)S(1)} %pad_maximum_fusion.12), channel_id=1, source_target_pairs={{0,4},{1,5},{2,6},{3,7},{4,0},{5,1},{6,2},{7,3},{8,12},{9,13},{10,... | collective-permute-start | bytes 331784 | tf_op jit(solution)/shard_map/ppermute | solution.py:333
  105.0 5.4 %collective-permute-start.17 = (bf16[32,2560]{1,0:T(8,128)(2,1)S(1)}, bf16[32,2560]{1,0:T(8,128)(2,1)S(1)}, u32[]{:S(2)}, u32[]{:S(2)}) collective-permute-start(bf16[32,2560]{1,0:T(8,128)(2,1)S(1)} %add_convert_fusion.8), channel_id=1, source_target_pairs={{0,16},{8,24},{16,0},{24,8},{1,17},{9,25},{17,1},{25,9},{2,18},{10... | collective-permute-start | bytes 491528 | tf_op jit(solution)/shard_map/ppermute | solution.py:333
  105.5 6.7 %collective-permute-start.26 = (bf16[128,512]{1,0:T(8,128)(2,1)S(1)}, bf16[128,512]{1,0:T(8,128)(2,1)S(1)}, u32[]{:S(2)}, u32[]{:S(2)}) collective-permute-start(bf16[128,512]{1,0:T(8,128)(2,1)S(1)} %add_convert_fusion.11), channel_id=1, source_target_pairs={{0,2},{1,3},{2,0},{3,1},{4,6},{5,7},{6,4},{7,5},{8,10},{9,11},{10,... | collective-permute-start | bytes 393224 | tf_op jit(solution)/shard_map/ppermute | solution.py:333
  110.5 8.1 %collective-permute-start.18 = (bf16[32,2560]{1,0:T(8,128)(2,1)S(1)}, bf16[32,2560]{1,0:T(8,128)(2,1)S(1)}, u32[]{:S(2)}, u32[]{:S(2)}) collective-permute-start(bf16[32,2560]{1,0:T(8,128)(2,1)S(1)} %add_convert_fusion.7), channel_id=1, source_target_pairs={{0,4},{1,5},{2,6},{3,7},{4,0},{5,1},{6,2},{7,3},{8,12},{9,13},{10,... | collective-permute-start | bytes 491528 | tf_op jit(solution)/shard_map/ppermute | solution.py:333
  112.3 9.2 %collective-permute-start.27 = (bf16[128,512]{1,0:T(8,128)(2,1)S(1)}, bf16[128,512]{1,0:T(8,128)(2,1)S(1)}, u32[]{:S(2)}, u32[]{:S(2)}) collective-permute-start(bf16[128,512]{1,0:T(8,128)(2,1)S(1)} %add_convert_fusion.10), channel_id=1, source_target_pairs={{0,4},{1,5},{2,6},{3,7},{4,0},{5,1},{6,2},{7,3},{8,12},{9,13},{10,... | collective-permute-start | bytes 393224 | tf_op jit(solution)/shard_map/ppermute | solution.py:333
  118.6 5.4 %collective-permute-start.19 = (bf16[32,2560]{1,0:T(8,128)(2,1)S(1)}, bf16[32,2560]{1,0:T(8,128)(2,1)S(1)}, u32[]{:S(2)}, u32[]{:S(2)}) collective-permute-start(bf16[32,2560]{1,0:T(8,128)(2,1)S(1)} %add_convert_fusion.6), channel_id=1, source_target_pairs={{0,16},{8,24},{16,0},{24,8},{1,17},{9,25},{17,1},{25,9},{2,18},{10... | collective-permute-start | bytes 491528 | tf_op jit(solution)/shard_map/ppermute | solution.py:333
  121.5 5.3 %collective-permute-start.28 = (bf16[128,512]{1,0:T(8,128)(2,1)S(1)}, bf16[128,512]{1,0:T(8,128)(2,1)S(1)}, u32[]{:S(2)}, u32[]{:S(2)}) collective-permute-start(bf16[128,512]{1,0:T(8,128)(2,1)S(1)} %add_convert_fusion.9), channel_id=1, source_target_pairs={{0,2},{1,3},{2,0},{3,1},{4,6},{5,7},{6,4},{7,5},{8,10},{9,11},{10,... | collective-permute-start | bytes 393224 | tf_op jit(solution)/shard_map/ppermute | solution.py:333
  124.1 7.1 %collective-permute-start.20 = (bf16[64,2560]{1,0:T(8,128)(2,1)S(1)}, bf16[64,2560]{1,0:T(8,128)(2,1)S(1)}, u32[]{:S(2)}, u32[]{:S(2)}) collective-permute-start(bf16[64,2560]{1,0:T(8,128)(2,1)S(1)} %pad_maximum_fusion.7), channel_id=1, source_target_pairs={{0,2},{1,3},{2,0},{3,1},{4,6},{5,7},{6,4},{7,5},{8,10},{9,11},{10,... | collective-permute-start | bytes 983048 | tf_op jit(solution)/shard_map/ppermute | solution.py:333
  125.3 7.6 %collective-permute-start.10 = (bf16[32,1536]{1,0:T(8,128)(2,1)S(1)}, bf16[32,1536]{1,0:T(8,128)(2,1)S(1)}, u32[]{:S(2)}, u32[]{:S(2)}) collective-permute-start(bf16[32,1536]{1,0:T(8,128)(2,1)S(1)} %add_convert_fusion.12), channel_id=1, source_target_pairs={{0,1},{1,0},{2,3},{3,2},{4,5},{5,4},{6,7},{7,6},{8,9},{9,8},{10,11... | collective-permute-start | bytes 294920 | tf_op jit(solution)/shard_map/ppermute | solution.py:333
  126.9 9.8 %collective-permute-start.29 = (bf16[256,512]{1,0:T(8,128)(2,1)S(1)}, bf16[256,512]{1,0:T(8,128)(2,1)S(1)}, u32[]{:S(2)}, u32[]{:S(2)}) collective-permute-start(bf16[256,512]{1,0:T(8,128)(2,1)S(1)} %pad_maximum_fusion.8), channel_id=1, source_target_pairs={{0,1},{1,0},{2,3},{3,2},{4,5},{5,4},{6,7},{7,6},{8,9},{9,8},{10,11... | collective-permute-start | bytes 786440 | tf_op jit(solution)/shard_map/ppermute | solution.py:333
  131.2 13.5 %collective-permute-start.21 = (bf16[128,2560]{1,0:T(8,128)(2,1)S(1)}, bf16[128,2560]{1,0:T(8,128)(2,1)S(1)}, u32[]{:S(2)}, u32[]{:S(2)}) collective-permute-start(bf16[128,2560]{1,0:T(8,128)(2,1)S(1)} %pad_maximum_fusion.3), channel_id=1, source_target_pairs={{0,1},{1,0},{2,3},{3,2},{4,5},{5,4},{6,7},{7,6},{8,9},{9,8},{10,11... | collective-permute-start | bytes 1966088 | tf_op jit(solution)/shard_map/ppermute | solution.py:333
  132.8 5.7 %collective-permute-start.11 = (bf16[64,1536]{1,0:T(8,128)(2,1)S(1)}, bf16[64,1536]{1,0:T(8,128)(2,1)S(1)}, u32[]{:S(2)}, u32[]{:S(2)}) collective-permute-start(bf16[64,1536]{1,0:T(8,128)(2,1)S(1)} %pad_maximum_fusion.10), channel_id=1, source_target_pairs={{0,16},{8,24},{16,0},{24,8},{1,17},{9,25},{17,1},{25,9},{2,18},{10... | collective-permute-start | bytes 589832 | tf_op jit(solution)/shard_map/ppermute | solution.py:333
  136.7 9.2 %collective-permute-start.30 = (bf16[512,512]{1,0:T(8,128)(2,1)S(1)}, bf16[512,512]{1,0:T(8,128)(2,1)S(1)}, u32[]{:S(2)}, u32[]{:S(2)}) collective-permute-start(bf16[512,512]{1,0:T(8,128)(2,1)S(1)} %pad_maximum_fusion.4), channel_id=1, source_target_pairs={{0,16},{8,24},{16,0},{24,8},{1,17},{9,25},{17,1},{25,9},{2,18},{10... | collective-permute-start | bytes 1572872 | tf_op jit(solution)/shard_map/ppermute | solution.py:333
  138.6 7.8 %collective-permute-start.12 = (bf16[128,1536]{1,0:T(8,128)(2,1)S(1)}, bf16[128,1536]{1,0:T(8,128)(2,1)S(1)}, u32[]{:S(2)}, u32[]{:S(2)}) collective-permute-start(bf16[128,1536]{1,0:T(8,128)(2,1)S(1)} %pad_maximum_fusion.6), channel_id=1, source_target_pairs={{0,2},{1,3},{2,0},{3,1},{4,6},{5,7},{6,4},{7,5},{8,10},{9,11},{10,... | collective-permute-start | bytes 1179656 | tf_op jit(solution)/shard_map/ppermute | solution.py:333
  144.8 12.4 %collective-permute-start.22 = (bf16[256,2560]{1,0:T(8,128)(2,1)S(1)}, bf16[256,2560]{1,0:T(8,128)(2,1)}, u32[]{:S(2)}, u32[]{:S(2)}) collective-permute-start(bf16[256,2560]{1,0:T(8,128)(2,1)S(1)} %pad_maximum_fusion.own), channel_id=1, source_target_pairs={{0,8},{8,0},{16,24},{24,16},{1,9},{9,1},{17,25},{25,17},{2,10},{10... | collective-permute-start | bytes 3932168 | tf_op jit(solution)/shard_map/ppermute | solution.py:333
  146.0 7.7 %collective-permute-start.31 = (bf16[1024,512]{1,0:T(8,128)(2,1)S(1)}, bf16[1024,512]{1,0:T(8,128)(2,1)}, u32[]{:S(2)}, u32[]{:S(2)}) collective-permute-start(bf16[1024,512]{1,0:T(8,128)(2,1)S(1)} %pad_maximum_fusion.1.own), channel_id=1, source_target_pairs={{0,8},{8,0},{16,24},{24,16},{1,9},{9,1},{17,25},{25,17},{2,10},{10... | collective-permute-start | bytes 3145736 | tf_op jit(solution)/shard_map/ppermute | solution.py:333
  146.5 4.2 %collective-permute-start.13 = (bf16[256,1536]{1,0:T(8,128)(2,1)S(1)}, bf16[256,1536]{1,0:T(8,128)(2,1)}, u32[]{:S(2)}, u32[]{:S(2)}) collective-permute-start(bf16[256,1536]{1,0:T(8,128)(2,1)S(1)} %pad_maximum_fusion.2.own), channel_id=1, source_target_pairs={{0,8},{8,0},{16,24},{24,16},{1,9},{9,1},{17,25},{25,17},{2,10},{10... | collective-permute-start | bytes 2359304 | tf_op jit(solution)/shard_map/ppermute | solution.py:333
  (11 other events, 8.1 us)

commit v2 on v1

v2 whole, which is shorter than its diff:
```python
import functools
import math

import jax
import jax.numpy as jnp
from jax import lax
from jax.experimental import pallas as pl
from jax.experimental.pallas import tpu as pltpu
from jax.sharding import PartitionSpec as P

HEAD_DIM = 32
ROW_REACH = 1
COL_REACH = 2
GROUP = 128 // HEAD_DIM
EPSILON = 1e-06
SCALE = HEAD_DIM ** (-0.5)
SQRT_HALF = 0.5**0.5
PHI_SCALE = (2.0 * math.pi) ** (-0.5)
NEGATIVE = -1e30
ORDERS = (("zxyw", "xyzw"), ("zywx", "yzxw"), ("yxwz", "xywz"))
ORDER = (2, 3, 1, 3, 2, 1, 3, 2, 1, 3, 2, 1, 3, 2, 1, 3, 2, 3, 1, 2, 3, 1, 3, 2, 1, 3, 2, 1, 3)

f32 = jnp.float32
bf16 = jnp.bfloat16
MIB = 1024 * 1024


def dot_nn(left, right):
    return lax.dot_general(left, right, (((1,), (0,)), ((), ())), preferred_element_type=f32)


def dot_nt(left, right):
    return lax.dot_general(left, right, (((1,), (1,)), ((), ())), preferred_element_type=f32)


def dot_tn(left, right):
    return lax.dot_general(left, right, (((0,), (0,)), ((), ())), preferred_element_type=f32)


def normed(values):
    mean = jnp.mean(values, axis=-1, keepdims=True)
    centred = values - mean
    spread = jnp.mean(centred * centred, axis=-1, keepdims=True)
    scale = lax.rsqrt(spread + EPSILON)
    return centred * scale, scale


def norm_back(grad, gain, unit, scale):
    scaled = grad * gain
    first = jnp.mean(scaled, axis=-1, keepdims=True)
    second = jnp.mean(scaled * unit, axis=-1, keepdims=True)
    return scale * (scaled - first - unit * second)


def as_row(ref):
    return ref[...].astype(f32).reshape(1, ref.shape[0])


def stack_heads(block, lane_head):
    zero = jnp.zeros_like(block)
    return jnp.concatenate(
        [jnp.where(lane_head == head, block, zero) for head in range(GROUP)], axis=0
    )


def fold_heads(stacked, lane_head, rows):
    total = jnp.where(lane_head == 0, stacked[:rows], 0.0)
    for head in range(1, GROUP):
        total = jnp.where(lane_head == head, stacked[head * rows : (head + 1) * rows], total)
    return total


def window_bias(axes, steps, lat_dev, lon):
    band = steps * lat_dev * lon
    keys = band + 2 * steps * lon
    query = lax.broadcasted_iota(jnp.int32, (band, keys), 0)
    key = lax.broadcasted_iota(jnp.int32, (band, keys), 1)
    query_row = query // lon % lat_dev
    first = jnp.where(axes.has_below(), -1, -2 - ROW_REACH)
    last = jnp.where(axes.has_above(), lat_dev, lat_dev + 1 + ROW_REACH)
    key_row = jnp.where(
        key < band, key // lon % lat_dev, jnp.where(key < band + steps * lon, first, last)
    )
    gap = jnp.abs(query % lon - key % lon)
    gap = jnp.minimum(gap, lon - gap)
    seen = (jnp.abs(query_row - key_row) <= ROW_REACH) & (gap <= COL_REACH)
    return jnp.where(seen, 0.0, NEGATIVE)


def block_kernel(
    axes,
    shards,
    items,
    steps,
    lat_dev,
    lon,
    *refs,
):
    sources, finals, refs = refs[:16], refs[16:29], refs[29:]
    targets, locals_, refs = refs[:16], refs[16:29], refs[29:]
    kv_ref, q_ref, p_ref, do_ref, o_ref, c_ref, g_ref, du_ref, dy_ref, in_sems, out_sems = refs
    fetches = start_copies(sources, targets, in_sems)
    (tok, gain1, bias1, qv_bias, beside, across, wqkv, wproj) = targets[:8]
    (bproj, gain2, bias2, w1, b1, w2, b2, cot) = targets[8:]
    (mixed_out, a_out, dx1_out, small_out, keep1, send1, keep2, send2) = locals_[:8]
    (dq_out, dk_out, dv_out, to_beside, to_across) = locals_[8:]
    leaving = []

    def leave(index, slot=0, window=None):
        source, target = locals_[index], finals[index]
        if window is not None:
            source, target = source.at[window], target.at[window]
        copy = pltpu.make_async_copy(source, target, out_sems.at[index, slot])
        copy.start()
        leaving.append(copy)

    for copy in fetches[:6]:
        copy.wait()
    rows, width = tok.shape
    hidden = w1.shape[1]
    side = beside.shape[0]
    band = rows // items
    edge = side // items
    groups = width // 128
    lane_head = lax.broadcasted_iota(jnp.int32, (1, 128), 1) // HEAD_DIM

    g1 = as_row(gain1)
    h1 = as_row(bias1)
    x = tok[...].astype(f32)
    unit, _ = normed(x)
    a_own = (unit * g1 + h1).astype(bf16)
    a_out[...] = a_own
    leave(1)
    wide = jnp.concatenate([beside[...], across[...]], axis=0).astype(f32)
    unit_wide, _ = normed(wide)
    a_wide = (unit_wide * g1 + h1).astype(bf16)
    a_all = jnp.concatenate([a_own, a_wide], axis=0)
    fetches[6].wait()
    q_ref[...] = (dot_nn(a_own, wqkv[:, :width]) + qv_bias[0:1, :].astype(f32)).astype(bf16)
    kv_ref[0] = dot_nn(a_all, wqkv[:, width : 2 * width]).astype(bf16)
    kv_ref[1] = (dot_nn(a_all, wqkv[:, 2 * width :]) + qv_bias[1:2, :].astype(f32)).astype(bf16)

    window = jnp.concatenate([window_bias(axes, steps, lat_dev, lon)] * GROUP, axis=0)
    odd = axes.bit(axes.core)
    below = pl.multiple_of(rows + (1 - odd) * side, 16)
    above = pl.multiple_of(rows + odd * side, 16)

    def keys_of(which, item, lanes):
        return jnp.concatenate(
            [
                kv_ref[which, item * band : (item + 1) * band, lanes],
                kv_ref[which, pl.ds(below + item * edge, edge), lanes],
                kv_ref[which, pl.ds(above + item * edge, edge), lanes],
            ],
            axis=0,
        )

    for item in range(items):
        for group in range(groups):
            lanes = slice(group * 128, (group + 1) * 128)
            own = slice(item * band, (item + 1) * band)
            queries = stack_heads(q_ref[own, lanes], lane_head)
            scores = dot_nt(queries, keys_of(0, item, lanes)) * SCALE + window
            top = jnp.max(scores, axis=-1, keepdims=True)
            weights = jnp.exp(scores - top)
            total = jnp.sum(weights, axis=-1, keepdims=True)
            soft = weights * (1.0 / total)
            p_ref[item * groups + group] = soft
            mixed_heads = dot_nn(soft.astype(bf16), keys_of(1, item, lanes))
            o_ref[own, lanes] = fold_heads(mixed_heads, lane_head, band).astype(bf16)

    for copy in fetches[7:]:
        copy.wait()
    g2 = as_row(gain2)
    h2 = as_row(bias2)
    x1 = x + dot_nn(o_ref[...], wproj[...]) + as_row(bproj)
    unit2, scale2 = normed(x1)
    c_low = (unit2 * g2 + h2).astype(bf16)
    c_ref[...] = c_low
    cot_low = cot[...]
    branch = jnp.zeros((rows, width), f32)
    dc = jnp.zeros((rows, width), f32)
    b1_row = as_row(b1)
    for part in range(hidden // width):
        cols = slice(part * width, (part + 1) * width)
        u = dot_nn(c_low, w1[:, cols]) + b1_row[:, cols]
        cdf = 0.5 + 0.5 * lax.erf(u * SQRT_HALF)
        slope = cdf + u * (jnp.exp(u * u * -0.5) * PHI_SCALE)
        act = (u * cdf).astype(bf16)
        g_ref[:, cols] = act
        branch = branch + dot_nn(act, w2[cols, :])
        dh = dot_nt(cot_low, w2[cols, :])
        du_low = (dh * slope).astype(bf16)
        du_ref[:, cols] = du_low
        small_out[4 + part : 5 + part, :] = jnp.sum(du_low.astype(f32), axis=0, keepdims=True)
        dc = dc + dot_nt(du_low, w1[:, cols])
    mixed_out[...] = (x1 + branch + as_row(b2)).astype(bf16)
    cot_wide = cot_low.astype(f32)
    small_out[0:1, :] = jnp.sum(dc * unit2, axis=0, keepdims=True)
    small_out[1:2, :] = jnp.sum(dc, axis=0, keepdims=True)
    small_out[2:3, :] = jnp.sum(cot_wide, axis=0, keepdims=True)
    dx1 = cot_wide + norm_back(dc, g2, unit2, scale2)
    dx1_out[...] = dx1
    leave(0)
    leave(2)
    dy = dx1.astype(bf16)
    dy_ref[...] = dy
    small_out[3:4, :] = jnp.sum(dy.astype(f32), axis=0, keepdims=True)
    do_ref[...] = dot_nt(dy, wproj[...]).astype(bf16)
    leave(3)
    grad_halves(axes, 0, shards, g_ref, cot, keep1, send1)
    leave(4)
    leave(5)
    grad_halves(axes, 1, shards, c_ref, du_ref, keep2, send2, slice(0, hidden))
    grad_halves(axes, 1, shards, o_ref, dy_ref, keep2, send2, slice(hidden, hidden + width))
    leave(6)
    leave(7)

    for item in range(items):
        for group in range(groups):
            lanes = slice(group * 128, (group + 1) * 128)
            own = slice(item * band, (item + 1) * band)
            ends = slice(item * edge, (item + 1) * edge)
            grads = stack_heads(do_ref[own, lanes], lane_head)
            queries = stack_heads(q_ref[own, lanes], lane_head)
            soft = p_ref[item * groups + group]
            dp = dot_nt(grads, keys_of(1, item, lanes))
            inner = jnp.sum(soft * dp, axis=-1, keepdims=True)
            ds = (soft * (dp - inner)).astype(bf16)
            dq = fold_heads(dot_nn(ds, keys_of(0, item, lanes)), lane_head, band) * SCALE
            dq_out[own, lanes] = dq.astype(bf16)
            dk = dot_tn(ds, queries) * SCALE
            dv = dot_tn(soft.astype(bf16), grads)
            dk_out[own, lanes] = dk[:band]
            dv_out[own, lanes] = dv[:band]
            for index, grad in ((0, dk), (1, dv)):
                down = grad[band : band + edge]
                up = grad[band + edge :]
                to_beside[index, ends, lanes] = jnp.where(odd == 1, down, up).astype(bf16)
                to_across[index, ends, lanes] = jnp.where(odd == 1, up, down).astype(bf16)
        for index in (8, 9, 10):
            leave(index, item, (own, slice(None)))
        for index in (11, 12):
            leave(index, item, (slice(None), ends, slice(None)))
    for copy in leaving:
        copy.wait()


def start_copies(sources, targets, sems, first=0):
    copies = [
        pltpu.make_async_copy(source, target, sems.at[first + index])
        for index, (source, target) in enumerate(zip(sources, targets))
    ]
    for copy in copies:
        copy.start()
    return copies


def grad_halves(axes, stream, shards, left, right, keep, send, lanes=slice(None)):
    half = left.shape[1] // 2
    per = half // shards
    step = min(half, 256)
    core = axes.bit(axes.core)
    values = right[...]
    for ref, owner in ((keep, core), (send, 1 - core)):
        slot = axes.slot(stream, owner)
        for start in range(0, half, step):
            columns = pl.ds(pl.multiple_of(owner * half + start, 128), step)
            product = dot_tn(left[:, columns], values)
            for index in range(step // per):
                spot = pl.multiple_of(((start // per + index) ^ slot) * per, per)
                ref[pl.ds(spot, per), lanes] = product[index * per : (index + 1) * per].astype(bf16)


def qkv_grad_kernel(
    axes,
    shards,
    lat_dev,
    lon,
    *refs,
):
    sources, finals, refs = refs[:11], refs[11:15], refs[15:]
    targets, locals_, refs = refs[:11], refs[11:15], refs[15:]
    joined, in_sems, out_sems = refs
    fetches = start_copies(sources, targets, in_sems)
    dq, dk, dv, from_beside, from_across, a_low, wqkv, tok, gain1, dx1, small_in = targets
    keep, send, tokens_out, small_out = locals_
    for copy in fetches[:6]:
        copy.wait()
    rows, width = tok.shape
    joined[:, :width] = dq[...]
    odd = axes.bit(axes.core) == 1
    for which, grads in ((0, dk), (1, dv)):
        columns = slice((1 + which) * width, (2 + which) * width)
        for strip in range(rows // (lat_dev * lon)):
            edge = slice(strip * lon, (strip + 1) * lon)
            for row in range(lat_dev):
                start = (strip * lat_dev + row) * lon
                value = grads[start : start + lon, :]
                near = from_beside[which, edge, :].astype(f32)
                far = from_across[which, edge, :].astype(f32)
                if row == 0:
                    value = value + jnp.where(odd, near, far)
                if row == lat_dev - 1:
                    value = value + jnp.where(odd, far, near)
                joined[start : start + lon, columns] = value.astype(bf16)
    grad_halves(axes, 2, shards, a_low, joined, keep, send)
    leaving = start_copies(locals_[:2], finals[:2], out_sems)
    for copy in fetches[6:]:
        copy.wait()
    da = dot_nt(joined[...], wqkv[...])
    unit, scale = normed(tok[...].astype(f32))
    grad = dx1[...] + norm_back(da, as_row(gain1), unit, scale)
    tokens_out[...] = grad.astype(bf16)
    sums = [
        jnp.sum(da * unit, axis=0, keepdims=True),
        jnp.sum(da, axis=0, keepdims=True),
        jnp.sum(joined[:, :width].astype(f32), axis=0, keepdims=True),
        jnp.sum(joined[:, 2 * width :].astype(f32), axis=0, keepdims=True),
    ] + [small_in[index : index + 1, :] for index in range(small_in.shape[0])]
    for index, row in enumerate(sums):
        place_of = slice(index % 3 * width, (index % 3 + 1) * width)
        small_out[index // 3 : index // 3 + 1, place_of] = row.astype(bf16)
    leaving += start_copies(locals_[2:], finals[2:], out_sems, 2)
    for copy in leaving:
        copy.wait()


def spread_kernel(axes, stream, shards, splits, other, piece, *refs):
    count = len(splits)
    outs, wide, sems = refs[-2 * count - 1 : -count - 1], refs[-count - 1 : -1], refs[-1]
    half = piece.shape[0]
    per = half // shards
    core = axes.bit(axes.core)
    owner = 1 - core if other else core
    slot = axes.slot(stream, owner)
    copies = []
    for index in range(shards):
        spot = pl.multiple_of(owner * half + (index ^ slot) * per, per)
        rows = slice(index * per, (index + 1) * per)
        first = 0
        for part, (out, buffer, width) in enumerate(zip(outs, wide, splits)):
            buffer[rows, :] = piece[rows, first : first + width].astype(f32)
            first += width
            copy = pltpu.make_async_copy(
                buffer.at[rows, :], out.at[pl.ds(spot, per), :], sems.at[index, part]
            )
            copy.start()
            copies.append(copy)
    for copy in copies:
        copy.wait()


def spread_half(axes, stream, shards, splits, piece, outs=None):
    half = piece.shape[0]
    hbm = pl.BlockSpec(memory_space=pltpu.HBM)
    other = outs is not None
    return pl.pallas_call(
        functools.partial(spread_kernel, axes, stream, shards, splits, other),
        out_shape=[jax.ShapeDtypeStruct((2 * half, width), f32) for width in splits],
        in_specs=[pl.BlockSpec(memory_space=pltpu.VMEM)] + ([hbm] * len(splits) if other else []),
        out_specs=[hbm] * len(splits),
        scratch_shapes=[pltpu.VMEM((half, width), f32) for width in splits]
        + [pltpu.SemaphoreType.DMA((shards, len(splits)))],
        input_output_aliases={1 + index: index for index in range(len(splits))} if other else {},
        compiler_params=pltpu.CompilerParams(vmem_limit_bytes=8 * MIB),
    )(piece, *(outs or ()))


def on_device(kernel, operands, outs, scratch=(), sems=()):
    buffers = [pltpu.VMEM(value.shape, value.dtype) for value in operands]
    buffers += [pltpu.VMEM(shape, dtype) for shape, dtype in outs]
    hbm = pl.BlockSpec(memory_space=pltpu.HBM)
    return pl.pallas_call(
        kernel,
        out_shape=[jax.ShapeDtypeStruct(shape, dtype) for shape, dtype in outs],
        in_specs=[hbm] * len(operands),
        out_specs=[hbm] * len(outs),
        scratch_shapes=buffers
        + [pltpu.VMEM(shape, dtype) for shape, dtype in scratch]
        + [pltpu.SemaphoreType.DMA(shape) for shape in sems],
        compiler_params=pltpu.CompilerParams(vmem_limit_bytes=60 * MIB),
    )(*operands)


class Axes:
    def __init__(self, mesh):
        self.sizes = dict(mesh.shape)
        bits = self.sizes["items"].bit_length() - 1
        self.core = ("lat", 1)
        named = {"x": ("lat", 2), "y": ("items", 1), "z": ("items", 2), "w": ("items", 4)}
        self.orders = [[[named[key] for key in order] for order in pair] for pair in ORDERS]
        self.extra = [("items", 1 << bit) for bit in range(3, bits)]

    def bit(self, dim):
        axis, value = dim
        return (lax.axis_index(axis) // value) % 2

    def slot(self, stream, core):
        pair = []
        for order in self.orders[stream]:
            total = 0
            for dim in order[:-1]:
                total = total * 2 + self.bit(dim)
            pair.append(total)
        return jnp.where(core == 0, pair[0], pair[1])

    def has_below(self):
        return lax.axis_index("lat") > 0

    def has_above(self):
        return lax.axis_index("lat") < self.sizes["lat"] - 1

    def beside(self, value):
        return self.exchange(value, (self.core, self.core))

    def across(self, value):
        count = self.sizes["lat"]
        pairs = [(index, (index + 1) // 2 * 4 - 1 - index) for index in range(1, count - 1)]
        return lax.ppermute(value, "lat", pairs)

    def exchange(self, value, dims):
        items = self.sizes["items"]
        pairs = []
        for index in range(self.sizes["lat"] * items):
            axis, bit = dims[index // items % 2]
            pairs.append((index, index ^ (bit * items if axis == "lat" else bit)))
        return lax.ppermute(value, ("lat", "items"), pairs)


def add_rows(terms, low, high):
    total = terms[0][low:high].astype(f32)
    for term in terms[1:]:
        total = total + term[low:high].astype(f32)
    return total


def sum_stream(axes, stream, keep, send, half_done, small=None, small_done=None):
    core = (axes.core, axes.core)
    terms = [keep, (yield send, core)]
    rows = keep.shape[0]
    extra = 0 if small is None else small.shape[0]
    pairs = list(zip(*axes.orders[stream]))
    hops, whole = pairs[:-1], pairs[-1:] + [(dim, dim) for dim in axes.extra]
    for dims in hops:
        rows //= 2
        value = add_rows(terms, rows, 2 * rows).astype(bf16)
        if extra:
            value = jnp.concatenate([value, small], axis=0)
        got = yield value, dims
        if extra:
            small = (small.astype(f32) + got[rows:].astype(f32)).astype(bf16)
        terms.append(got)
    piece = add_rows(terms, 0, rows).astype(bf16)
    for dims in whole:
        value = jnp.concatenate([piece, small], axis=0) if extra else piece
        got = yield value, dims
        if extra:
            small = (small.astype(f32) + got[rows:].astype(f32)).astype(bf16)
        piece = (piece.astype(f32) + got[:rows].astype(f32)).astype(bf16)
    if extra:
        got = yield small, core
        small_done(small.astype(f32) + got.astype(f32))
    for dims in reversed(hops):
        got = yield piece, dims
        piece = jnp.concatenate([piece, got], axis=0)
    half_done(piece)
    return (yield piece, core)


def after(value, token):
    if token is None:
        return value
    return lax.optimization_barrier((value, token))[0]


class Sequence:
    def __init__(self, axes):
        self.axes = axes
        self.token = None
        self.waiting = {}
        self.streams = {}
        self.done = {}
        self.count = {}
        self.then = None
        self.held = None

    def add(self, name, stream):
        self.streams[name] = stream
        self.waiting[name] = None

    def step(self, name):
        got = self.waiting[name]
        try:
            value, dims = self.streams[name].send(None if got is None else after(got, self.token))
        except StopIteration as end:
            self.done[name] = end.value
            return
        if self.held is not None:
            value = after(value, self.held)
            self.held = None
        self.token = value
        self.count[name] = self.count.get(name, -1) + 1
        with jax.named_scope(f"s{name}h{self.count[name]}"):
            self.waiting[name] = self.axes.exchange(value, dims)
        if self.then is not None:
            act, self.then = self.then, None
            act()

    def steps(self, names):
        for name in names:
            if name not in self.done:
                self.step(name)


def body(
    axes,
    tokens,
    norm1_gain,
    norm1_bias,
    qkv_weight,
    qv_bias,
    proj_weight,
    proj_bias,
    norm2_gain,
    norm2_bias,
    fc1_weight,
    fc1_bias,
    fc2_weight,
    fc2_bias,
    cotangent,
):
    items, steps, lat_dev, lon, width = tokens.shape
    hidden = fc1_weight.shape[1]
    rows = items * steps * lat_dev * lon
    side = items * steps * lon
    lat_total = axes.sizes["lat"]
    shards = 8
    odd = axes.bit(axes.core) == 1
    first = tokens[:, :, 0].reshape(side, width)
    last = tokens[:, :, lat_dev - 1].reshape(side, width)
    beside = axes.beside(jnp.where(odd, first, last))
    across = axes.across(jnp.where(odd, last, first))
    flat_tokens = tokens.reshape(rows, width)
    flat_cot = cotangent.reshape(rows, width)
    operands = (
        flat_tokens,
        norm1_gain,
        norm1_bias,
        qv_bias,
        beside,
        across,
        qkv_weight,
        proj_weight,
        proj_bias,
        norm2_gain,
        norm2_bias,
        fc1_weight,
        fc1_bias,
        fc2_weight,
        fc2_bias,
        flat_cot,
    )
    band = rows // items
    keys = band + 2 * side // items
    groups = width // 128
    both = hidden + width
    (mixed, a_low, dx1, small, keep1, send1, keep2, send2, dq, dk, dv, to_beside, to_across) = on_device(
        functools.partial(block_kernel, axes, shards, items, steps, lat_dev, lon),
        operands,
        [
            ((rows, width), bf16),
            ((rows, width), bf16),
            ((rows, width), f32),
            ((4 + hidden // width, width), f32),
            ((hidden // 2, width), bf16),
            ((hidden // 2, width), bf16),
            ((width // 2, both), bf16),
            ((width // 2, both), bf16),
            ((rows, width), bf16),
            ((rows, width), f32),
            ((rows, width), f32),
            ((2, side, width), bf16),
            ((2, side, width), bf16),
        ],
        scratch=[
            ((2, rows + 2 * side, width), bf16),
            ((rows, width), bf16),
            ((items * groups, GROUP * band, keys), f32),
            ((rows, width), bf16),
            ((rows, width), bf16),
            ((rows, width), bf16),
            ((rows, hidden), bf16),
            ((rows, hidden), bf16),
            ((rows, width), bf16),
        ],
        sems=[(16,), (13, items)],
    )

    from_beside = axes.beside(to_beside)
    from_across = axes.across(to_across)
    grads = {}
    splits = {1: (width,), 2: (hidden, width), 3: (3 * width,)}

    def half_done(name):
        def act(piece):
            def run():
                held = after(piece, sequence.token)
                grads[name] = spread_half(axes, name - 1, shards, splits[name], held)
                sequence.token = grads[name][0]

            sequence.then = run

        return act

    def small_done(total):
        total = total.reshape(8 + hidden // width, width)
        grads["small"] = (
            total[0],
            total[1],
            total[2:4],
            total[7],
            total[4],
            total[5],
            total[8:].reshape(hidden),
            total[6],
        )
        sequence.held = grads["small"]

    sequence = Sequence(axes)
    sequence.token = (to_beside, to_across)
    sequence.add(1, sum_stream(axes, 0, keep1, send1, half_done(1)))
    sequence.add(2, sum_stream(axes, 1, keep2, send2, half_done(2)))
    sequence.steps((2, 1))
    sequence.token = (from_beside, from_across)
    def join():
        operands = (
            after(dq, sequence.token),
            dk,
            dv,
            from_beside,
            from_across,
            a_low,
            qkv_weight,
            flat_tokens,
            norm1_gain,
            dx1,
            small,
        )
        keep, send, grad, sums = on_device(
            functools.partial(qkv_grad_kernel, axes, shards, lat_dev, lon),
            operands,
            [
                ((width // 2, 3 * width), bf16),
                ((width // 2, 3 * width), bf16),
                ((rows, width), bf16),
                (((8 + hidden // width) // 3, 3 * width), bf16),
            ],
            scratch=[((rows, 3 * width), bf16)],
            sems=[(11,), (4,)],
        )
        sequence.add(3, sum_stream(axes, 2, keep, send, half_done(3), sums, small_done))
        return grad

    for name in ORDER + (1, 2, 3) * 12:
        if name in sequence.done:
            continue
        if name == 3 and 3 not in sequence.streams:
            tokens_grad = join()
        sequence.step(name)
        if name in sequence.done:
            other = after(sequence.done[name], sequence.token)
            grads[name] = spread_half(axes, name - 1, shards, splits[name], other, grads[name])
            sequence.token = grads[name][0]
    (grad_fc2,) = grads[1]
    grad_fc1, grad_proj = grads[2]
    (grad_qkv,) = grads[3]
    sums = grads["small"]
    return (
        mixed.reshape(tokens.shape),
        tokens_grad.reshape(tokens.shape),
        sums[0],
        sums[1],
        grad_qkv,
        sums[2],
        grad_proj,
        sums[3],
        sums[4],
        sums[5],
        grad_fc1,
        sums[6],
        grad_fc2,
        sums[7],
    )


def solution(mesh):
    split = P("items", None, "lat", None, None)
    whole = P()
    return jax.shard_map(
        functools.partial(body, Axes(mesh)),
        mesh=mesh,
        in_specs=(split,) + (whole,) * 12 + (split,),
        out_specs=(split, split) + (whole,) * 12,
        check_vma=False,
    )
```

time: 162 us -> 119 us (0.73)
  waiting for transfers between devices: 65.7 us -> 35.7 us
  local copies, waits for them, and re-layouts: 28.9 us -> 2.52 us
  starting transfers between devices: 37.8 us -> 49 us
  other arithmetic: 2.11 us -> 3.97 us
    ppermute x32, waiting for transfers between devices: 65.7 us -> 35.7 us  [the longest x30 35.7 us: exchange(): return lax.ppermute(value, ('lat', 'items'), pairs)]
    unnamed x64 -> x18, local copies, waits for them, and re-layouts: 26 us -> 1.31 us
    ppermute x32, starting transfers between devices: 37.8 us -> 49 us  [the longest x30 47.5 us: exchange(): return lax.ppermute(value, ('lat', 'items'), pairs)]
    pallas_call x6 -> x8, Pallas kernels: 25.7 us -> 26.8 us  [the longest x2 18.2 us: on_device(): pl.pallas_call(kernel, out_shape=[jax.ShapeDtypeStruct(shape, dtype) for...]
  transfers between devices with their start and end apart: 32 -> 32, of which waited for: 17 -> 11; matrix products, arithmetic and copies ran while one was open for 7% -> 4% of each run, Pallas kernels for 5% -> 9%
where the time goes in v2:
time: 119 us
  starting transfers between devices  49 us (41%)
  waiting for transfers between devices  35.7 us (30%)
  Pallas kernels  26.8 us (23%)
  other arithmetic  3.97 us (3%)
  local copies, waits for them, and re-layouts  2.52 us (2%)
  between operations  1.22 us (1%)
    ppermute x30, starting transfers between devices, exchange(): return lax.ppermute(value, ('lat', 'items'), pairs)  47.5 us
    ppermute x30, waiting for transfers between devices, exchange(): return lax.ppermute(value, ('lat', 'items'), pairs)  35.7 us
    pallas_call x2, Pallas kernels, on_device(): pl.pallas_call(kernel, out_shape=[jax.ShapeDtypeStruct(shape, dtype) for...  18.2 us
    pallas_call x6, Pallas kernels, spread_half(): pl.pallas_call(functools.partial(spread_kernel, axes, stream, shards, spl...  8.55 us
  transfers between devices with their start and end apart: 32, of which 11 were waited for; matrix products, arithmetic and copies ran while one was open for 4% of the time, Pallas kernels for 9%

profile of v2, /device:TPU:0, one launch (start us, length us, event | category | flops | bytes accessed | tf_op | source)
XLA Modules:
  0.0 119.2 jit_solution(3350650687684868396)
XLA Ops:
  0.7 1.0 broadcast_select_fusion
  2.1 0.7 collective-permute-start.1
  3.1 0.6 copy-done.5
  3.8 14.5 %shard_map.245 = (bf16[192,512]{1,0:T(8,128)(2,1)}, bf16[192,512]{1,0:T(8,128)(2,1)}, f32[192,512]{1,0:T(8,128)}, f32[8,512]{1,0:T(8,128)}, bf16[1024,512]{1,0:T...) custom-call(bf16[192,512]{1,0:T(8,128)(2,1)} %bitcast.15, ...), custom_call_target="tpu_custom_call" | custom-call | tf_op jit(solution)/shard_map/pallas_call | solution.py:374
  18.3 5.9 %collective-permute-start.2 = (bf16[256,2560]{1,0:T(8,128)(2,1)}, bf16[256,2560]{1,0:T(8,128)(2,1)S(1)}, u32[]{:S(2)}, u32[]{:S(2)}) collective-permute-start(bf16[256,2560]{1,0:T(8,128)(2,1)} %get-tuple-element.74), channel_id=1, source_target_pairs={{0,8},{1,9},{2,10},{3,11},{4,12},{5,13},{6,14},{7,15},{8,0},{9,1},... | collective-permute-start | bytes 3932168 | tf_op jit(solution)/shard_map/s2h0/ppermute | solution.py:428
  24.2 0.8 collective-permute-start.4
  25.1 3.5 %collective-permute-start.6 = (bf16[1024,512]{1,0:T(8,128)(2,1)}, bf16[1024,512]{1,0:T(8,128)(2,1)S(1)}, u32[]{:S(2)}, u32[]{:S(2)}) collective-permute-start(bf16[1024,512]{1,0:T(8,128)(2,1)} %get-tuple-element.89), channel_id=1, source_target_pairs={{0,8},{1,9},{2,10},{3,11},{4,12},{5,13},{6,14},{7,15},{8,0},{9,1},... | collective-permute-start | bytes 3145736 | tf_op jit(solution)/shard_map/s1h0/ppermute | solution.py:428
  28.6 1.4 %add_convert_fusion = bf16[128,2560]{1,0:T(8,128)(2,1)S(1)} fusion(bf16[256,2560]{1,0:T(8,128)(2,1)S(1)} %collective-permute-done.2, bf16[256,2560]{1,0:T(8,128)(2,1)} %get-tuple-element.73), kind=kLoop, calls=%fused_computation.1 | loop fusion | flops 1310720 | bytes 1966080 | tf_op jit(solution)/shard_map/convert_element_type | solution.py:447
  30.0 3.8 %shard_map.246 = (bf16[256,1536]{1,0:T(8,128)(2,1)}, bf16[256,1536]{1,0:T(8,128)(2,1)}, bf16[192,512]{1,0:T(8,128)(2,1)}, bf16[4,1536]{1,0:T(4,128)(2,1)}) custom-call(bf16[192,512]{1,0:T(8,128)(2,1)} %get-tuple-element.78.refs_0_, f32[192,512]{1,0:T(8,128)} %get-tuple-element.79.refs_1_, f32[192,512]{1,0:T(8,128)} %get-tuple-element.80.refs_2_, ...), custom_call_target="tpu_custom_call" | custom-call | tf_op jit(solution)/shard_map/pallas_call | solution.py:374
  33.8 3.3 %collective-permute-start.5 = (bf16[256,1536]{1,0:T(8,128)(2,1)}, bf16[256,1536]{1,0:T(8,128)(2,1)S(1)}, u32[]{:S(2)}, u32[]{:S(2)}) collective-permute-start(bf16[256,1536]{1,0:T(8,128)(2,1)} %get-tuple-element.87), channel_id=1, source_target_pairs={{0,8},{1,9},{2,10},{3,11},{4,12},{5,13},{6,14},{7,15},{8,0},{9,1},... | collective-permute-start | bytes 2359304 | tf_op jit(solution)/shard_map/s3h0/ppermute | solution.py:428
  37.1 2.2 %collective-permute-start.9 = (bf16[128,2560]{1,0:T(8,128)(2,1)S(1)}, bf16[128,2560]{1,0:T(8,128)(2,1)S(1)}, u32[]{:S(2)}, u32[]{:S(2)}) collective-permute-start(bf16[128,2560]{1,0:T(8,128)(2,1)S(1)} %add_convert_fusion), channel_id=1, source_target_pairs={{0,2},{1,3},{2,0},{3,1},{4,6},{5,7},{6,4},{7,5},{8,9},{9,8},{10,11... | collective-permute-start | bytes 1966088 | tf_op jit(solution)/shard_map/s2h1/ppermute | solution.py:428
  39.7 2.0 %collective-permute-start.7 = (bf16[132,1536]{1,0:T(8,128)(2,1)S(1)}, bf16[132,1536]{1,0:T(8,128)(2,1)S(1)}, u32[]{:S(2)}, u32[]{:S(2)}) collective-permute-start(bf16[132,1536]{1,0:T(8,128)(2,1)S(1)} %pad_maximum_fusion.5), channel_id=1, source_target_pairs={{0,1},{1,0},{2,3},{3,2},{4,5},{5,4},{6,7},{7,6},{8,24},{9,25},{10,... | collective-permute-start | bytes 1216520 | tf_op jit(solution)/shard_map/s3h1/ppermute | solution.py:428
  41.6 6.2 %collective-permute-done.9 = bf16[128,2560]{1,0:T(8,128)(2,1)S(1)} collective-permute-done((bf16[128,2560]{1,0:T(8,128)(2,1)S(1)}, bf16[128,2560]{1,0:T(8,128)(2,1)S(1)}, u32[]{:S(2)}, u32[]{:S(2)}) %collective-permute-start.9) | collective-permute-done | bytes 655392 | tf_op jit(solution)/shard_map/s2h1/ppermute | solution.py:428
  47.9 2.0 %collective-permute-start.12 = (bf16[64,2560]{1,0:T(8,128)(2,1)S(1)}, bf16[64,2560]{1,0:T(8,128)(2,1)S(1)}, u32[]{:S(2)}, u32[]{:S(2)}) collective-permute-start(bf16[64,2560]{1,0:T(8,128)(2,1)S(1)} %add_convert_fusion.3), channel_id=1, source_target_pairs={{0,1},{1,0},{2,3},{3,2},{4,5},{5,4},{6,7},{7,6},{8,10},{9,11},{10,... | collective-permute-start | bytes 983048 | tf_op jit(solution)/shard_map/s2h2/ppermute | solution.py:428
  50.0 3.5 %collective-permute-done.8 = bf16[512,512]{1,0:T(8,128)(2,1)S(1)} collective-permute-done((bf16[512,512]{1,0:T(8,128)(2,1)S(1)}, bf16[512,512]{1,0:T(8,128)(2,1)S(1)}, u32[]{:S(2)}, u32[]{:S(2)}) %collective-permute-start.8) | collective-permute-done | bytes 524320 | tf_op jit(solution)/shard_map/s1h1/ppermute | solution.py:428
  53.5 1.6 %collective-permute-start.11 = (bf16[256,512]{1,0:T(8,128)(2,1)S(1)}, bf16[256,512]{1,0:T(8,128)(2,1)S(1)}, u32[]{:S(2)}, u32[]{:S(2)}) collective-permute-start(bf16[256,512]{1,0:T(8,128)(2,1)S(1)} %add_convert_fusion.4), channel_id=1, source_target_pairs={{0,16},{1,17},{2,18},{3,19},{4,20},{5,21},{6,22},{7,23},{8,9},{9,8... | collective-permute-start | bytes 786440 | tf_op jit(solution)/shard_map/s1h2/ppermute | solution.py:428
  55.3 0.6 collective-permute-start.10
  55.9 3.1 %collective-permute-start.15 = (bf16[32,2560]{1,0:T(8,128)(2,1)S(1)}, bf16[32,2560]{1,0:T(8,128)(2,1)S(1)}, u32[]{:S(2)}, u32[]{:S(2)}) collective-permute-start(bf16[32,2560]{1,0:T(8,128)(2,1)S(1)} %add_convert_fusion.8), channel_id=1, source_target_pairs={{0,4},{1,5},{2,6},{3,7},{4,0},{5,1},{6,2},{7,3},{8,24},{9,25},{10,... | collective-permute-start | bytes 491528 | tf_op jit(solution)/shard_map/s2h3/ppermute | solution.py:428
  59.0 1.0 collective-permute-done.11
  60.1 2.2 %collective-permute-start.14 = (bf16[128,512]{1,0:T(8,128)(2,1)S(1)}, bf16[128,512]{1,0:T(8,128)(2,1)S(1)}, u32[]{:S(2)}, u32[]{:S(2)}) collective-permute-start(bf16[128,512]{1,0:T(8,128)(2,1)S(1)} %add_convert_fusion.11), channel_id=1, source_target_pairs={{0,1},{1,0},{2,3},{3,2},{4,5},{5,4},{6,7},{7,6},{8,10},{9,11},{10,... | collective-permute-start | bytes 393224 | tf_op jit(solution)/shard_map/s1h3/ppermute | solution.py:428
  62.3 1.8 %collective-permute-done.10 = bf16[68,1536]{1,0:T(8,128)(2,1)S(1)} collective-permute-done((bf16[68,1536]{1,0:T(8,128)(2,1)S(1)}, bf16[68,1536]{1,0:T(8,128)(2,1)S(1)}, u32[]{:S(2)}, u32[]{:S(2)}) %collective-permute-start.10) | collective-permute-done | bytes 208928 | tf_op jit(solution)/shard_map/s3h2/ppermute | solution.py:428
  64.2 3.1 %collective-permute-start.13 = (bf16[36,1536]{1,0:T(8,128)(2,1)S(1)}, bf16[36,1536]{1,0:T(8,128)(2,1)S(1)}, u32[]{:S(2)}, u32[]{:S(2)}) collective-permute-start(bf16[36,1536]{1,0:T(8,128)(2,1)S(1)} %pad_maximum_fusion.11), channel_id=1, source_target_pairs={{0,4},{1,5},{2,6},{3,7},{4,0},{5,1},{6,2},{7,3},{8,12},{9,13},{10,... | collective-permute-start | bytes 331784 | tf_op jit(solution)/shard_map/s3h3/ppermute | solution.py:428
  67.4 1.1 collective-permute-start.18
  69.1 8.1 %collective-permute-done.13 = bf16[36,1536]{1,0:T(8,128)(2,1)S(1)} collective-permute-done((bf16[36,1536]{1,0:T(8,128)(2,1)S(1)}, bf16[36,1536]{1,0:T(8,128)(2,1)S(1)}, u32[]{:S(2)}, u32[]{:S(2)}) %collective-permute-start.13) | collective-permute-done | bytes 110624 | tf_op jit(solution)/shard_map/s3h3/ppermute | solution.py:428
  77.4 3.0 %collective-permute-start.20 = (bf16[32,2560]{1,0:T(8,128)(2,1)S(1)}, bf16[32,2560]{1,0:T(8,128)(2,1)S(1)}, u32[]{:S(2)}, u32[]{:S(2)}) collective-permute-start(bf16[32,2560]{1,0:T(8,128)(2,1)S(1)} %add_convert_fusion.6), channel_id=1, source_target_pairs={{0,4},{1,5},{2,6},{3,7},{4,0},{5,1},{6,2},{7,3},{8,24},{9,25},{10,... | collective-permute-start | bytes 491528 | tf_op jit(solution)/shard_map/s2h5/ppermute | solution.py:428
  80.5 1.6 %collective-permute-start.23 = (bf16[128,512]{1,0:T(8,128)(2,1)S(1)}, bf16[128,512]{1,0:T(8,128)(2,1)S(1)}, u32[]{:S(2)}, u32[]{:S(2)}) collective-permute-start(bf16[128,512]{1,0:T(8,128)(2,1)S(1)} %add_convert_fusion.9), channel_id=1, source_target_pairs={{0,1},{1,0},{2,3},{3,2},{4,5},{5,4},{6,7},{7,6},{8,10},{9,11},{10,... | collective-permute-start | bytes 393224 | tf_op jit(solution)/shard_map/s1h5/ppermute | solution.py:428
  82.1 2.6 %collective-permute-done.16 = bf16[36,1536]{1,0:T(8,128)(2,1)S(1)} collective-permute-done((bf16[36,1536]{1,0:T(8,128)(2,1)S(1)}, bf16[36,1536]{1,0:T(8,128)(2,1)S(1)}, u32[]{:S(2)}, u32[]{:S(2)}) %collective-permute-start.16) | collective-permute-done | bytes 110624 | tf_op jit(solution)/shard_map/s3h4/ppermute | solution.py:428
  84.9 1.1 collective-permute-done.19
  86.0 0.6 slice.222
  86.6 1.8 %collective-permute-start.22 = (bf16[64,2560]{1,0:T(8,128)(2,1)S(1)}, bf16[64,2560]{1,0:T(8,128)(2,1)S(1)}, u32[]{:S(2)}, u32[]{:S(2)}) collective-permute-start(bf16[64,2560]{1,0:T(8,128)(2,1)S(1)} %pad_maximum_fusion.7), channel_id=1, source_target_pairs={{0,1},{1,0},{2,3},{3,2},{4,5},{5,4},{6,7},{7,6},{8,10},{9,11},{10,... | collective-permute-start | bytes 983048 | tf_op jit(solution)/shard_map/s2h6/ppermute | solution.py:428
  88.4 0.6 copy.32
  89.0 0.6 fusion
  89.6 0.7 collective-permute-start.21
  90.3 1.8 %collective-permute-start.25 = (bf16[256,512]{1,0:T(8,128)(2,1)S(1)}, bf16[256,512]{1,0:T(8,128)(2,1)S(1)}, u32[]{:S(2)}, u32[]{:S(2)}) collective-permute-start(bf16[256,512]{1,0:T(8,128)(2,1)S(1)} %pad_maximum_fusion.8), channel_id=1, source_target_pairs={{0,16},{1,17},{2,18},{3,19},{4,20},{5,21},{6,22},{7,23},{8,9},{9,8... | collective-permute-start | bytes 786440 | tf_op jit(solution)/shard_map/s1h6/ppermute | solution.py:428
  92.1 2.9 %collective-permute-done.22 = bf16[64,2560]{1,0:T(8,128)(2,1)S(1)} collective-permute-done((bf16[64,2560]{1,0:T(8,128)(2,1)S(1)}, bf16[64,2560]{1,0:T(8,128)(2,1)S(1)}, u32[]{:S(2)}, u32[]{:S(2)}) %collective-permute-start.22) | collective-permute-done | bytes 327712 | tf_op jit(solution)/shard_map/s2h6/ppermute | solution.py:428
  95.0 2.1 %collective-permute-start.28 = (bf16[128,2560]{1,0:T(8,128)(2,1)S(1)}, bf16[128,2560]{1,0:T(8,128)(2,1)S(1)}, u32[]{:S(2)}, u32[]{:S(2)}) collective-permute-start(bf16[128,2560]{1,0:T(8,128)(2,1)S(1)} %pad_maximum_fusion.3), channel_id=1, source_target_pairs={{0,2},{1,3},{2,0},{3,1},{4,6},{5,7},{6,4},{7,5},{8,9},{9,8},{10,11... | collective-permute-start | bytes 1966088 | tf_op jit(solution)/shard_map/s2h7/ppermute | solution.py:428
  97.1 1.5 %collective-permute-start.24 = (bf16[64,1536]{1,0:T(8,128)(2,1)S(1)}, bf16[64,1536]{1,0:T(8,128)(2,1)S(1)}, u32[]{:S(2)}, u32[]{:S(2)}) collective-permute-start(bf16[64,1536]{1,0:T(8,128)(2,1)S(1)} %pad_maximum_fusion.10), channel_id=1, source_target_pairs={{0,16},{1,17},{2,18},{3,19},{4,20},{5,21},{6,22},{7,23},{8,9},{9,8... | collective-permute-start | bytes 589832 | tf_op jit(solution)/shard_map/s3h7/ppermute | solution.py:428
  98.8 6.3 %collective-permute-done.24 = bf16[64,1536]{1,0:T(8,128)(2,1)S(1)} collective-permute-done((bf16[64,1536]{1,0:T(8,128)(2,1)S(1)}, bf16[64,1536]{1,0:T(8,128)(2,1)S(1)}, u32[]{:S(2)}, u32[]{:S(2)}) %collective-permute-start.24) | collective-permute-done | bytes 196640 | tf_op jit(solution)/shard_map/s3h7/ppermute | solution.py:428
  105.1 1.6 %collective-permute-start.26 = (bf16[128,1536]{1,0:T(8,128)(2,1)S(1)}, bf16[128,1536]{1,0:T(8,128)(2,1)S(1)}, u32[]{:S(2)}, u32[]{:S(2)}) collective-permute-start(bf16[128,1536]{1,0:T(8,128)(2,1)S(1)} %pad_maximum_fusion.6), channel_id=1, source_target_pairs={{0,1},{1,0},{2,3},{3,2},{4,5},{5,4},{6,7},{7,6},{8,24},{9,25},{10,... | collective-permute-start | bytes 1179656 | tf_op jit(solution)/shard_map/s3h8/ppermute | solution.py:428
  106.7 0.9 collective-permute-start.31
  107.7 1.6 %shard_map.247 = (f32[512,2048]{1,0:T(8,128)}, f32[512,512]{1,0:T(8,128)}) custom-call(bf16[256,2560]{1,0:T(8,128)(2,1)S(1)} %pad_maximum_fusion.piece), custom_call_target="tpu_custom_call" | custom-call | tf_op jit(solution)/shard_map/pallas_call | solution.py:358
  109.3 2.0 %collective-permute-done.27 = bf16[512,512]{1,0:T(8,128)(2,1)S(1)} collective-permute-done((bf16[512,512]{1,0:T(8,128)(2,1)S(1)}, bf16[512,512]{1,0:T(8,128)(2,1)S(1)}, u32[]{:S(2)}, u32[]{:S(2)}) %collective-permute-start.27) | collective-permute-done | bytes 524320 | tf_op jit(solution)/shard_map/s1h7/ppermute | solution.py:428
  111.5 1.4 %shard_map.248.refs_0_ = f32[2048,512]{1,0:T(8,128)} custom-call(bf16[1024,512]{1,0:T(8,128)(2,1)S(1)} %pad_maximum_fusion.1.piece), custom_call_target="tpu_custom_call" | custom-call | tf_op jit(solution)/shard_map/pallas_call | solution.py:358
  113.0 0.6 collective-permute-start.29
  113.5 1.2 %shard_map.249.refs_0_ = f32[512,1536]{1,0:T(8,128)} custom-call(bf16[256,1536]{1,0:T(8,128)(2,1)S(1)} %pad_maximum_fusion.2.piece), custom_call_target="tpu_custom_call" | custom-call | tf_op jit(solution)/shard_map/pallas_call | solution.py:358
  114.8 1.6 %shard_map.250 = (f32[512,2048]{1,0:T(8,128)}, f32[512,512]{1,0:T(8,128)}) custom-call(bf16[256,2560]{1,0:T(8,128)(2,1)S(1)} %collective-permute-done.31.piece, f32[512,2048]{1,0:T(8,128)} %get-tuple-element.114.refs_0_, f32[512,512]{1,0:T(8,128)} %get-tuple-element.121.refs_1_), custom_call_target="tpu_custom_call", output_to_operand_aliasing={{0}: (1, {}), {1}: (2, {})} | custom-call | tf_op jit(solution)/shard_map/pallas_call | solution.py:358
  116.4 1.4 %shard_map.251 = f32[2048,512]{1,0:T(8,128)} custom-call(bf16[1024,512]{1,0:T(8,128)(2,1)S(1)} %collective-permute-done.30.piece, f32[2048,512]{1,0:T(8,128)} %shard_map.248.refs_0_), custom_call_target="tpu_custom_call", output_to_operand_aliasing={{}: (1, {})} | custom-call | tf_op jit(solution)/shard_map/pallas_call | solution.py:358
  117.8 1.2 %shard_map.252 = f32[512,1536]{1,0:T(8,128)} custom-call(bf16[256,1536]{1,0:T(8,128)(2,1)S(1)} %collective-permute-done.29.piece, f32[512,1536]{1,0:T(8,128)} %shard_map.249.refs_0_), custom_call_target="tpu_custom_call", output_to_operand_aliasing={{}: (1, {})} | custom-call | tf_op jit(solution)/shard_map/pallas_call | solution.py:358
  (79 shorter events, 3.5 us)
Async XLA Ops:
  1.6 1.5 %collective-permute-start = (bf16[96,512]{1,0:T(8,128)(2,1)S(1)}, bf16[96,512]{1,0:T(8,128)(2,1)S(1)}, u32[]{:S(2)}, u32[]{:S(2)}) collective-permute-start(bf16[96,512]{1,0:T(8,128)(2,1)S(1)} %bitcast.19), channel_id=1, source_target_pairs={{0,8},{1,9},{2,10},{3,11},{4,12},{5,13},{6,14},{7,15},{8,0},{9,1},... | collective-permute-start | bytes 294920 | tf_op jit(solution)/shard_map/ppermute | solution.py:428
  2.1 0.9 collective-permute-start.1
  3.1 0.7 copy-start.5
  3.1 0.7 copy-start.6
  18.3 10.3 %collective-permute-start.2 = (bf16[256,2560]{1,0:T(8,128)(2,1)}, bf16[256,2560]{1,0:T(8,128)(2,1)S(1)}, u32[]{:S(2)}, u32[]{:S(2)}) collective-permute-start(bf16[256,2560]{1,0:T(8,128)(2,1)} %get-tuple-element.74), channel_id=1, source_target_pairs={{0,8},{1,9},{2,10},{3,11},{4,12},{5,13},{6,14},{7,15},{8,0},{9,1},... | collective-permute-start | bytes 3932168 | tf_op jit(solution)/shard_map/s2h0/ppermute | solution.py:428
  24.1 4.4 %collective-permute-start.3 = (bf16[2,96,512]{2,1,0:T(8,128)(2,1)}, bf16[2,96,512]{2,1,0:T(8,128)(2,1)S(1)}, u32[]{:S(2)}, u32[]{:S(2)}) collective-permute-start(bf16[2,96,512]{2,1,0:T(8,128)(2,1)} %get-tuple-element.75), channel_id=1, source_target_pairs={{0,8},{1,9},{2,10},{3,11},{4,12},{5,13},{6,14},{7,15},{8,0},{9,1},... | collective-permute-start | bytes 589832 | tf_op jit(solution)/shard_map/ppermute | solution.py:428
  24.2 4.3 %collective-permute-start.4 = (bf16[2,96,512]{2,1,0:T(8,128)(2,1)}, bf16[2,96,512]{2,1,0:T(8,128)(2,1)S(1)}, u32[]{:S(2)}, u32[]{:S(2)}) collective-permute-start(bf16[2,96,512]{2,1,0:T(8,128)(2,1)} %get-tuple-element.76), channel_id=1, source_target_pairs={{8,16},{16,8},{9,17},{17,9},{10,18},{18,10},{11,19},{19,11},{12,20... | collective-permute-start | bytes 589832 | tf_op jit(solution)/shard_map/ppermute | solution.py:420
  25.1 14.2 %collective-permute-start.6 = (bf16[1024,512]{1,0:T(8,128)(2,1)}, bf16[1024,512]{1,0:T(8,128)(2,1)S(1)}, u32[]{:S(2)}, u32[]{:S(2)}) collective-permute-start(bf16[1024,512]{1,0:T(8,128)(2,1)} %get-tuple-element.89), channel_id=1, source_target_pairs={{0,8},{1,9},{2,10},{3,11},{4,12},{5,13},{6,14},{7,15},{8,0},{9,1},... | collective-permute-start | bytes 3145736 | tf_op jit(solution)/shard_map/s1h0/ppermute | solution.py:428
  28.5 1.4 %copy-start.3 = (bf16[2,96,512]{2,1,0:T(8,128)(2,1)}, bf16[2,96,512]{2,1,0:T(8,128)(2,1)S(1)}, u32[]{:S(2)}) copy-start(bf16[2,96,512]{2,1,0:T(8,128)(2,1)S(1)} %collective-permute-done.3.refs_3_) | copy-start | bytes 589828
  28.6 1.4 %copy-start.4 = (bf16[2,96,512]{2,1,0:T(8,128)(2,1)}, bf16[2,96,512]{2,1,0:T(8,128)(2,1)S(1)}, u32[]{:S(2)}) copy-start(bf16[2,96,512]{2,1,0:T(8,128)(2,1)S(1)} %collective-permute-done.4.refs_4_) | copy-start | bytes 589828
  30.0 9.3 %copy-start.1 = (bf16[1024,512]{1,0:T(8,128)(2,1)S(1)}, bf16[1024,512]{1,0:T(8,128)(2,1)}, u32[]{:S(2)}) copy-start(bf16[1024,512]{1,0:T(8,128)(2,1)} %get-tuple-element.88) | copy-start | bytes 3145732
  33.8 5.7 %copy-start.2 = (bf16[256,1536]{1,0:T(8,128)(2,1)S(1)}, bf16[256,1536]{1,0:T(8,128)(2,1)}, u32[]{:S(2)}) copy-start(bf16[256,1536]{1,0:T(8,128)(2,1)} %get-tuple-element.86) | copy-start | bytes 2359300
  33.8 5.8 %copy-start.7 = (bf16[4,1536]{1,0:T(4,128)(2,1)S(1)}, bf16[4,1536]{1,0:T(4,128)(2,1)}, u32[]{:S(2)}) copy-start(bf16[4,1536]{1,0:T(4,128)(2,1)} %get-tuple-element.85) | copy-start | bytes 36868
  33.8 5.7 %collective-permute-start.5 = (bf16[256,1536]{1,0:T(8,128)(2,1)}, bf16[256,1536]{1,0:T(8,128)(2,1)S(1)}, u32[]{:S(2)}, u32[]{:S(2)}) collective-permute-start(bf16[256,1536]{1,0:T(8,128)(2,1)} %get-tuple-element.87), channel_id=1, source_target_pairs={{0,8},{1,9},{2,10},{3,11},{4,12},{5,13},{6,14},{7,15},{8,0},{9,1},... | collective-permute-start | bytes 2359304 | tf_op jit(solution)/shard_map/s3h0/ppermute | solution.py:428
  37.1 10.8 %collective-permute-start.9 = (bf16[128,2560]{1,0:T(8,128)(2,1)S(1)}, bf16[128,2560]{1,0:T(8,128)(2,1)S(1)}, u32[]{:S(2)}, u32[]{:S(2)}) collective-permute-start(bf16[128,2560]{1,0:T(8,128)(2,1)S(1)} %add_convert_fusion), channel_id=1, source_target_pairs={{0,2},{1,3},{2,0},{3,1},{4,6},{5,7},{6,4},{7,5},{8,9},{9,8},{10,11... | collective-permute-start | bytes 1966088 | tf_op jit(solution)/shard_map/s2h1/ppermute | solution.py:428
  39.3 8.6 %copy-start = (bf16[256,2560]{1,0:T(8,128)(2,1)S(1)}, bf16[256,2560]{1,0:T(8,128)(2,1)}, u32[]{:S(2)}) copy-start(bf16[256,2560]{1,0:T(8,128)(2,1)} %get-tuple-element.73) | copy-start | bytes 3932164
  39.4 14.0 %collective-permute-start.8 = (bf16[512,512]{1,0:T(8,128)(2,1)S(1)}, bf16[512,512]{1,0:T(8,128)(2,1)S(1)}, u32[]{:S(2)}, u32[]{:S(2)}) collective-permute-start(bf16[512,512]{1,0:T(8,128)(2,1)S(1)} %add_convert_fusion.1), channel_id=1, source_target_pairs={{0,2},{1,3},{2,0},{3,1},{4,6},{5,7},{6,4},{7,5},{8,24},{9,25},{10,... | collective-permute-start | bytes 1572872 | tf_op jit(solution)/shard_map/s1h1/ppermute | solution.py:428
  39.7 15.5 %collective-permute-start.7 = (bf16[132,1536]{1,0:T(8,128)(2,1)S(1)}, bf16[132,1536]{1,0:T(8,128)(2,1)S(1)}, u32[]{:S(2)}, u32[]{:S(2)}) collective-permute-start(bf16[132,1536]{1,0:T(8,128)(2,1)S(1)} %pad_maximum_fusion.5), channel_id=1, source_target_pairs={{0,1},{1,0},{2,3},{3,2},{4,5},{5,4},{6,7},{7,6},{8,24},{9,25},{10,... | collective-permute-start | bytes 1216520 | tf_op jit(solution)/shard_map/s3h1/ppermute | solution.py:428
  47.9 7.9 %collective-permute-start.12 = (bf16[64,2560]{1,0:T(8,128)(2,1)S(1)}, bf16[64,2560]{1,0:T(8,128)(2,1)S(1)}, u32[]{:S(2)}, u32[]{:S(2)}) collective-permute-start(bf16[64,2560]{1,0:T(8,128)(2,1)S(1)} %add_convert_fusion.3), channel_id=1, source_target_pairs={{0,1},{1,0},{2,3},{3,2},{4,5},{5,4},{6,7},{7,6},{8,10},{9,11},{10,... | collective-permute-start | bytes 983048 | tf_op jit(solution)/shard_map/s2h2/ppermute | solution.py:428
  53.5 6.4 %collective-permute-start.11 = (bf16[256,512]{1,0:T(8,128)(2,1)S(1)}, bf16[256,512]{1,0:T(8,128)(2,1)S(1)}, u32[]{:S(2)}, u32[]{:S(2)}) collective-permute-start(bf16[256,512]{1,0:T(8,128)(2,1)S(1)} %add_convert_fusion.4), channel_id=1, source_target_pairs={{0,16},{1,17},{2,18},{3,19},{4,20},{5,21},{6,22},{7,23},{8,9},{9,8... | collective-permute-start | bytes 786440 | tf_op jit(solution)/shard_map/s1h2/ppermute | solution.py:428
  55.3 8.9 %collective-permute-start.10 = (bf16[68,1536]{1,0:T(8,128)(2,1)S(1)}, bf16[68,1536]{1,0:T(8,128)(2,1)S(1)}, u32[]{:S(2)}, u32[]{:S(2)}) collective-permute-start(bf16[68,1536]{1,0:T(8,128)(2,1)S(1)} %pad_maximum_fusion.9), channel_id=1, source_target_pairs={{0,16},{1,17},{2,18},{3,19},{4,20},{5,21},{6,22},{7,23},{8,9},{9,8... | collective-permute-start | bytes 626696 | tf_op jit(solution)/shard_map/s3h2/ppermute | solution.py:428
  55.9 11.4 %collective-permute-start.15 = (bf16[32,2560]{1,0:T(8,128)(2,1)S(1)}, bf16[32,2560]{1,0:T(8,128)(2,1)S(1)}, u32[]{:S(2)}, u32[]{:S(2)}) collective-permute-start(bf16[32,2560]{1,0:T(8,128)(2,1)S(1)} %add_convert_fusion.8), channel_id=1, source_target_pairs={{0,4},{1,5},{2,6},{3,7},{4,0},{5,1},{6,2},{7,3},{8,24},{9,25},{10,... | collective-permute-start | bytes 491528 | tf_op jit(solution)/shard_map/s2h3/ppermute | solution.py:428
  60.1 8.5 %collective-permute-start.14 = (bf16[128,512]{1,0:T(8,128)(2,1)S(1)}, bf16[128,512]{1,0:T(8,128)(2,1)S(1)}, u32[]{:S(2)}, u32[]{:S(2)}) collective-permute-start(bf16[128,512]{1,0:T(8,128)(2,1)S(1)} %add_convert_fusion.11), channel_id=1, source_target_pairs={{0,1},{1,0},{2,3},{3,2},{4,5},{5,4},{6,7},{7,6},{8,10},{9,11},{10,... | collective-permute-start | bytes 393224 | tf_op jit(solution)/shard_map/s1h3/ppermute | solution.py:428
  64.2 13.0 %collective-permute-start.13 = (bf16[36,1536]{1,0:T(8,128)(2,1)S(1)}, bf16[36,1536]{1,0:T(8,128)(2,1)S(1)}, u32[]{:S(2)}, u32[]{:S(2)}) collective-permute-start(bf16[36,1536]{1,0:T(8,128)(2,1)S(1)} %pad_maximum_fusion.11), channel_id=1, source_target_pairs={{0,4},{1,5},{2,6},{3,7},{4,0},{5,1},{6,2},{7,3},{8,12},{9,13},{10,... | collective-permute-start | bytes 331784 | tf_op jit(solution)/shard_map/s3h3/ppermute | solution.py:428
  67.4 9.9 %collective-permute-start.18 = (bf16[32,2560]{1,0:T(8,128)(2,1)S(1)}, bf16[32,2560]{1,0:T(8,128)(2,1)S(1)}, u32[]{:S(2)}, u32[]{:S(2)}) collective-permute-start(bf16[32,2560]{1,0:T(8,128)(2,1)S(1)} %add_convert_fusion.7), channel_id=1, source_target_pairs={{0,16},{1,17},{2,18},{3,19},{4,20},{5,21},{6,22},{7,23},{8,12},{9,... | collective-permute-start | bytes 491528 | tf_op jit(solution)/shard_map/s2h4/ppermute | solution.py:428
  68.7 11.8 %collective-permute-start.17 = (bf16[128,512]{1,0:T(8,128)(2,1)S(1)}, bf16[128,512]{1,0:T(8,128)(2,1)S(1)}, u32[]{:S(2)}, u32[]{:S(2)}) collective-permute-start(bf16[128,512]{1,0:T(8,128)(2,1)S(1)} %add_convert_fusion.10), channel_id=1, source_target_pairs={{0,4},{1,5},{2,6},{3,7},{4,0},{5,1},{6,2},{7,3},{8,12},{9,13},{10,... | collective-permute-start | bytes 393224 | tf_op jit(solution)/shard_map/s1h4/ppermute | solution.py:428
  77.3 7.4 %collective-permute-start.16 = (bf16[36,1536]{1,0:T(8,128)(2,1)S(1)}, bf16[36,1536]{1,0:T(8,128)(2,1)S(1)}, u32[]{:S(2)}, u32[]{:S(2)}) collective-permute-start(bf16[36,1536]{1,0:T(8,128)(2,1)S(1)} %pad_maximum_fusion.12), channel_id=1, source_target_pairs={{0,2},{1,3},{2,0},{3,1},{4,6},{5,7},{6,4},{7,5},{8,10},{9,11},{10,... | collective-permute-start | bytes 331784 | tf_op jit(solution)/shard_map/s3h4/ppermute | solution.py:428
  77.4 7.4 %collective-permute-start.20 = (bf16[32,2560]{1,0:T(8,128)(2,1)S(1)}, bf16[32,2560]{1,0:T(8,128)(2,1)S(1)}, u32[]{:S(2)}, u32[]{:S(2)}) collective-permute-start(bf16[32,2560]{1,0:T(8,128)(2,1)S(1)} %add_convert_fusion.6), channel_id=1, source_target_pairs={{0,4},{1,5},{2,6},{3,7},{4,0},{5,1},{6,2},{7,3},{8,24},{9,25},{10,... | collective-permute-start | bytes 491528 | tf_op jit(solution)/shard_map/s2h5/ppermute | solution.py:428
  80.5 9.8 %collective-permute-start.23 = (bf16[128,512]{1,0:T(8,128)(2,1)S(1)}, bf16[128,512]{1,0:T(8,128)(2,1)S(1)}, u32[]{:S(2)}, u32[]{:S(2)}) collective-permute-start(bf16[128,512]{1,0:T(8,128)(2,1)S(1)} %add_convert_fusion.9), channel_id=1, source_target_pairs={{0,1},{1,0},{2,3},{3,2},{4,5},{5,4},{6,7},{7,6},{8,10},{9,11},{10,... | collective-permute-start | bytes 393224 | tf_op jit(solution)/shard_map/s1h5/ppermute | solution.py:428
  84.8 1.2 %collective-permute-start.19 = (bf16[4,1536]{1,0:T(4,128)(2,1)S(1)}, bf16[4,1536]{1,0:T(4,128)(2,1)S(1)}, u32[]{:S(2)}, u32[]{:S(2)}) collective-permute-start(bf16[4,1536]{1,0:T(4,128)(2,1)S(1)} %add_convert_fusion.15), channel_id=1, source_target_pairs={{0,8},{1,9},{2,10},{3,11},{4,12},{5,13},{6,14},{7,15},{8,0},{9,1},... | collective-permute-start | bytes 36872 | tf_op jit(solution)/shard_map/s3h5/ppermute | solution.py:428
  86.6 8.4 %collective-permute-start.22 = (bf16[64,2560]{1,0:T(8,128)(2,1)S(1)}, bf16[64,2560]{1,0:T(8,128)(2,1)S(1)}, u32[]{:S(2)}, u32[]{:S(2)}) collective-permute-start(bf16[64,2560]{1,0:T(8,128)(2,1)S(1)} %pad_maximum_fusion.7), channel_id=1, source_target_pairs={{0,1},{1,0},{2,3},{3,2},{4,5},{5,4},{6,7},{7,6},{8,10},{9,11},{10,... | collective-permute-start | bytes 983048 | tf_op jit(solution)/shard_map/s2h6/ppermute | solution.py:428
  89.6 7.5 %collective-permute-start.21 = (bf16[32,1536]{1,0:T(8,128)(2,1)S(1)}, bf16[32,1536]{1,0:T(8,128)(2,1)S(1)}, u32[]{:S(2)}, u32[]{:S(2)}) collective-permute-start(bf16[32,1536]{1,0:T(8,128)(2,1)S(1)} %add_convert_fusion.12), channel_id=1, source_target_pairs={{0,4},{1,5},{2,6},{3,7},{4,0},{5,1},{6,2},{7,3},{8,12},{9,13},{10,... | collective-permute-start | bytes 294920 | tf_op jit(solution)/shard_map/s3h6/ppermute | solution.py:428
  90.3 8.3 %collective-permute-start.25 = (bf16[256,512]{1,0:T(8,128)(2,1)S(1)}, bf16[256,512]{1,0:T(8,128)(2,1)S(1)}, u32[]{:S(2)}, u32[]{:S(2)}) collective-permute-start(bf16[256,512]{1,0:T(8,128)(2,1)S(1)} %pad_maximum_fusion.8), channel_id=1, source_target_pairs={{0,16},{1,17},{2,18},{3,19},{4,20},{5,21},{6,22},{7,23},{8,9},{9,8... | collective-permute-start | bytes 786440 | tf_op jit(solution)/shard_map/s1h6/ppermute | solution.py:428
  95.0 11.6 %collective-permute-start.28 = (bf16[128,2560]{1,0:T(8,128)(2,1)S(1)}, bf16[128,2560]{1,0:T(8,128)(2,1)S(1)}, u32[]{:S(2)}, u32[]{:S(2)}) collective-permute-start(bf16[128,2560]{1,0:T(8,128)(2,1)S(1)} %pad_maximum_fusion.3), channel_id=1, source_target_pairs={{0,2},{1,3},{2,0},{3,1},{4,6},{5,7},{6,4},{7,5},{8,9},{9,8},{10,11... | collective-permute-start | bytes 1966088 | tf_op jit(solution)/shard_map/s2h7/ppermute | solution.py:428
  97.1 7.9 %collective-permute-start.24 = (bf16[64,1536]{1,0:T(8,128)(2,1)S(1)}, bf16[64,1536]{1,0:T(8,128)(2,1)S(1)}, u32[]{:S(2)}, u32[]{:S(2)}) collective-permute-start(bf16[64,1536]{1,0:T(8,128)(2,1)S(1)} %pad_maximum_fusion.10), channel_id=1, source_target_pairs={{0,16},{1,17},{2,18},{3,19},{4,20},{5,21},{6,22},{7,23},{8,9},{9,8... | collective-permute-start | bytes 589832 | tf_op jit(solution)/shard_map/s3h7/ppermute | solution.py:428
  98.7 12.6 %collective-permute-start.27 = (bf16[512,512]{1,0:T(8,128)(2,1)S(1)}, bf16[512,512]{1,0:T(8,128)(2,1)S(1)}, u32[]{:S(2)}, u32[]{:S(2)}) collective-permute-start(bf16[512,512]{1,0:T(8,128)(2,1)S(1)} %pad_maximum_fusion.4), channel_id=1, source_target_pairs={{0,2},{1,3},{2,0},{3,1},{4,6},{5,7},{6,4},{7,5},{8,24},{9,25},{10,... | collective-permute-start | bytes 1572872 | tf_op jit(solution)/shard_map/s1h7/ppermute | solution.py:428
  105.1 7.8 %collective-permute-start.26 = (bf16[128,1536]{1,0:T(8,128)(2,1)S(1)}, bf16[128,1536]{1,0:T(8,128)(2,1)S(1)}, u32[]{:S(2)}, u32[]{:S(2)}) collective-permute-start(bf16[128,1536]{1,0:T(8,128)(2,1)S(1)} %pad_maximum_fusion.6), channel_id=1, source_target_pairs={{0,1},{1,0},{2,3},{3,2},{4,5},{5,4},{6,7},{7,6},{8,24},{9,25},{10,... | collective-permute-start | bytes 1179656 | tf_op jit(solution)/shard_map/s3h8/ppermute | solution.py:428
  106.7 8.0 %collective-permute-start.31 = (bf16[256,2560]{1,0:T(8,128)(2,1)S(1)}, bf16[256,2560]{1,0:T(8,128)(2,1)S(1)}, u32[]{:S(2)}, u32[]{:S(2)}) collective-permute-start(bf16[256,2560]{1,0:T(8,128)(2,1)S(1)} %pad_maximum_fusion.piece), channel_id=1, source_target_pairs={{0,8},{1,9},{2,10},{3,11},{4,12},{5,13},{6,14},{7,15},{8,0},{9,1},... | collective-permute-start | bytes 3932168 | tf_op jit(solution)/shard_map/s2h8/ppermute | solution.py:428
  111.4 5.0 %collective-permute-start.30 = (bf16[1024,512]{1,0:T(8,128)(2,1)S(1)}, bf16[1024,512]{1,0:T(8,128)(2,1)S(1)}, u32[]{:S(2)}, u32[]{:S(2)}) collective-permute-start(bf16[1024,512]{1,0:T(8,128)(2,1)S(1)} %pad_maximum_fusion.1.piece), channel_id=1, source_target_pairs={{0,8},{1,9},{2,10},{3,11},{4,12},{5,13},{6,14},{7,15},{8,0},{9,1},... | collective-permute-start | bytes 3145736 | tf_op jit(solution)/shard_map/s1h8/ppermute | solution.py:428
  113.0 4.9 %collective-permute-start.29 = (bf16[256,1536]{1,0:T(8,128)(2,1)S(1)}, bf16[256,1536]{1,0:T(8,128)(2,1)S(1)}, u32[]{:S(2)}, u32[]{:S(2)}) collective-permute-start(bf16[256,1536]{1,0:T(8,128)(2,1)S(1)} %pad_maximum_fusion.2.piece), channel_id=1, source_target_pairs={{0,8},{1,9},{2,10},{3,11},{4,12},{5,13},{6,14},{7,15},{8,0},{9,1},... | collective-permute-start | bytes 2359304 | tf_op jit(solution)/shard_map/s3h9/ppermute | solution.py:428

commit v3 on v2

--- a/solution.py
+++ b/solution.py
@@ -17,8 +17,8 @@
 SQRT_HALF = 0.5**0.5
 PHI_SCALE = (2.0 * math.pi) ** (-0.5)
 NEGATIVE = -1e30
-ORDERS = (("zxyw", "xyzw"), ("zywx", "yzxw"), ("yxwz", "xywz"))
-ORDER = (2, 3, 1, 3, 2, 1, 3, 2, 1, 3, 2, 1, 3, 2, 1, 3, 2, 3, 1, 2, 3, 1, 3, 2, 1, 3, 2, 1, 3)
+ORDERS = (("zxyw", "xyzw"), ("yzxw", "zywx"), ("yxwz", "xywz"))
+ORDER = (2, 3, 1, 3, 2, 1, 3, 2, 1, 3, 2, 1, 3, 2, 1, 2, 3, 1, 2, 3, 1, 3, 2, 1, 3, 2, 1, 3)
 
 f32 = jnp.float32
 bf16 = jnp.bfloat16
@@ -326,50 +326,70 @@
         copy.wait()
 
 
-def spread_kernel(axes, stream, shards, splits, other, piece, *refs):
+def spread_kernel(axes, stream, shards, splits, other, sums, *refs):
     count = len(splits)
-    outs, wide, sems = refs[-2 * count - 1 : -count - 1], refs[-count - 1 : -1], refs[-1]
-    half = piece.shape[0]
-    per = half // shards
+    piece = refs[0]
+    outs = refs[-2 * (count + len(sums)) - 1 : -count - len(sums) - 1]
+    wide, sems = refs[-count - len(sums) - 1 : -1], refs[-1]
     core = axes.bit(axes.core)
     owner = 1 - core if other else core
     slot = axes.slot(stream, owner)
+    per = outs[0].shape[0] // (2 * shards)
     copies = []
+
+    def leave(source, target, index, part):
+        copy = pltpu.make_async_copy(source, target, sems.at[index, part])
+        copy.start()
+        copies.append(copy)
+
     for index in range(shards):
-        spot = pl.multiple_of(owner * half + (index ^ slot) * per, per)
+        spot = pl.multiple_of((owner * shards + (index ^ slot)) * per, per)
         rows = slice(index * per, (index + 1) * per)
         first = 0
-        for part, (out, buffer, width) in enumerate(zip(outs, wide, splits)):
-            buffer[rows, :] = piece[rows, first : first + width].astype(f32)
+        for part, width in enumerate(splits):
+            wide[part][rows, :] = piece[rows, first : first + width].astype(f32)
             first += width
-            copy = pltpu.make_async_copy(
-                buffer.at[rows, :], out.at[pl.ds(spot, per), :], sems.at[index, part]
-            )
-            copy.start()
-            copies.append(copy)
+            leave(wide[part].at[rows, :], outs[part].at[pl.ds(spot, per), :], index, part)
+    if sums:
+        rows = slice(shards * per, piece.shape[0])
+        total = refs[1][rows, :].astype(f32) + piece[rows, :].astype(f32)
+        width = total.shape[1] // 3
+        taken = [total[k // 3 : k // 3 + 1, k % 3 * width : (k % 3 + 1) * width] for k in range(3 * total.shape[0])]
+        for part, (first, shape) in enumerate(sums):
+            buffer = wide[count + part]
+            for k in range(math.prod(shape) // width):
+                if len(shape) == 1:
+                    buffer[k * width : (k + 1) * width] = taken[first + k].reshape(width)
+                else:
+                    buffer[k : k + 1, :] = taken[first + k]
+            leave(buffer, outs[count + part], part, count)
     for copy in copies:
         copy.wait()
 
 
-def spread_half(axes, stream, shards, splits, piece, outs=None):
-    half = piece.shape[0]
+def spread(axes, stream, shards, splits, rows, pieces, outs=(), sums=()):
+    held = rows // 2
     hbm = pl.BlockSpec(memory_space=pltpu.HBM)
-    other = outs is not None
+    shapes = [(rows, width) for width in splits] + [shape for _, shape in sums]
     return pl.pallas_call(
-        functools.partial(spread_kernel, axes, stream, shards, splits, other),
-        out_shape=[jax.ShapeDtypeStruct((2 * half, width), f32) for width in splits],
-        in_specs=[pl.BlockSpec(memory_space=pltpu.VMEM)] + ([hbm] * len(splits) if other else []),
-        out_specs=[hbm] * len(splits),
-        scratch_shapes=[pltpu.VMEM((half, width), f32) for width in splits]
-        + [pltpu.SemaphoreType.DMA((shards, len(splits)))],
-        input_output_aliases={1 + index: index for index in range(len(splits))} if other else {},
+        functools.partial(spread_kernel, axes, stream, shards, splits, bool(outs), sums),
+        out_shape=[jax.ShapeDtypeStruct(shape, f32) for shape in shapes],
+        in_specs=[pl.BlockSpec(memory_space=pltpu.VMEM)] * len(pieces) + [hbm] * len(outs),
+        out_specs=[hbm] * len(shapes),
+        scratch_shapes=[pltpu.VMEM((held, width), f32) for width in splits]
+        + [pltpu.VMEM(shape, f32) for _, shape in sums]
+        + [pltpu.SemaphoreType.DMA((max(shards, len(sums)), len(splits) + 1))],
+        input_output_aliases={len(pieces) + index: index for index in range(len(outs))},
         compiler_params=pltpu.CompilerParams(vmem_limit_bytes=8 * MIB),
-    )(piece, *(outs or ()))
-
-
-def on_device(kernel, operands, outs, scratch=(), sems=()):
+        cost_estimate=pl.CostEstimate(
+            flops=0, bytes_accessed=6 * held * sum(splits), transcendentals=0
+        ),
+    )(*pieces, *outs)
+
+
+def on_device(kernel, operands, outs, scratch=(), sems=(), flops=0):
     buffers = [pltpu.VMEM(value.shape, value.dtype) for value in operands]
-    buffers += [pltpu.VMEM(shape, dtype) for shape, dtype in outs]
+    buffers += [pltpu.VMEM(shape, jnp.dtype(dtype)) for shape, dtype in outs]
     hbm = pl.BlockSpec(memory_space=pltpu.HBM)
     return pl.pallas_call(
         kernel,
@@ -380,6 +400,11 @@
         + [pltpu.VMEM(shape, dtype) for shape, dtype in scratch]
         + [pltpu.SemaphoreType.DMA(shape) for shape in sems],
         compiler_params=pltpu.CompilerParams(vmem_limit_bytes=60 * MIB),
+        cost_estimate=pl.CostEstimate(
+            flops=flops,
+            bytes_accessed=sum(math.prod(buffer.shape) * buffer.dtype.itemsize for buffer in buffers),
+            transcendentals=0,
+        ),
     )(*operands)
 
 
@@ -435,9 +460,31 @@
     return total
 
 
-def sum_stream(axes, stream, keep, send, half_done, small=None, small_done=None):
+def after(value, token):
+    return lax.optimization_barrier((value, token))[0]
+
+
+class Sequence:
+    def __init__(self, axes, token):
+        self.axes = axes
+        self.token = token
+
+    def ready(self, value):
+        return after(value, self.token)
+
+    def swap(self, value, dims, scope="swap"):
+        self.token = value
+        with jax.named_scope(scope):
+            return self.axes.exchange(value, dims)
+
+
+def sum_stream(sequence, stream, keep, send, write, small=None):
+    axes = sequence.axes
     core = (axes.core, axes.core)
-    terms = [keep, (yield send, core)]
+    label = (f"s{stream + 1}h{hop}" for hop in range(99))
+    got = sequence.swap(send, core, next(label))
+    yield
+    terms = [keep, sequence.ready(got)]
     rows = keep.shape[0]
     extra = 0 if small is None else small.shape[0]
     pairs = list(zip(*axes.orders[stream]))
@@ -447,70 +494,32 @@
         value = add_rows(terms, rows, 2 * rows).astype(bf16)
         if extra:
             value = jnp.concatenate([value, small], axis=0)
-        got = yield value, dims
+        got = sequence.swap(value, dims, next(label))
+        yield
+        got = sequence.ready(got)
         if extra:
             small = (small.astype(f32) + got[rows:].astype(f32)).astype(bf16)
         terms.append(got)
     piece = add_rows(terms, 0, rows).astype(bf16)
     for dims in whole:
         value = jnp.concatenate([piece, small], axis=0) if extra else piece
-        got = yield value, dims
+        got = sequence.swap(value, dims, next(label))
+        yield
+        got = sequence.ready(got)
         if extra:
             small = (small.astype(f32) + got[rows:].astype(f32)).astype(bf16)
         piece = (piece.astype(f32) + got[:rows].astype(f32)).astype(bf16)
-    if extra:
-        got = yield small, core
-        small_done(small.astype(f32) + got.astype(f32))
     for dims in reversed(hops):
-        got = yield piece, dims
-        piece = jnp.concatenate([piece, got], axis=0)
-    half_done(piece)
-    return (yield piece, core)
-
-
-def after(value, token):
-    if token is None:
-        return value
-    return lax.optimization_barrier((value, token))[0]
-
-
-class Sequence:
-    def __init__(self, axes):
-        self.axes = axes
-        self.token = None
-        self.waiting = {}
-        self.streams = {}
-        self.done = {}
-        self.count = {}
-        self.then = None
-        self.held = None
-
-    def add(self, name, stream):
-        self.streams[name] = stream
-        self.waiting[name] = None
-
-    def step(self, name):
-        got = self.waiting[name]
-        try:
-            value, dims = self.streams[name].send(None if got is None else after(got, self.token))
-        except StopIteration as end:
-            self.done[name] = end.value
-            return
-        if self.held is not None:
-            value = after(value, self.held)
-            self.held = None
-        self.token = value
-        self.count[name] = self.count.get(name, -1) + 1
-        with jax.named_scope(f"s{name}h{self.count[name]}"):
-            self.waiting[name] = self.axes.exchange(value, dims)
-        if self.then is not None:
-            act, self.then = self.then, None
-            act()
-
-    def steps(self, names):
-        for name in names:
-            if name not in self.done:
-                self.step(name)
+        got = sequence.swap(piece, dims, next(label))
+        yield
+        parts = [piece, sequence.ready(got)]
+        if extra and dims is hops[0]:
+            parts.append(small)
+        piece = jnp.concatenate(parts, axis=0)
+    near = sequence.swap(piece, core, next(label))
+    write(piece)
+    yield
+    write(piece, sequence.ready(near))
 
 
 def body(
@@ -595,44 +604,45 @@
             ((rows, width), bf16),
         ],
         sems=[(16,), (13, items)],
+        flops=2 * rows * width * (4 * width + 6 * hidden),
     )
 
     from_beside = axes.beside(to_beside)
     from_across = axes.across(to_across)
+    sequence = Sequence(axes, (to_beside, to_across))
     grads = {}
     splits = {1: (width,), 2: (hidden, width), 3: (3 * width,)}
 
-    def half_done(name):
-        def act(piece):
-            def run():
-                held = after(piece, sequence.token)
-                grads[name] = spread_half(axes, name - 1, shards, splits[name], held)
-                sequence.token = grads[name][0]
-
-            sequence.then = run
-
-        return act
-
-    def small_done(total):
-        total = total.reshape(8 + hidden // width, width)
-        grads["small"] = (
-            total[0],
-            total[1],
-            total[2:4],
-            total[7],
-            total[4],
-            total[5],
-            total[8:].reshape(hidden),
-            total[6],
-        )
-        sequence.held = grads["small"]
-
-    sequence = Sequence(axes)
-    sequence.token = (to_beside, to_across)
-    sequence.add(1, sum_stream(axes, 0, keep1, send1, half_done(1)))
-    sequence.add(2, sum_stream(axes, 1, keep2, send2, half_done(2)))
-    sequence.steps((2, 1))
-    sequence.token = (from_beside, from_across)
+    def stream(name, keep, send, small=None):
+        rows = 2 * keep.shape[0]
+        settings = (axes, name - 1, shards, splits[name], rows)
+
+        def write(own, other=None):
+            if other is None:
+                grads[name] = spread(*settings, (own,))
+            elif small is None:
+                grads[name] = spread(*settings, (other,), grads[name])
+            else:
+                grads[name] = spread(*settings, (other, own), grads[name], small_places)
+            sequence.token = grads[name][0]
+
+        return sum_stream(sequence, name - 1, keep, send, write, small)
+
+    small_places = (
+        (0, (width,)),
+        (1, (width,)),
+        (2, (2, width)),
+        (7, (width,)),
+        (4, (width,)),
+        (5, (width,)),
+        (8, (hidden,)),
+        (6, (width,)),
+    )
+    streams = {1: stream(1, keep1, send1), 2: stream(2, keep2, send2)}
+    next(streams[2])
+    next(streams[1])
+    sequence.token = from_beside
+
     def join():
         operands = (
             after(dq, sequence.token),
@@ -658,24 +668,18 @@
             ],
             scratch=[((rows, 3 * width), bf16)],
             sems=[(11,), (4,)],
+            flops=12 * rows * width * width,
         )
-        sequence.add(3, sum_stream(axes, 2, keep, send, half_done(3), sums, small_done))
+        streams[3] = stream(3, keep, send, sums)
         return grad
 
     for name in ORDER + (1, 2, 3) * 12:
-        if name in sequence.done:
-            continue
-        if name == 3 and 3 not in sequence.streams:
+        if name not in streams:
             tokens_grad = join()
-        sequence.step(name)
-        if name in sequence.done:
-            other = after(sequence.done[name], sequence.token)
-            grads[name] = spread_half(axes, name - 1, shards, splits[name], other, grads[name])
-            sequence.token = grads[name][0]
+        next(streams[name], None)
     (grad_fc2,) = grads[1]
     grad_fc1, grad_proj = grads[2]
-    (grad_qkv,) = grads[3]
-    sums = grads["small"]
+    grad_qkv, *sums = grads[3]
     return (
         mixed.reshape(tokens.shape),
         tokens_grad.reshape(tokens.shape),

time: 119 us -> 116 us (0.975)
  waiting for transfers between devices: 35.7 us -> 25.8 us
  starting transfers between devices: 49 us -> 55.9 us
    ppermute x30 -> x29, waiting for transfers between devices: 35.7 us -> 25.8 us  [exchange(): return lax.ppermute(value, ('lat', 'items'), pairs)]
    ppermute x30 -> x29, starting transfers between devices: 47.5 us -> 54.4 us  [exchange(): return lax.ppermute(value, ('lat', 'items'), pairs)]
    slice x2 -> x0, local copies, waits for them, and re-layouts: 1.2 us -> none  [the longest x1 0.6 us: small_done(): total[6]]
  transfers between devices with their start and end apart: 32 -> 31, of which waited for: 11 -> 14; matrix products, arithmetic and copies ran while one was open for 4% -> 3% of each run, Pallas kernels for 9% -> 10%
where the time goes in v3:
time: 116 us; the launch traced here: 115 us
  starting transfers between devices  55.9 us (48%)
  Pallas kernels  27.3 us (24%)
  waiting for transfers between devices  25.8 us (22%)
  other arithmetic  3.83 us (3%)
  local copies, waits for them, and re-layouts  1.41 us (1%)
  between operations  1.17 us (1%)
    ppermute x29, starting transfers between devices, exchange(): return lax.ppermute(value, ('lat', 'items'), pairs)  54.4 us
    ppermute x29, waiting for transfers between devices, exchange(): return lax.ppermute(value, ('lat', 'items'), pairs)  25.8 us
    pallas_call x2, Pallas kernels, on_device(): pl.pallas_call(kernel, out_shape=[jax.ShapeDtypeStruct(shape, dtype) for...  18.2 us
    pallas_call x6, Pallas kernels, spread(): pl.pallas_call(functools.partial(spread_kernel, axes, stream, shards, spl...  9.01 us
  transfers between devices with their start and end apart: 31, of which 14 were waited for; matrix products, arithmetic and copies ran while one was open for 3% of the time, Pallas kernels for 10%

profile of v3, /device:TPU:0, one launch (start us, length us, event | category | flops | bytes accessed | tf_op | source)
XLA Modules:
  0.0 115.4 jit_solution(11067556362155139242)
XLA Ops:
  0.7 1.0 broadcast_select_fusion
  2.1 0.7 collective-permute-start.1
  3.1 0.6 copy-done.6
  3.8 14.5 %shard_map.245 = (bf16[192,512]{1,0:T(8,128)(2,1)}, bf16[192,512]{1,0:T(8,128)(2,1)}, f32[192,512]{1,0:T(8,128)}, f32[8,512]{1,0:T(8,128)}, bf16[1024,512]{1,0:T...) custom-call(bf16[192,512]{1,0:T(8,128)(2,1)} %bitcast.6, ...), custom_call_target="tpu_custom_call" | custom-call | flops 2818572288 | bytes 13791232 | tf_op jit(solution)/shard_map/pallas_call | solution.py:394
  18.3 5.9 %collective-permute-start.2 = (bf16[256,2560]{1,0:T(8,128)(2,1)}, bf16[256,2560]{1,0:T(8,128)(2,1)S(1)}, u32[]{:S(2)}, u32[]{:S(2)}) collective-permute-start(bf16[256,2560]{1,0:T(8,128)(2,1)} %get-tuple-element.75), channel_id=1, source_target_pairs={{0,8},{1,9},{2,10},{3,11},{4,12},{5,13},{6,14},{7,15},{8,0},{9,1},... | collective-permute-start | bytes 3932168 | tf_op jit(solution)/shard_map/s2h0/ppermute | solution.py:453
  24.2 0.8 collective-permute-start.4
  25.1 3.5 %collective-permute-start.6 = (bf16[1024,512]{1,0:T(8,128)(2,1)}, bf16[1024,512]{1,0:T(8,128)(2,1)S(1)}, u32[]{:S(2)}, u32[]{:S(2)}) collective-permute-start(bf16[1024,512]{1,0:T(8,128)(2,1)} %get-tuple-element.89), channel_id=1, source_target_pairs={{0,8},{1,9},{2,10},{3,11},{4,12},{5,13},{6,14},{7,15},{8,0},{9,1},... | collective-permute-start | bytes 3145736 | tf_op jit(solution)/shard_map/s1h0/ppermute | solution.py:453
  28.6 1.3 %add_convert_fusion = bf16[128,2560]{1,0:T(8,128)(2,1)S(1)} fusion(bf16[256,2560]{1,0:T(8,128)(2,1)S(1)} %collective-permute-done.2, bf16[256,2560]{1,0:T(8,128)(2,1)} %get-tuple-element.74), kind=kLoop, calls=%fused_computation.1 | loop fusion | flops 1310720 | bytes 1966080 | tf_op jit(solution)/shard_map/convert_element_type | solution.py:494
  29.9 0.7 copy-done.4
  30.6 3.8 %shard_map.246 = (bf16[256,1536]{1,0:T(8,128)(2,1)}, bf16[256,1536]{1,0:T(8,128)(2,1)}, bf16[192,512]{1,0:T(8,128)(2,1)}, bf16[4,1536]{1,0:T(4,128)(2,1)}) custom-call(bf16[192,512]{1,0:T(8,128)(2,1)} %get-tuple-element.78.refs_0_, f32[192,512]{1,0:T(8,128)} %get-tuple-element.79.refs_1_, f32[192,512]{1,0:T(8,128)} %get-tuple-element.80.refs_2_, ...), custom_call_target="tpu_custom_call" | custom-call | flops 603979776 | bytes 5534720 | tf_op jit(solution)/shard_map/pallas_call | solution.py:394
  34.3 2.0 %collective-permute-start.5 = (bf16[256,1536]{1,0:T(8,128)(2,1)}, bf16[256,1536]{1,0:T(8,128)(2,1)S(1)}, u32[]{:S(2)}, u32[]{:S(2)}) collective-permute-start(bf16[256,1536]{1,0:T(8,128)(2,1)} %get-tuple-element.87), channel_id=1, source_target_pairs={{0,8},{1,9},{2,10},{3,11},{4,12},{5,13},{6,14},{7,15},{8,0},{9,1},... | collective-permute-start | bytes 2359304 | tf_op jit(solution)/shard_map/s3h0/ppermute | solution.py:453
  36.4 2.1 %collective-permute-start.9 = (bf16[128,2560]{1,0:T(8,128)(2,1)S(1)}, bf16[128,2560]{1,0:T(8,128)(2,1)S(1)}, u32[]{:S(2)}, u32[]{:S(2)}) collective-permute-start(bf16[128,2560]{1,0:T(8,128)(2,1)S(1)} %add_convert_fusion), channel_id=1, source_target_pairs={{0,1},{1,0},{2,3},{3,2},{4,5},{5,4},{6,7},{7,6},{8,10},{9,11},{10,... | collective-permute-start | bytes 1966088 | tf_op jit(solution)/shard_map/s2h1/ppermute | solution.py:453
  38.7 1.6 %collective-permute-start.8 = (bf16[512,512]{1,0:T(8,128)(2,1)S(1)}, bf16[512,512]{1,0:T(8,128)(2,1)S(1)}, u32[]{:S(2)}, u32[]{:S(2)}) collective-permute-start(bf16[512,512]{1,0:T(8,128)(2,1)S(1)} %add_convert_fusion.1), channel_id=1, source_target_pairs={{0,2},{1,3},{2,0},{3,1},{4,6},{5,7},{6,4},{7,5},{8,24},{9,25},{10,... | collective-permute-start | bytes 1572872 | tf_op jit(solution)/shard_map/s1h1/ppermute | solution.py:453
  40.4 0.6 collective-permute-start.7
  41.0 6.0 %collective-permute-done.9 = bf16[128,2560]{1,0:T(8,128)(2,1)S(1)} collective-permute-done((bf16[128,2560]{1,0:T(8,128)(2,1)S(1)}, bf16[128,2560]{1,0:T(8,128)(2,1)S(1)}, u32[]{:S(2)}, u32[]{:S(2)}) %collective-permute-start.9) | collective-permute-done | bytes 655392 | tf_op jit(solution)/shard_map/s2h1/ppermute | solution.py:453
  47.2 2.2 %collective-permute-start.12 = (bf16[64,2560]{1,0:T(8,128)(2,1)S(1)}, bf16[64,2560]{1,0:T(8,128)(2,1)S(1)}, u32[]{:S(2)}, u32[]{:S(2)}) collective-permute-start(bf16[64,2560]{1,0:T(8,128)(2,1)S(1)} %add_convert_fusion.3), channel_id=1, source_target_pairs={{0,2},{1,3},{2,0},{3,1},{4,6},{5,7},{6,4},{7,5},{8,9},{9,8},{10,11... | collective-permute-start | bytes 983048 | tf_op jit(solution)/shard_map/s2h2/ppermute | solution.py:453
  49.4 2.8 %collective-permute-done.8 = bf16[512,512]{1,0:T(8,128)(2,1)S(1)} collective-permute-done((bf16[512,512]{1,0:T(8,128)(2,1)S(1)}, bf16[512,512]{1,0:T(8,128)(2,1)S(1)}, u32[]{:S(2)}, u32[]{:S(2)}) %collective-permute-start.8) | collective-permute-done | bytes 524320 | tf_op jit(solution)/shard_map/s1h1/ppermute | solution.py:453
  52.2 1.7 %collective-permute-start.11 = (bf16[256,512]{1,0:T(8,128)(2,1)S(1)}, bf16[256,512]{1,0:T(8,128)(2,1)S(1)}, u32[]{:S(2)}, u32[]{:S(2)}) collective-permute-start(bf16[256,512]{1,0:T(8,128)(2,1)S(1)} %add_convert_fusion.4), channel_id=1, source_target_pairs={{0,16},{1,17},{2,18},{3,19},{4,20},{5,21},{6,22},{7,23},{8,9},{9,8... | collective-permute-start | bytes 786440 | tf_op jit(solution)/shard_map/s1h2/ppermute | solution.py:453
  54.5 1.1 collective-permute-done.12
  55.7 1.7 %collective-permute-start.15 = (bf16[32,2560]{1,0:T(8,128)(2,1)S(1)}, bf16[32,2560]{1,0:T(8,128)(2,1)S(1)}, u32[]{:S(2)}, u32[]{:S(2)}) collective-permute-start(bf16[32,2560]{1,0:T(8,128)(2,1)S(1)} %add_convert_fusion.8), channel_id=1, source_target_pairs={{0,16},{1,17},{2,18},{3,19},{4,20},{5,21},{6,22},{7,23},{8,12},{9,... | collective-permute-start | bytes 491528 | tf_op jit(solution)/shard_map/s2h3/ppermute | solution.py:453
  57.4 1.3 %collective-permute-done.11 = bf16[256,512]{1,0:T(8,128)(2,1)S(1)} collective-permute-done((bf16[256,512]{1,0:T(8,128)(2,1)S(1)}, bf16[256,512]{1,0:T(8,128)(2,1)S(1)}, u32[]{:S(2)}, u32[]{:S(2)}) %collective-permute-start.11) | collective-permute-done | bytes 262176 | tf_op jit(solution)/shard_map/s1h2/ppermute | solution.py:453
  58.8 1.5 %collective-permute-start.14 = (bf16[128,512]{1,0:T(8,128)(2,1)S(1)}, bf16[128,512]{1,0:T(8,128)(2,1)S(1)}, u32[]{:S(2)}, u32[]{:S(2)}) collective-permute-start(bf16[128,512]{1,0:T(8,128)(2,1)S(1)} %add_convert_fusion.11), channel_id=1, source_target_pairs={{0,1},{1,0},{2,3},{3,2},{4,5},{5,4},{6,7},{7,6},{8,10},{9,11},{10,... | collective-permute-start | bytes 393224 | tf_op jit(solution)/shard_map/s1h3/ppermute | solution.py:453
  60.3 0.8 collective-permute-done.10
  61.2 2.8 %collective-permute-start.13 = (bf16[36,1536]{1,0:T(8,128)(2,1)S(1)}, bf16[36,1536]{1,0:T(8,128)(2,1)S(1)}, u32[]{:S(2)}, u32[]{:S(2)}) collective-permute-start(bf16[36,1536]{1,0:T(8,128)(2,1)S(1)} %pad_maximum_fusion.10), channel_id=1, source_target_pairs={{0,4},{1,5},{2,6},{3,7},{4,0},{5,1},{6,2},{7,3},{8,12},{9,13},{10,... | collective-permute-start | bytes 331784 | tf_op jit(solution)/shard_map/s3h3/ppermute | solution.py:453
  64.1 1.7 %collective-permute-start.17 = (bf16[32,2560]{1,0:T(8,128)(2,1)S(1)}, bf16[32,2560]{1,0:T(8,128)(2,1)S(1)}, u32[]{:S(2)}, u32[]{:S(2)}) collective-permute-start(bf16[32,2560]{1,0:T(8,128)(2,1)S(1)} %add_convert_fusion.7), channel_id=1, source_target_pairs={{0,4},{1,5},{2,6},{3,7},{4,0},{5,1},{6,2},{7,3},{8,24},{9,25},{10,... | collective-permute-start | bytes 491528 | tf_op jit(solution)/shard_map/s2h4/ppermute | solution.py:453
  65.8 1.7 %collective-permute-start.19 = (bf16[128,512]{1,0:T(8,128)(2,1)S(1)}, bf16[128,512]{1,0:T(8,128)(2,1)S(1)}, u32[]{:S(2)}, u32[]{:S(2)}) collective-permute-start(bf16[128,512]{1,0:T(8,128)(2,1)S(1)} %add_convert_fusion.10), channel_id=1, source_target_pairs={{0,4},{1,5},{2,6},{3,7},{4,0},{5,1},{6,2},{7,3},{8,12},{9,13},{10,... | collective-permute-start | bytes 393224 | tf_op jit(solution)/shard_map/s1h4/ppermute | solution.py:453
  67.5 1.1 collective-permute-done.13
  68.7 7.2 %collective-permute-start.16 = (bf16[36,1536]{1,0:T(8,128)(2,1)S(1)}, bf16[36,1536]{1,0:T(8,128)(2,1)S(1)}, u32[]{:S(2)}, u32[]{:S(2)}) collective-permute-start(bf16[36,1536]{1,0:T(8,128)(2,1)S(1)} %pad_maximum_fusion.11), channel_id=1, source_target_pairs={{0,2},{1,3},{2,0},{3,1},{4,6},{5,7},{6,4},{7,5},{8,10},{9,11},{10,... | collective-permute-start | bytes 331784 | tf_op jit(solution)/shard_map/s3h4/ppermute | solution.py:453
  76.0 1.7 %collective-permute-done.17 = bf16[32,2560]{1,0:T(8,128)(2,1)S(1)} collective-permute-done((bf16[32,2560]{1,0:T(8,128)(2,1)S(1)}, bf16[32,2560]{1,0:T(8,128)(2,1)S(1)}, u32[]{:S(2)}, u32[]{:S(2)}) %collective-permute-start.17) | collective-permute-done | bytes 163872 | tf_op jit(solution)/shard_map/s2h4/ppermute | solution.py:453
  77.7 2.3 %collective-permute-start.18 = (bf16[32,2560]{1,0:T(8,128)(2,1)S(1)}, bf16[32,2560]{1,0:T(8,128)(2,1)S(1)}, u32[]{:S(2)}, u32[]{:S(2)}) collective-permute-start(bf16[32,2560]{1,0:T(8,128)(2,1)S(1)} %add_convert_fusion.6), channel_id=1, source_target_pairs={{0,16},{1,17},{2,18},{3,19},{4,20},{5,21},{6,22},{7,23},{8,12},{9,... | collective-permute-start | bytes 491528 | tf_op jit(solution)/shard_map/s2h5/ppermute | solution.py:453
  80.9 2.4 %collective-permute-done.18 = bf16[32,2560]{1,0:T(8,128)(2,1)S(1)} collective-permute-done((bf16[32,2560]{1,0:T(8,128)(2,1)S(1)}, bf16[32,2560]{1,0:T(8,128)(2,1)S(1)}, u32[]{:S(2)}, u32[]{:S(2)}) %collective-permute-start.18) | collective-permute-done | bytes 163872 | tf_op jit(solution)/shard_map/s2h5/ppermute | solution.py:453
  83.3 1.5 %collective-permute-start.21 = (bf16[64,2560]{1,0:T(8,128)(2,1)S(1)}, bf16[64,2560]{1,0:T(8,128)(2,1)S(1)}, u32[]{:S(2)}, u32[]{:S(2)}) collective-permute-start(bf16[64,2560]{1,0:T(8,128)(2,1)S(1)} %pad_maximum_fusion.6), channel_id=1, source_target_pairs={{0,2},{1,3},{2,0},{3,1},{4,6},{5,7},{6,4},{7,5},{8,9},{9,8},{10,11... | collective-permute-start | bytes 983048 | tf_op jit(solution)/shard_map/s2h6/ppermute | solution.py:453
  84.9 3.4 %collective-permute-start.20 = (bf16[32,1536]{1,0:T(8,128)(2,1)S(1)}, bf16[32,1536]{1,0:T(8,128)(2,1)S(1)}, u32[]{:S(2)}, u32[]{:S(2)}) collective-permute-start(bf16[32,1536]{1,0:T(8,128)(2,1)S(1)} %get-tuple-element.131), channel_id=1, source_target_pairs={{0,4},{1,5},{2,6},{3,7},{4,0},{5,1},{6,2},{7,3},{8,12},{9,13},{10,... | collective-permute-start | bytes 294920 | tf_op jit(solution)/shard_map/s3h5/ppermute | solution.py:453
  88.4 1.5 %collective-permute-start.24 = (bf16[256,512]{1,0:T(8,128)(2,1)S(1)}, bf16[256,512]{1,0:T(8,128)(2,1)S(1)}, u32[]{:S(2)}, u32[]{:S(2)}) collective-permute-start(bf16[256,512]{1,0:T(8,128)(2,1)S(1)} %pad_maximum_fusion.7), channel_id=1, source_target_pairs={{0,16},{1,17},{2,18},{3,19},{4,20},{5,21},{6,22},{7,23},{8,9},{9,8... | collective-permute-start | bytes 786440 | tf_op jit(solution)/shard_map/s1h6/ppermute | solution.py:453
  89.9 1.8 %collective-permute-done.21 = bf16[64,2560]{1,0:T(8,128)(2,1)S(1)} collective-permute-done((bf16[64,2560]{1,0:T(8,128)(2,1)S(1)}, bf16[64,2560]{1,0:T(8,128)(2,1)S(1)}, u32[]{:S(2)}, u32[]{:S(2)}) %collective-permute-start.21) | collective-permute-done | bytes 327712 | tf_op jit(solution)/shard_map/s2h6/ppermute | solution.py:453
  91.8 0.6 collective-permute-start.27
  92.4 2.4 %collective-permute-start.23 = (bf16[64,1536]{1,0:T(8,128)(2,1)S(1)}, bf16[64,1536]{1,0:T(8,128)(2,1)S(1)}, u32[]{:S(2)}, u32[]{:S(2)}) collective-permute-start(bf16[64,1536]{1,0:T(8,128)(2,1)S(1)} %pad_maximum_fusion.9), channel_id=1, source_target_pairs={{0,16},{1,17},{2,18},{3,19},{4,20},{5,21},{6,22},{7,23},{8,9},{9,8... | collective-permute-start | bytes 589832 | tf_op jit(solution)/shard_map/s3h6/ppermute | solution.py:453
  94.9 2.2 %collective-permute-start.26 = (bf16[512,512]{1,0:T(8,128)(2,1)S(1)}, bf16[512,512]{1,0:T(8,128)(2,1)S(1)}, u32[]{:S(2)}, u32[]{:S(2)}) collective-permute-start(bf16[512,512]{1,0:T(8,128)(2,1)S(1)} %pad_maximum_fusion.3), channel_id=1, source_target_pairs={{0,2},{1,3},{2,0},{3,1},{4,6},{5,7},{6,4},{7,5},{8,24},{9,25},{10,... | collective-permute-start | bytes 1572872 | tf_op jit(solution)/shard_map/s1h7/ppermute | solution.py:453
  97.1 3.0 %collective-permute-done.23 = bf16[64,1536]{1,0:T(8,128)(2,1)S(1)} collective-permute-done((bf16[64,1536]{1,0:T(8,128)(2,1)S(1)}, bf16[64,1536]{1,0:T(8,128)(2,1)S(1)}, u32[]{:S(2)}, u32[]{:S(2)}) %collective-permute-start.23) | collective-permute-done | bytes 196640 | tf_op jit(solution)/shard_map/s3h6/ppermute | solution.py:453
  100.1 2.0 %collective-permute-start.25 = (bf16[128,1536]{1,0:T(8,128)(2,1)S(1)}, bf16[128,1536]{1,0:T(8,128)(2,1)S(1)}, u32[]{:S(2)}, u32[]{:S(2)}) collective-permute-start(bf16[128,1536]{1,0:T(8,128)(2,1)S(1)} %pad_maximum_fusion.5), channel_id=1, source_target_pairs={{0,1},{1,0},{2,3},{3,2},{4,5},{5,4},{6,7},{7,6},{8,24},{9,25},{10,... | collective-permute-start | bytes 1179656 | tf_op jit(solution)/shard_map/s3h7/ppermute | solution.py:453
  102.2 2.3 %collective-permute-done.27 = bf16[128,2560]{1,0:T(8,128)(2,1)S(1)} collective-permute-done((bf16[128,2560]{1,0:T(8,128)(2,1)S(1)}, bf16[128,2560]{1,0:T(8,128)(2,1)S(1)}, u32[]{:S(2)}, u32[]{:S(2)}) %collective-permute-start.27) | collective-permute-done | bytes 655392 | tf_op jit(solution)/shard_map/s2h7/ppermute | solution.py:453
  104.6 1.7 %shard_map.247 = (f32[512,2048]{1,0:T(8,128)}, f32[512,512]{1,0:T(8,128)}) custom-call(bf16[256,2560]{1,0:T(8,128)(2,1)S(1)} %pad_maximum_fusion.refs_0_), custom_call_target="tpu_custom_call" | custom-call | bytes 3932160 | tf_op jit(solution)/shard_map/pallas_call | solution.py:374
  106.4 0.7 collective-permute-done.26
  107.2 1.5 %shard_map.248.refs_1_ = f32[2048,512]{1,0:T(8,128)} custom-call(bf16[1024,512]{1,0:T(8,128)(2,1)S(1)} %pad_maximum_fusion.1.refs_0_), custom_call_target="tpu_custom_call" | custom-call | bytes 3145728 | tf_op jit(solution)/shard_map/pallas_call | solution.py:374
  109.4 1.3 %shard_map.249.refs_2_ = f32[512,1536]{1,0:T(8,128)} custom-call(bf16[260,1536]{1,0:T(8,128)(2,1)S(1)} %fusion.refs_0_.refs_1_), custom_call_target="tpu_custom_call" | custom-call | bytes 2359296 | tf_op jit(solution)/shard_map/pallas_call | solution.py:374
  110.7 1.7 %shard_map.250 = (f32[512,2048]{1,0:T(8,128)}, f32[512,512]{1,0:T(8,128)}) custom-call(bf16[256,2560]{1,0:T(8,128)(2,1)S(1)} %collective-permute-done.30.refs_0_, f32[512,2048]{1,0:T(8,128)} %get-tuple-element.112.refs_1_, f32[512,512]{1,0:T(8,128)} %get-tuple-element.116.refs_2_), custom_call_target="tpu_custom_call", output_to_operand_aliasing={{0}: (1, {}), {1}: (2, {})} | custom-call | bytes 3932160 | tf_op jit(solution)/shard_map/pallas_call | solution.py:374
  112.4 1.5 %shard_map.251 = f32[2048,512]{1,0:T(8,128)} custom-call(bf16[1024,512]{1,0:T(8,128)(2,1)S(1)} %collective-permute-done.29.refs_0_, f32[2048,512]{1,0:T(8,128)} %shard_map.248.refs_1_), custom_call_target="tpu_custom_call", output_to_operand_aliasing={{}: (1, {})} | custom-call | bytes 3145728 | tf_op jit(solution)/shard_map/pallas_call | solution.py:374
  113.9 1.3 %shard_map.252 = (f32[512,1536]{1,0:T(8,128)}, f32[512]{0:T(512)}, f32[512]{0:T(512)}, f32[2,512]{1,0:T(2,128)}, f32[512]{0:T(512)}, /*index=5*/f32[512]{0:T(512)}, f32[512]{0:T(512)}, f32[2048]{0:T(1024)}, f32[512]{0:T(512)}) custom-call(bf16[260,1536]{1,0:T(8,128)(2,1)S(1)} %collective-permute-done.28.refs_0_, ...), custom_call_target="tpu_custom_call", output_to_operand_aliasing={{0}: (2, {})} | custom-call | bytes 2359296 | tf_op jit(solution)/shard_map/pallas_call | solution.py:374
  (73 shorter events, 4.7 us)
Async XLA Ops:
  1.6 1.5 %collective-permute-start = (bf16[96,512]{1,0:T(8,128)(2,1)S(1)}, bf16[96,512]{1,0:T(8,128)(2,1)S(1)}, u32[]{:S(2)}, u32[]{:S(2)}) collective-permute-start(bf16[96,512]{1,0:T(8,128)(2,1)S(1)} %bitcast.9), channel_id=1, source_target_pairs={{0,8},{1,9},{2,10},{3,11},{4,12},{5,13},{6,14},{7,15},{8,0},{9,1},... | collective-permute-start | bytes 294920 | tf_op jit(solution)/shard_map/ppermute | solution.py:453
  2.1 0.9 collective-permute-start.1
  3.1 0.7 copy-start.6
  3.1 0.7 copy-start.7
  18.3 10.3 %collective-permute-start.2 = (bf16[256,2560]{1,0:T(8,128)(2,1)}, bf16[256,2560]{1,0:T(8,128)(2,1)S(1)}, u32[]{:S(2)}, u32[]{:S(2)}) collective-permute-start(bf16[256,2560]{1,0:T(8,128)(2,1)} %get-tuple-element.75), channel_id=1, source_target_pairs={{0,8},{1,9},{2,10},{3,11},{4,12},{5,13},{6,14},{7,15},{8,0},{9,1},... | collective-permute-start | bytes 3932168 | tf_op jit(solution)/shard_map/s2h0/ppermute | solution.py:453
  24.1 4.4 %collective-permute-start.3 = (bf16[2,96,512]{2,1,0:T(8,128)(2,1)}, bf16[2,96,512]{2,1,0:T(8,128)(2,1)S(1)}, u32[]{:S(2)}, u32[]{:S(2)}) collective-permute-start(bf16[2,96,512]{2,1,0:T(8,128)(2,1)} %get-tuple-element.76), channel_id=1, source_target_pairs={{0,8},{1,9},{2,10},{3,11},{4,12},{5,13},{6,14},{7,15},{8,0},{9,1},... | collective-permute-start | bytes 589832 | tf_op jit(solution)/shard_map/ppermute | solution.py:453
  24.2 5.6 %collective-permute-start.4 = (bf16[2,96,512]{2,1,0:T(8,128)(2,1)}, bf16[2,96,512]{2,1,0:T(8,128)(2,1)S(1)}, u32[]{:S(2)}, u32[]{:S(2)}) collective-permute-start(bf16[2,96,512]{2,1,0:T(8,128)(2,1)} %get-tuple-element.81), channel_id=1, source_target_pairs={{8,16},{16,8},{9,17},{17,9},{10,18},{18,10},{11,19},{19,11},{12,20... | collective-permute-start | bytes 589832 | tf_op jit(solution)/shard_map/ppermute | solution.py:445
  25.1 13.4 %collective-permute-start.6 = (bf16[1024,512]{1,0:T(8,128)(2,1)}, bf16[1024,512]{1,0:T(8,128)(2,1)S(1)}, u32[]{:S(2)}, u32[]{:S(2)}) collective-permute-start(bf16[1024,512]{1,0:T(8,128)(2,1)} %get-tuple-element.89), channel_id=1, source_target_pairs={{0,8},{1,9},{2,10},{3,11},{4,12},{5,13},{6,14},{7,15},{8,0},{9,1},... | collective-permute-start | bytes 3145736 | tf_op jit(solution)/shard_map/s1h0/ppermute | solution.py:453
  28.5 1.3 %copy-start.3 = (bf16[2,96,512]{2,1,0:T(8,128)(2,1)}, bf16[2,96,512]{2,1,0:T(8,128)(2,1)S(1)}, u32[]{:S(2)}) copy-start(bf16[2,96,512]{2,1,0:T(8,128)(2,1)S(1)} %collective-permute-done.3.refs_3_) | copy-start | bytes 589828
  29.9 0.7 copy-start.4
  30.6 8.0 %copy-start.1 = (bf16[1024,512]{1,0:T(8,128)(2,1)S(1)}, bf16[1024,512]{1,0:T(8,128)(2,1)}, u32[]{:S(2)}) copy-start(bf16[1024,512]{1,0:T(8,128)(2,1)} %get-tuple-element.88) | copy-start | bytes 3145732
  34.3 6.0 %copy-start.2 = (bf16[256,1536]{1,0:T(8,128)(2,1)S(1)}, bf16[256,1536]{1,0:T(8,128)(2,1)}, u32[]{:S(2)}) copy-start(bf16[256,1536]{1,0:T(8,128)(2,1)} %get-tuple-element.86) | copy-start | bytes 2359300
  34.3 6.0 %collective-permute-start.5 = (bf16[256,1536]{1,0:T(8,128)(2,1)}, bf16[256,1536]{1,0:T(8,128)(2,1)S(1)}, u32[]{:S(2)}, u32[]{:S(2)}) collective-permute-start(bf16[256,1536]{1,0:T(8,128)(2,1)} %get-tuple-element.87), channel_id=1, source_target_pairs={{0,8},{1,9},{2,10},{3,11},{4,12},{5,13},{6,14},{7,15},{8,0},{9,1},... | collective-permute-start | bytes 2359304 | tf_op jit(solution)/shard_map/s3h0/ppermute | solution.py:453
  36.4 10.7 %collective-permute-start.9 = (bf16[128,2560]{1,0:T(8,128)(2,1)S(1)}, bf16[128,2560]{1,0:T(8,128)(2,1)S(1)}, u32[]{:S(2)}, u32[]{:S(2)}) collective-permute-start(bf16[128,2560]{1,0:T(8,128)(2,1)S(1)} %add_convert_fusion), channel_id=1, source_target_pairs={{0,1},{1,0},{2,3},{3,2},{4,5},{5,4},{6,7},{7,6},{8,10},{9,11},{10,... | collective-permute-start | bytes 1966088 | tf_op jit(solution)/shard_map/s2h1/ppermute | solution.py:453
  38.5 1.9 %copy-start.5 = (bf16[4,1536]{1,0:T(4,128)(2,1)S(1)}, bf16[4,1536]{1,0:T(4,128)(2,1)}, u32[]{:S(2)}) copy-start(bf16[4,1536]{1,0:T(4,128)(2,1)} %get-tuple-element.92) | copy-start | bytes 36868
  38.7 8.4 %copy-start = (bf16[256,2560]{1,0:T(8,128)(2,1)S(1)}, bf16[256,2560]{1,0:T(8,128)(2,1)}, u32[]{:S(2)}) copy-start(bf16[256,2560]{1,0:T(8,128)(2,1)} %get-tuple-element.74) | copy-start | bytes 3932164
  38.7 13.5 %collective-permute-start.8 = (bf16[512,512]{1,0:T(8,128)(2,1)S(1)}, bf16[512,512]{1,0:T(8,128)(2,1)S(1)}, u32[]{:S(2)}, u32[]{:S(2)}) collective-permute-start(bf16[512,512]{1,0:T(8,128)(2,1)S(1)} %add_convert_fusion.1), channel_id=1, source_target_pairs={{0,2},{1,3},{2,0},{3,1},{4,6},{5,7},{6,4},{7,5},{8,24},{9,25},{10,... | collective-permute-start | bytes 1572872 | tf_op jit(solution)/shard_map/s1h1/ppermute | solution.py:453
  40.4 13.5 %collective-permute-start.7 = (bf16[132,1536]{1,0:T(8,128)(2,1)S(1)}, bf16[132,1536]{1,0:T(8,128)(2,1)S(1)}, u32[]{:S(2)}, u32[]{:S(2)}) collective-permute-start(bf16[132,1536]{1,0:T(8,128)(2,1)S(1)} %pad_maximum_fusion.4), channel_id=1, source_target_pairs={{0,1},{1,0},{2,3},{3,2},{4,5},{5,4},{6,7},{7,6},{8,24},{9,25},{10,... | collective-permute-start | bytes 1216520 | tf_op jit(solution)/shard_map/s3h1/ppermute | solution.py:453
  47.2 8.5 %collective-permute-start.12 = (bf16[64,2560]{1,0:T(8,128)(2,1)S(1)}, bf16[64,2560]{1,0:T(8,128)(2,1)S(1)}, u32[]{:S(2)}, u32[]{:S(2)}) collective-permute-start(bf16[64,2560]{1,0:T(8,128)(2,1)S(1)} %add_convert_fusion.3), channel_id=1, source_target_pairs={{0,2},{1,3},{2,0},{3,1},{4,6},{5,7},{6,4},{7,5},{8,9},{9,8},{10,11... | collective-permute-start | bytes 983048 | tf_op jit(solution)/shard_map/s2h2/ppermute | solution.py:453
  52.2 6.4 %collective-permute-start.11 = (bf16[256,512]{1,0:T(8,128)(2,1)S(1)}, bf16[256,512]{1,0:T(8,128)(2,1)S(1)}, u32[]{:S(2)}, u32[]{:S(2)}) collective-permute-start(bf16[256,512]{1,0:T(8,128)(2,1)S(1)} %add_convert_fusion.4), channel_id=1, source_target_pairs={{0,16},{1,17},{2,18},{3,19},{4,20},{5,21},{6,22},{7,23},{8,9},{9,8... | collective-permute-start | bytes 786440 | tf_op jit(solution)/shard_map/s1h2/ppermute | solution.py:453
  54.0 7.0 %collective-permute-start.10 = (bf16[68,1536]{1,0:T(8,128)(2,1)S(1)}, bf16[68,1536]{1,0:T(8,128)(2,1)S(1)}, u32[]{:S(2)}, u32[]{:S(2)}) collective-permute-start(bf16[68,1536]{1,0:T(8,128)(2,1)S(1)} %pad_maximum_fusion.8), channel_id=1, source_target_pairs={{0,16},{1,17},{2,18},{3,19},{4,20},{5,21},{6,22},{7,23},{8,9},{9,8... | collective-permute-start | bytes 626696 | tf_op jit(solution)/shard_map/s3h2/ppermute | solution.py:453
  55.7 8.2 %collective-permute-start.15 = (bf16[32,2560]{1,0:T(8,128)(2,1)S(1)}, bf16[32,2560]{1,0:T(8,128)(2,1)S(1)}, u32[]{:S(2)}, u32[]{:S(2)}) collective-permute-start(bf16[32,2560]{1,0:T(8,128)(2,1)S(1)} %add_convert_fusion.8), channel_id=1, source_target_pairs={{0,16},{1,17},{2,18},{3,19},{4,20},{5,21},{6,22},{7,23},{8,12},{9,... | collective-permute-start | bytes 491528 | tf_op jit(solution)/shard_map/s2h3/ppermute | solution.py:453
  58.8 7.0 %collective-permute-start.14 = (bf16[128,512]{1,0:T(8,128)(2,1)S(1)}, bf16[128,512]{1,0:T(8,128)(2,1)S(1)}, u32[]{:S(2)}, u32[]{:S(2)}) collective-permute-start(bf16[128,512]{1,0:T(8,128)(2,1)S(1)} %add_convert_fusion.11), channel_id=1, source_target_pairs={{0,1},{1,0},{2,3},{3,2},{4,5},{5,4},{6,7},{7,6},{8,10},{9,11},{10,... | collective-permute-start | bytes 393224 | tf_op jit(solution)/shard_map/s1h3/ppermute | solution.py:453
  61.2 7.5 %collective-permute-start.13 = (bf16[36,1536]{1,0:T(8,128)(2,1)S(1)}, bf16[36,1536]{1,0:T(8,128)(2,1)S(1)}, u32[]{:S(2)}, u32[]{:S(2)}) collective-permute-start(bf16[36,1536]{1,0:T(8,128)(2,1)S(1)} %pad_maximum_fusion.10), channel_id=1, source_target_pairs={{0,4},{1,5},{2,6},{3,7},{4,0},{5,1},{6,2},{7,3},{8,12},{9,13},{10,... | collective-permute-start | bytes 331784 | tf_op jit(solution)/shard_map/s3h3/ppermute | solution.py:453
  64.1 13.6 %collective-permute-start.17 = (bf16[32,2560]{1,0:T(8,128)(2,1)S(1)}, bf16[32,2560]{1,0:T(8,128)(2,1)S(1)}, u32[]{:S(2)}, u32[]{:S(2)}) collective-permute-start(bf16[32,2560]{1,0:T(8,128)(2,1)S(1)} %add_convert_fusion.7), channel_id=1, source_target_pairs={{0,4},{1,5},{2,6},{3,7},{4,0},{5,1},{6,2},{7,3},{8,24},{9,25},{10,... | collective-permute-start | bytes 491528 | tf_op jit(solution)/shard_map/s2h4/ppermute | solution.py:453
  65.8 14.6 %collective-permute-start.19 = (bf16[128,512]{1,0:T(8,128)(2,1)S(1)}, bf16[128,512]{1,0:T(8,128)(2,1)S(1)}, u32[]{:S(2)}, u32[]{:S(2)}) collective-permute-start(bf16[128,512]{1,0:T(8,128)(2,1)S(1)} %add_convert_fusion.10), channel_id=1, source_target_pairs={{0,4},{1,5},{2,6},{3,7},{4,0},{5,1},{6,2},{7,3},{8,12},{9,13},{10,... | collective-permute-start | bytes 393224 | tf_op jit(solution)/shard_map/s1h4/ppermute | solution.py:453
  68.7 16.1 %collective-permute-start.16 = (bf16[36,1536]{1,0:T(8,128)(2,1)S(1)}, bf16[36,1536]{1,0:T(8,128)(2,1)S(1)}, u32[]{:S(2)}, u32[]{:S(2)}) collective-permute-start(bf16[36,1536]{1,0:T(8,128)(2,1)S(1)} %pad_maximum_fusion.11), channel_id=1, source_target_pairs={{0,2},{1,3},{2,0},{3,1},{4,6},{5,7},{6,4},{7,5},{8,10},{9,11},{10,... | collective-permute-start | bytes 331784 | tf_op jit(solution)/shard_map/s3h4/ppermute | solution.py:453
  77.7 5.6 %collective-permute-start.18 = (bf16[32,2560]{1,0:T(8,128)(2,1)S(1)}, bf16[32,2560]{1,0:T(8,128)(2,1)S(1)}, u32[]{:S(2)}, u32[]{:S(2)}) collective-permute-start(bf16[32,2560]{1,0:T(8,128)(2,1)S(1)} %add_convert_fusion.6), channel_id=1, source_target_pairs={{0,16},{1,17},{2,18},{3,19},{4,20},{5,21},{6,22},{7,23},{8,12},{9,... | collective-permute-start | bytes 491528 | tf_op jit(solution)/shard_map/s2h5/ppermute | solution.py:453
  80.5 7.8 %collective-permute-start.22 = (bf16[128,512]{1,0:T(8,128)(2,1)S(1)}, bf16[128,512]{1,0:T(8,128)(2,1)S(1)}, u32[]{:S(2)}, u32[]{:S(2)}) collective-permute-start(bf16[128,512]{1,0:T(8,128)(2,1)S(1)} %add_convert_fusion.9), channel_id=1, source_target_pairs={{0,1},{1,0},{2,3},{3,2},{4,5},{5,4},{6,7},{7,6},{8,10},{9,11},{10,... | collective-permute-start | bytes 393224 | tf_op jit(solution)/shard_map/s1h5/ppermute | solution.py:453
  83.3 8.4 %collective-permute-start.21 = (bf16[64,2560]{1,0:T(8,128)(2,1)S(1)}, bf16[64,2560]{1,0:T(8,128)(2,1)S(1)}, u32[]{:S(2)}, u32[]{:S(2)}) collective-permute-start(bf16[64,2560]{1,0:T(8,128)(2,1)S(1)} %pad_maximum_fusion.6), channel_id=1, source_target_pairs={{0,2},{1,3},{2,0},{3,1},{4,6},{5,7},{6,4},{7,5},{8,9},{9,8},{10,11... | collective-permute-start | bytes 983048 | tf_op jit(solution)/shard_map/s2h6/ppermute | solution.py:453
  84.9 7.5 %collective-permute-start.20 = (bf16[32,1536]{1,0:T(8,128)(2,1)S(1)}, bf16[32,1536]{1,0:T(8,128)(2,1)S(1)}, u32[]{:S(2)}, u32[]{:S(2)}) collective-permute-start(bf16[32,1536]{1,0:T(8,128)(2,1)S(1)} %get-tuple-element.131), channel_id=1, source_target_pairs={{0,4},{1,5},{2,6},{3,7},{4,0},{5,1},{6,2},{7,3},{8,12},{9,13},{10,... | collective-permute-start | bytes 294920 | tf_op jit(solution)/shard_map/s3h5/ppermute | solution.py:453
  88.4 6.5 %collective-permute-start.24 = (bf16[256,512]{1,0:T(8,128)(2,1)S(1)}, bf16[256,512]{1,0:T(8,128)(2,1)S(1)}, u32[]{:S(2)}, u32[]{:S(2)}) collective-permute-start(bf16[256,512]{1,0:T(8,128)(2,1)S(1)} %pad_maximum_fusion.7), channel_id=1, source_target_pairs={{0,16},{1,17},{2,18},{3,19},{4,20},{5,21},{6,22},{7,23},{8,9},{9,8... | collective-permute-start | bytes 786440 | tf_op jit(solution)/shard_map/s1h6/ppermute | solution.py:453
  91.8 12.8 %collective-permute-start.27 = (bf16[128,2560]{1,0:T(8,128)(2,1)S(1)}, bf16[128,2560]{1,0:T(8,128)(2,1)S(1)}, u32[]{:S(2)}, u32[]{:S(2)}) collective-permute-start(bf16[128,2560]{1,0:T(8,128)(2,1)S(1)} %pad_maximum_fusion.2), channel_id=1, source_target_pairs={{0,1},{1,0},{2,3},{3,2},{4,5},{5,4},{6,7},{7,6},{8,10},{9,11},{10,... | collective-permute-start | bytes 1966088 | tf_op jit(solution)/shard_map/s2h7/ppermute | solution.py:453
  92.4 7.7 %collective-permute-start.23 = (bf16[64,1536]{1,0:T(8,128)(2,1)S(1)}, bf16[64,1536]{1,0:T(8,128)(2,1)S(1)}, u32[]{:S(2)}, u32[]{:S(2)}) collective-permute-start(bf16[64,1536]{1,0:T(8,128)(2,1)S(1)} %pad_maximum_fusion.9), channel_id=1, source_target_pairs={{0,16},{1,17},{2,18},{3,19},{4,20},{5,21},{6,22},{7,23},{8,9},{9,8... | collective-permute-start | bytes 589832 | tf_op jit(solution)/shard_map/s3h6/ppermute | solution.py:453
  94.9 12.3 %collective-permute-start.26 = (bf16[512,512]{1,0:T(8,128)(2,1)S(1)}, bf16[512,512]{1,0:T(8,128)(2,1)S(1)}, u32[]{:S(2)}, u32[]{:S(2)}) collective-permute-start(bf16[512,512]{1,0:T(8,128)(2,1)S(1)} %pad_maximum_fusion.3), channel_id=1, source_target_pairs={{0,2},{1,3},{2,0},{3,1},{4,6},{5,7},{6,4},{7,5},{8,24},{9,25},{10,... | collective-permute-start | bytes 1572872 | tf_op jit(solution)/shard_map/s1h7/ppermute | solution.py:453
  100.1 8.6 %collective-permute-start.25 = (bf16[128,1536]{1,0:T(8,128)(2,1)S(1)}, bf16[128,1536]{1,0:T(8,128)(2,1)S(1)}, u32[]{:S(2)}, u32[]{:S(2)}) collective-permute-start(bf16[128,1536]{1,0:T(8,128)(2,1)S(1)} %pad_maximum_fusion.5), channel_id=1, source_target_pairs={{0,1},{1,0},{2,3},{3,2},{4,5},{5,4},{6,7},{7,6},{8,24},{9,25},{10,... | collective-permute-start | bytes 1179656 | tf_op jit(solution)/shard_map/s3h7/ppermute | solution.py:453
  106.4 4.3 %collective-permute-start.30 = (bf16[256,2560]{1,0:T(8,128)(2,1)S(1)}, bf16[256,2560]{1,0:T(8,128)(2,1)S(1)}, u32[]{:S(2)}, u32[]{:S(2)}) collective-permute-start(bf16[256,2560]{1,0:T(8,128)(2,1)S(1)} %pad_maximum_fusion.refs_0_), channel_id=1, source_target_pairs={{0,8},{1,9},{2,10},{3,11},{4,12},{5,13},{6,14},{7,15},{8,0},{9,1},... | collective-permute-start | bytes 3932168 | tf_op jit(solution)/shard_map/s2h8/ppermute | solution.py:453
  108.7 3.7 %collective-permute-start.29 = (bf16[1024,512]{1,0:T(8,128)(2,1)S(1)}, bf16[1024,512]{1,0:T(8,128)(2,1)S(1)}, u32[]{:S(2)}, u32[]{:S(2)}) collective-permute-start(bf16[1024,512]{1,0:T(8,128)(2,1)S(1)} %pad_maximum_fusion.1.refs_0_), channel_id=1, source_target_pairs={{0,8},{1,9},{2,10},{3,11},{4,12},{5,13},{6,14},{7,15},{8,0},{9,1},... | collective-permute-start | bytes 3145736 | tf_op jit(solution)/shard_map/s1h8/ppermute | solution.py:453
  108.8 5.1 %collective-permute-start.28 = (bf16[260,1536]{1,0:T(8,128)(2,1)S(1)}, bf16[260,1536]{1,0:T(8,128)(2,1)S(1)}, u32[]{:S(2)}, u32[]{:S(2)}) collective-permute-start(bf16[260,1536]{1,0:T(8,128)(2,1)S(1)} %fusion.refs_0_.refs_1_), channel_id=1, source_target_pairs={{0,8},{1,9},{2,10},{3,11},{4,12},{5,13},{6,14},{7,15},{8,0},{9,1},... | collective-permute-start | bytes 2396168 | tf_op jit(solution)/shard_map/s3h8/ppermute | solution.py:453

commit v4 on v3

--- a/solution.py
+++ b/solution.py
@@ -17,7 +17,9 @@
 SQRT_HALF = 0.5**0.5
 PHI_SCALE = (2.0 * math.pi) ** (-0.5)
 NEGATIVE = -1e30
-ORDERS = (("zxyw", "xyzw"), ("yzxw", "zywx"), ("yxwz", "xywz"))
+CUT = 1024
+PACE = 2
+ORDERS = (("zxyw", "xyzw"), ("yzxw", "zywx"), ("yxzw", "xyzw"))
 ORDER = (2, 3, 1, 3, 2, 1, 3, 2, 1, 3, 2, 1, 3, 2, 1, 2, 3, 1, 2, 3, 1, 3, 2, 1, 3, 2, 1, 3)
 
 f32 = jnp.float32
@@ -208,19 +210,20 @@
     small_out[3:4, :] = jnp.sum(dy.astype(f32), axis=0, keepdims=True)
     do_ref[...] = dot_nt(dy, wproj[...]).astype(bf16)
     leave(3)
-    grad_halves(axes, 0, shards, g_ref, cot, keep1, send1)
-    leave(4)
-    leave(5)
-    grad_halves(axes, 1, shards, c_ref, du_ref, keep2, send2, slice(0, hidden))
-    grad_halves(axes, 1, shards, o_ref, dy_ref, keep2, send2, slice(hidden, hidden + width))
-    leave(6)
-    leave(7)
+    jobs = grad_jobs(axes, 1, shards, c_ref, du_ref, keep2, send2)
+    jobs += grad_jobs(axes, 1, shards, o_ref, dy_ref, keep2, send2, hidden)
+    jobs.append(lambda: (leave(6), leave(7)))
+    jobs += grad_jobs(axes, 0, shards, g_ref, cot, keep1, send1)
+    jobs.append(lambda: (leave(4), leave(5)))
 
     for item in range(items):
         for group in range(groups):
             lanes = slice(group * 128, (group + 1) * 128)
             own = slice(item * band, (item + 1) * band)
             ends = slice(item * edge, (item + 1) * edge)
+            for _ in range(PACE):
+                if jobs:
+                    jobs.pop(0)()
             grads = stack_heads(do_ref[own, lanes], lane_head)
             queries = stack_heads(q_ref[own, lanes], lane_head)
             soft = p_ref[item * groups + group]
@@ -256,20 +259,30 @@
     return copies
 
 
-def grad_halves(axes, stream, shards, left, right, keep, send, lanes=slice(None)):
+def grad_jobs(axes, stream, shards, left, right, keep, send, first=0):
     half = left.shape[1] // 2
     per = half // shards
     step = min(half, 256)
+    width = min(right.shape[1], CUT)
     core = axes.bit(axes.core)
-    values = right[...]
+    jobs = []
     for ref, owner in ((keep, core), (send, 1 - core)):
         slot = axes.slot(stream, owner)
         for start in range(0, half, step):
-            columns = pl.ds(pl.multiple_of(owner * half + start, 128), step)
-            product = dot_tn(left[:, columns], values)
-            for index in range(step // per):
-                spot = pl.multiple_of(((start // per + index) ^ slot) * per, per)
-                ref[pl.ds(spot, per), lanes] = product[index * per : (index + 1) * per].astype(bf16)
+            for column in range(0, right.shape[1], width):
+
+                def job(ref=ref, owner=owner, slot=slot, start=start, column=column):
+                    columns = pl.ds(pl.multiple_of(owner * half + start, 128), step)
+                    end = min(column + width, right.shape[1])
+                    product = dot_tn(left[:, columns], right[:, column:end])
+                    lanes = slice(first + column, first + end)
+                    for index in range(step // per):
+                        spot = pl.multiple_of(((start // per + index) ^ slot) * per, per)
+                        rows = slice(index * per, (index + 1) * per)
+                        ref[pl.ds(spot, per), lanes] = product[rows].astype(bf16)
+
+                jobs.append(job)
+    return jobs
 
 
 def qkv_grad_kernel(
@@ -304,7 +317,8 @@
                 if row == lat_dev - 1:
                     value = value + jnp.where(odd, far, near)
                 joined[start : start + lon, columns] = value.astype(bf16)
-    grad_halves(axes, 2, shards, a_low, joined, keep, send)
+    for job in grad_jobs(axes, 2, shards, a_low, joined, keep, send):
+        job()
     leaving = start_copies(locals_[:2], finals[:2], out_sems)
     for copy in fetches[6:]:
         copy.wait()
@@ -326,15 +340,13 @@
         copy.wait()
 
 
-def spread_kernel(axes, stream, shards, splits, other, sums, *refs):
-    count = len(splits)
-    piece = refs[0]
+def spread_kernel(axes, shards, streams, other, sums, *refs):
+    count = sum(len(widths) for _, widths in streams)
+    pieces = refs[: len(streams)]
     outs = refs[-2 * (count + len(sums)) - 1 : -count - len(sums) - 1]
     wide, sems = refs[-count - len(sums) - 1 : -1], refs[-1]
     core = axes.bit(axes.core)
     owner = 1 - core if other else core
-    slot = axes.slot(stream, owner)
-    per = outs[0].shape[0] // (2 * shards)
     copies = []
 
     def leave(source, target, index, part):
@@ -342,19 +354,27 @@
         copy.start()
         copies.append(copy)
 
-    for index in range(shards):
-        spot = pl.multiple_of((owner * shards + (index ^ slot)) * per, per)
-        rows = slice(index * per, (index + 1) * per)
-        first = 0
-        for part, width in enumerate(splits):
-            wide[part][rows, :] = piece[rows, first : first + width].astype(f32)
-            first += width
-            leave(wide[part].at[rows, :], outs[part].at[pl.ds(spot, per), :], index, part)
+    number = 0
+    for piece, (stream, widths) in zip(pieces, streams):
+        slot = axes.slot(stream, owner)
+        per = outs[number].shape[0] // (2 * shards)
+        for index in range(shards):
+            spot = pl.multiple_of((owner * shards + (index ^ slot)) * per, per)
+            rows = slice(index * per, (index + 1) * per)
+            first = 0
+            for part, width in enumerate(widths, number):
+                wide[part][rows, :] = piece[rows, first : first + width].astype(f32)
+                first += width
+                leave(wide[part].at[rows, :], outs[part].at[pl.ds(spot, per), :], index, part)
+        number += len(widths)
     if sums:
-        rows = slice(shards * per, piece.shape[0])
-        total = refs[1][rows, :].astype(f32) + piece[rows, :].astype(f32)
+        rows = slice(shards * per, pieces[-1].shape[0])
+        total = refs[len(streams)][rows, :].astype(f32) + pieces[-1][rows, :].astype(f32)
         width = total.shape[1] // 3
-        taken = [total[k // 3 : k // 3 + 1, k % 3 * width : (k % 3 + 1) * width] for k in range(3 * total.shape[0])]
+        taken = [
+            total[k // 3 : k // 3 + 1, k % 3 * width : (k % 3 + 1) * width]
+            for k in range(3 * total.shape[0])
+        ]
         for part, (first, shape) in enumerate(sums):
             buffer = wide[count + part]
             for k in range(math.prod(shape) // width):
@@ -367,22 +387,25 @@
         copy.wait()
 
 
-def spread(axes, stream, shards, splits, rows, pieces, outs=(), sums=()):
-    held = rows // 2
+def spread(axes, shards, streams, rows, pieces, outs=(), sums=()):
     hbm = pl.BlockSpec(memory_space=pltpu.HBM)
-    shapes = [(rows, width) for width in splits] + [shape for _, shape in sums]
+    shapes = [(count, width) for (_, widths), count in zip(streams, rows) for width in widths]
+    halves = [(count // 2, width) for count, width in shapes]
+    shapes += [shape for _, shape in sums]
     return pl.pallas_call(
-        functools.partial(spread_kernel, axes, stream, shards, splits, bool(outs), sums),
+        functools.partial(spread_kernel, axes, shards, streams, bool(outs), sums),
         out_shape=[jax.ShapeDtypeStruct(shape, f32) for shape in shapes],
         in_specs=[pl.BlockSpec(memory_space=pltpu.VMEM)] * len(pieces) + [hbm] * len(outs),
         out_specs=[hbm] * len(shapes),
-        scratch_shapes=[pltpu.VMEM((held, width), f32) for width in splits]
+        scratch_shapes=[pltpu.VMEM(shape, f32) for shape in halves]
         + [pltpu.VMEM(shape, f32) for _, shape in sums]
-        + [pltpu.SemaphoreType.DMA((max(shards, len(sums)), len(splits) + 1))],
+        + [pltpu.SemaphoreType.DMA((max(shards, len(sums)), len(halves) + 1))],
         input_output_aliases={len(pieces) + index: index for index in range(len(outs))},
-        compiler_params=pltpu.CompilerParams(vmem_limit_bytes=8 * MIB),
+        compiler_params=pltpu.CompilerParams(vmem_limit_bytes=(4 + 4 * len(streams)) * MIB),
         cost_estimate=pl.CostEstimate(
-            flops=0, bytes_accessed=6 * held * sum(splits), transcendentals=0
+            flops=0,
+            bytes_accessed=6 * sum(math.prod(shape) for shape in halves),
+            transcendentals=0,
         ),
     )(*pieces, *outs)
 
@@ -519,7 +542,7 @@
     near = sequence.swap(piece, core, next(label))
     write(piece)
     yield
-    write(piece, sequence.ready(near))
+    write(piece, near)
 
 
 def body(
@@ -613,18 +636,15 @@
     grads = {}
     splits = {1: (width,), 2: (hidden, width), 3: (3 * width,)}
 
+    last = {}
+    rows_of = {1: hidden, 2: width, 3: width}
+
     def stream(name, keep, send, small=None):
-        rows = 2 * keep.shape[0]
-        settings = (axes, name - 1, shards, splits[name], rows)
-
         def write(own, other=None):
             if other is None:
-                grads[name] = spread(*settings, (own,))
-            elif small is None:
-                grads[name] = spread(*settings, (other,), grads[name])
-            else:
-                grads[name] = spread(*settings, (other, own), grads[name], small_places)
-            sequence.token = grads[name][0]
+                grads[name] = spread(axes, shards, ((name - 1, splits[name]),), (rows_of[name],), (own,))
+                sequence.token = grads[name][0]
+            last[name] = own, other
 
         return sum_stream(sequence, name - 1, keep, send, write, small)
 
@@ -677,9 +697,15 @@
         if name not in streams:
             tokens_grad = join()
         next(streams[name], None)
-    (grad_fc2,) = grads[1]
-    grad_fc1, grad_proj = grads[2]
-    grad_qkv, *sums = grads[3]
+    grad_fc2, grad_fc1, grad_proj, grad_qkv, *sums = spread(
+        axes,
+        shards,
+        tuple((name - 1, splits[name]) for name in (1, 2, 3)),
+        tuple(rows_of[name] for name in (1, 2, 3)),
+        tuple(last[name][1] for name in (1, 2, 3)) + (last[3][0],),
+        tuple(out for name in (1, 2, 3) for out in grads[name]),
+        small_places,
+    )
     return (
         mixed.reshape(tokens.shape),
         tokens_grad.reshape(tokens.shape),

time: 116 us -> 114 us (0.983)
  waiting for transfers between devices: 25.8 us -> 36.5 us
  starting transfers between devices: 55.9 us -> 46 us
  Pallas kernels: 27.3 us -> 25.1 us
    ppermute x29, waiting for transfers between devices: 25.8 us -> 36.4 us  [exchange(): return lax.ppermute(value, ('lat', 'items'), pairs)]
    ppermute x29, starting transfers between devices: 54.4 us -> 44.5 us  [exchange(): return lax.ppermute(value, ('lat', 'items'), pairs)]
    pallas_call x6 -> x4, Pallas kernels: 9.01 us -> 7.51 us  [spread(): pl.pallas_call(functools.partial(spread_kernel, axes, shards, streams, bo...]
  transfers between devices with their start and end apart: 31 -> 31, of which waited for: 14 -> 14; matrix products, arithmetic and copies ran while one was open for 3% -> 3% of each run, Pallas kernels for 10% -> 7%
where the time goes in v4:
time: 114 us
  starting transfers between devices  46 us (40%)
  waiting for transfers between devices  36.5 us (32%)
  Pallas kernels  25.1 us (22%)
  other arithmetic  3.83 us (3%)
  local copies, waits for them, and re-layouts  1.41 us (1%)
    ppermute x29, starting transfers between devices, exchange(): return lax.ppermute(value, ('lat', 'items'), pairs)  44.5 us
    ppermute x29, waiting for transfers between devices, exchange(): return lax.ppermute(value, ('lat', 'items'), pairs)  36.4 us
    pallas_call x2, Pallas kernels, on_device(): pl.pallas_call(kernel, out_shape=[jax.ShapeDtypeStruct(shape, dtype) for...  17.6 us
    pallas_call x4, Pallas kernels, spread(): pl.pallas_call(functools.partial(spread_kernel, axes, shards, streams, bo...  7.51 us
  transfers between devices with their start and end apart: 31, of which 14 were waited for; matrix products, arithmetic and copies ran while one was open for 3% of the time, Pallas kernels for 7%

profile of v4, /device:TPU:0, one launch (start us, length us, event | category | flops | bytes accessed | tf_op | source)
XLA Modules:
  0.0 113.9 jit_solution(8402925577196881714)
XLA Ops:
  0.7 1.0 broadcast_select_fusion
  1.6 0.5 collective-permute-start
  2.1 0.7 collective-permute-start.1
  3.1 0.6 copy-done.6
  3.8 13.9 %shard_map.245 = (bf16[192,512]{1,0:T(8,128)(2,1)}, bf16[192,512]{1,0:T(8,128)(2,1)}, f32[192,512]{1,0:T(8,128)}, f32[8,512]{1,0:T(8,128)}, bf16[1024,512]{1,0:T...) custom-call(bf16[192,512]{1,0:T(8,128)(2,1)} %bitcast.6, ...), custom_call_target="tpu_custom_call" | custom-call | flops 2818572288 | bytes 13791232 | tf_op jit(solution)/shard_map/pallas_call | solution.py:417
  17.6 5.9 %collective-permute-start.2 = (bf16[256,2560]{1,0:T(8,128)(2,1)}, bf16[256,2560]{1,0:T(8,128)(2,1)S(1)}, u32[]{:S(2)}, u32[]{:S(2)}) collective-permute-start(bf16[256,2560]{1,0:T(8,128)(2,1)} %get-tuple-element.73), channel_id=1, source_target_pairs={{0,8},{1,9},{2,10},{3,11},{4,12},{5,13},{6,14},{7,15},{8,0},{9,1},... | collective-permute-start | bytes 3932168 | tf_op jit(solution)/shard_map/s2h0/ppermute | solution.py:476
  23.6 0.8 collective-permute-start.4
  24.5 3.5 %collective-permute-start.5 = (bf16[1024,512]{1,0:T(8,128)(2,1)}, bf16[1024,512]{1,0:T(8,128)(2,1)S(1)}, u32[]{:S(2)}, u32[]{:S(2)}) collective-permute-start(bf16[1024,512]{1,0:T(8,128)(2,1)} %get-tuple-element.85), channel_id=1, source_target_pairs={{0,8},{1,9},{2,10},{3,11},{4,12},{5,13},{6,14},{7,15},{8,0},{9,1},... | collective-permute-start | bytes 3145736 | tf_op jit(solution)/shard_map/s1h0/ppermute | solution.py:476
  28.0 1.3 %add_convert_fusion = bf16[128,2560]{1,0:T(8,128)(2,1)S(1)} fusion(bf16[256,2560]{1,0:T(8,128)(2,1)S(1)} %collective-permute-done.2, bf16[256,2560]{1,0:T(8,128)(2,1)} %get-tuple-element.72), kind=kLoop, calls=%fused_computation.1 | loop fusion | flops 1310720 | bytes 1966080 | tf_op jit(solution)/shard_map/convert_element_type | solution.py:517
  29.3 0.7 copy-done.4
  30.0 3.8 %shard_map.246 = (bf16[256,1536]{1,0:T(8,128)(2,1)}, bf16[256,1536]{1,0:T(8,128)(2,1)}, bf16[192,512]{1,0:T(8,128)(2,1)}, bf16[4,1536]{1,0:T(4,128)(2,1)}) custom-call(bf16[192,512]{1,0:T(8,128)(2,1)} %get-tuple-element.76.refs_0_, f32[192,512]{1,0:T(8,128)} %get-tuple-element.77.refs_1_, f32[192,512]{1,0:T(8,128)} %get-tuple-element.78.refs_2_, ...), custom_call_target="tpu_custom_call" | custom-call | flops 603979776 | bytes 5534720 | tf_op jit(solution)/shard_map/pallas_call | solution.py:417
  33.7 2.0 %collective-permute-start.8 = (bf16[256,1536]{1,0:T(8,128)(2,1)}, bf16[256,1536]{1,0:T(8,128)(2,1)S(1)}, u32[]{:S(2)}, u32[]{:S(2)}) collective-permute-start(bf16[256,1536]{1,0:T(8,128)(2,1)} %get-tuple-element.86), channel_id=1, source_target_pairs={{0,8},{1,9},{2,10},{3,11},{4,12},{5,13},{6,14},{7,15},{8,0},{9,1},... | collective-permute-start | bytes 2359304 | tf_op jit(solution)/shard_map/s3h0/ppermute | solution.py:476
  35.8 2.1 %collective-permute-start.7 = (bf16[128,2560]{1,0:T(8,128)(2,1)S(1)}, bf16[128,2560]{1,0:T(8,128)(2,1)S(1)}, u32[]{:S(2)}, u32[]{:S(2)}) collective-permute-start(bf16[128,2560]{1,0:T(8,128)(2,1)S(1)} %add_convert_fusion), channel_id=1, source_target_pairs={{0,1},{1,0},{2,3},{3,2},{4,5},{5,4},{6,7},{7,6},{8,10},{9,11},{10,... | collective-permute-start | bytes 1966088 | tf_op jit(solution)/shard_map/s2h1/ppermute | solution.py:476
  38.0 1.6 %collective-permute-start.6 = (bf16[512,512]{1,0:T(8,128)(2,1)S(1)}, bf16[512,512]{1,0:T(8,128)(2,1)S(1)}, u32[]{:S(2)}, u32[]{:S(2)}) collective-permute-start(bf16[512,512]{1,0:T(8,128)(2,1)S(1)} %add_convert_fusion.1), channel_id=1, source_target_pairs={{0,2},{1,3},{2,0},{3,1},{4,6},{5,7},{6,4},{7,5},{8,24},{9,25},{10,... | collective-permute-start | bytes 1572872 | tf_op jit(solution)/shard_map/s1h1/ppermute | solution.py:476
  39.8 0.6 collective-permute-start.11
  40.4 6.0 %collective-permute-done.7 = bf16[128,2560]{1,0:T(8,128)(2,1)S(1)} collective-permute-done((bf16[128,2560]{1,0:T(8,128)(2,1)S(1)}, bf16[128,2560]{1,0:T(8,128)(2,1)S(1)}, u32[]{:S(2)}, u32[]{:S(2)}) %collective-permute-start.7) | collective-permute-done | bytes 655392 | tf_op jit(solution)/shard_map/s2h1/ppermute | solution.py:476
  46.6 2.1 %collective-permute-start.10 = (bf16[64,2560]{1,0:T(8,128)(2,1)S(1)}, bf16[64,2560]{1,0:T(8,128)(2,1)S(1)}, u32[]{:S(2)}, u32[]{:S(2)}) collective-permute-start(bf16[64,2560]{1,0:T(8,128)(2,1)S(1)} %add_convert_fusion.3), channel_id=1, source_target_pairs={{0,2},{1,3},{2,0},{3,1},{4,6},{5,7},{6,4},{7,5},{8,9},{9,8},{10,11... | collective-permute-start | bytes 983048 | tf_op jit(solution)/shard_map/s2h2/ppermute | solution.py:476
  48.7 2.8 %collective-permute-done.6 = bf16[512,512]{1,0:T(8,128)(2,1)S(1)} collective-permute-done((bf16[512,512]{1,0:T(8,128)(2,1)S(1)}, bf16[512,512]{1,0:T(8,128)(2,1)S(1)}, u32[]{:S(2)}, u32[]{:S(2)}) %collective-permute-start.6) | collective-permute-done | bytes 524320 | tf_op jit(solution)/shard_map/s1h1/ppermute | solution.py:476
  51.6 1.7 %collective-permute-start.9 = (bf16[256,512]{1,0:T(8,128)(2,1)S(1)}, bf16[256,512]{1,0:T(8,128)(2,1)S(1)}, u32[]{:S(2)}, u32[]{:S(2)}) collective-permute-start(bf16[256,512]{1,0:T(8,128)(2,1)S(1)} %add_convert_fusion.4), channel_id=1, source_target_pairs={{0,16},{1,17},{2,18},{3,19},{4,20},{5,21},{6,22},{7,23},{8,9},{9,8... | collective-permute-start | bytes 786440 | tf_op jit(solution)/shard_map/s1h2/ppermute | solution.py:476
  53.4 0.5 collective-permute-start.14
  53.9 1.1 collective-permute-done.10
  55.1 1.7 %collective-permute-start.13 = (bf16[32,2560]{1,0:T(8,128)(2,1)S(1)}, bf16[32,2560]{1,0:T(8,128)(2,1)S(1)}, u32[]{:S(2)}, u32[]{:S(2)}) collective-permute-start(bf16[32,2560]{1,0:T(8,128)(2,1)S(1)} %add_convert_fusion.8), channel_id=1, source_target_pairs={{0,16},{1,17},{2,18},{3,19},{4,20},{5,21},{6,22},{7,23},{8,12},{9,... | collective-permute-start | bytes 491528 | tf_op jit(solution)/shard_map/s2h3/ppermute | solution.py:476
  56.8 1.3 %collective-permute-done.9 = bf16[256,512]{1,0:T(8,128)(2,1)S(1)} collective-permute-done((bf16[256,512]{1,0:T(8,128)(2,1)S(1)}, bf16[256,512]{1,0:T(8,128)(2,1)S(1)}, u32[]{:S(2)}, u32[]{:S(2)}) %collective-permute-start.9) | collective-permute-done | bytes 262176 | tf_op jit(solution)/shard_map/s1h2/ppermute | solution.py:476
  58.1 1.5 %collective-permute-start.12 = (bf16[128,512]{1,0:T(8,128)(2,1)S(1)}, bf16[128,512]{1,0:T(8,128)(2,1)S(1)}, u32[]{:S(2)}, u32[]{:S(2)}) collective-permute-start(bf16[128,512]{1,0:T(8,128)(2,1)S(1)} %add_convert_fusion.11), channel_id=1, source_target_pairs={{0,1},{1,0},{2,3},{3,2},{4,5},{5,4},{6,7},{7,6},{8,10},{9,11},{10,... | collective-permute-start | bytes 393224 | tf_op jit(solution)/shard_map/s1h3/ppermute | solution.py:476
  59.7 0.8 collective-permute-done.14
  60.5 1.8 %collective-permute-start.17 = (bf16[36,1536]{1,0:T(8,128)(2,1)S(1)}, bf16[36,1536]{1,0:T(8,128)(2,1)S(1)}, u32[]{:S(2)}, u32[]{:S(2)}) collective-permute-start(bf16[36,1536]{1,0:T(8,128)(2,1)S(1)} %pad_maximum_fusion.10), channel_id=1, source_target_pairs={{0,2},{1,3},{2,0},{3,1},{4,6},{5,7},{6,4},{7,5},{8,10},{9,11},{10,... | collective-permute-start | bytes 331784 | tf_op jit(solution)/shard_map/s3h3/ppermute | solution.py:476
  62.5 2.7 %collective-permute-start.16 = (bf16[32,2560]{1,0:T(8,128)(2,1)S(1)}, bf16[32,2560]{1,0:T(8,128)(2,1)S(1)}, u32[]{:S(2)}, u32[]{:S(2)}) collective-permute-start(bf16[32,2560]{1,0:T(8,128)(2,1)S(1)} %add_convert_fusion.7), channel_id=1, source_target_pairs={{0,4},{1,5},{2,6},{3,7},{4,0},{5,1},{6,2},{7,3},{8,24},{9,25},{10,... | collective-permute-start | bytes 491528 | tf_op jit(solution)/shard_map/s2h4/ppermute | solution.py:476
  65.2 1.7 %collective-permute-start.15 = (bf16[128,512]{1,0:T(8,128)(2,1)S(1)}, bf16[128,512]{1,0:T(8,128)(2,1)S(1)}, u32[]{:S(2)}, u32[]{:S(2)}) collective-permute-start(bf16[128,512]{1,0:T(8,128)(2,1)S(1)} %add_convert_fusion.10), channel_id=1, source_target_pairs={{0,4},{1,5},{2,6},{3,7},{4,0},{5,1},{6,2},{7,3},{8,12},{9,13},{10,... | collective-permute-start | bytes 393224 | tf_op jit(solution)/shard_map/s1h4/ppermute | solution.py:476
  66.9 2.3 %collective-permute-done.17 = bf16[36,1536]{1,0:T(8,128)(2,1)S(1)} collective-permute-done((bf16[36,1536]{1,0:T(8,128)(2,1)S(1)}, bf16[36,1536]{1,0:T(8,128)(2,1)S(1)}, u32[]{:S(2)}, u32[]{:S(2)}) %collective-permute-start.17) | collective-permute-done | bytes 110624 | tf_op jit(solution)/shard_map/s3h3/ppermute | solution.py:476
  70.0 1.6 %collective-permute-start.20 = (bf16[32,2560]{1,0:T(8,128)(2,1)S(1)}, bf16[32,2560]{1,0:T(8,128)(2,1)S(1)}, u32[]{:S(2)}, u32[]{:S(2)}) collective-permute-start(bf16[32,2560]{1,0:T(8,128)(2,1)S(1)} %add_convert_fusion.6), channel_id=1, source_target_pairs={{0,16},{1,17},{2,18},{3,19},{4,20},{5,21},{6,22},{7,23},{8,12},{9,... | collective-permute-start | bytes 491528 | tf_op jit(solution)/shard_map/s2h5/ppermute | solution.py:476
  71.6 8.3 %collective-permute-done.15 = bf16[128,512]{1,0:T(8,128)(2,1)S(1)} collective-permute-done((bf16[128,512]{1,0:T(8,128)(2,1)S(1)}, bf16[128,512]{1,0:T(8,128)(2,1)S(1)}, u32[]{:S(2)}, u32[]{:S(2)}) %collective-permute-start.15) | collective-permute-done | bytes 131104 | tf_op jit(solution)/shard_map/s1h4/ppermute | solution.py:476
  80.0 1.3 %collective-permute-start.18 = (bf16[128,512]{1,0:T(8,128)(2,1)S(1)}, bf16[128,512]{1,0:T(8,128)(2,1)S(1)}, u32[]{:S(2)}, u32[]{:S(2)}) collective-permute-start(bf16[128,512]{1,0:T(8,128)(2,1)S(1)} %add_convert_fusion.9), channel_id=1, source_target_pairs={{0,1},{1,0},{2,3},{3,2},{4,5},{5,4},{6,7},{7,6},{8,10},{9,11},{10,... | collective-permute-start | bytes 393224 | tf_op jit(solution)/shard_map/s1h5/ppermute | solution.py:476
  81.3 3.6 %collective-permute-start.23 = (bf16[64,2560]{1,0:T(8,128)(2,1)S(1)}, bf16[64,2560]{1,0:T(8,128)(2,1)S(1)}, u32[]{:S(2)}, u32[]{:S(2)}) collective-permute-start(bf16[64,2560]{1,0:T(8,128)(2,1)S(1)} %pad_maximum_fusion.6), channel_id=1, source_target_pairs={{0,2},{1,3},{2,0},{3,1},{4,6},{5,7},{6,4},{7,5},{8,9},{9,8},{10,11... | collective-permute-start | bytes 983048 | tf_op jit(solution)/shard_map/s2h6/ppermute | solution.py:476
  85.0 1.5 %collective-permute-start.21 = (bf16[256,512]{1,0:T(8,128)(2,1)S(1)}, bf16[256,512]{1,0:T(8,128)(2,1)S(1)}, u32[]{:S(2)}, u32[]{:S(2)}) collective-permute-start(bf16[256,512]{1,0:T(8,128)(2,1)S(1)} %pad_maximum_fusion.7), channel_id=1, source_target_pairs={{0,16},{1,17},{2,18},{3,19},{4,20},{5,21},{6,22},{7,23},{8,9},{9,8... | collective-permute-start | bytes 786440 | tf_op jit(solution)/shard_map/s1h6/ppermute | solution.py:476
  86.6 4.4 %collective-permute-done.23 = bf16[64,2560]{1,0:T(8,128)(2,1)S(1)} collective-permute-done((bf16[64,2560]{1,0:T(8,128)(2,1)S(1)}, bf16[64,2560]{1,0:T(8,128)(2,1)S(1)}, u32[]{:S(2)}, u32[]{:S(2)}) %collective-permute-start.23) | collective-permute-done | bytes 327712 | tf_op jit(solution)/shard_map/s2h6/ppermute | solution.py:476
  91.0 1.5 %collective-permute-start.25 = (bf16[128,2560]{1,0:T(8,128)(2,1)S(1)}, bf16[128,2560]{1,0:T(8,128)(2,1)S(1)}, u32[]{:S(2)}, u32[]{:S(2)}) collective-permute-start(bf16[128,2560]{1,0:T(8,128)(2,1)S(1)} %pad_maximum_fusion.2), channel_id=1, source_target_pairs={{0,1},{1,0},{2,3},{3,2},{4,5},{5,4},{6,7},{7,6},{8,10},{9,11},{10,... | collective-permute-start | bytes 1966088 | tf_op jit(solution)/shard_map/s2h7/ppermute | solution.py:476
  92.6 1.4 %collective-permute-start.26 = (bf16[64,1536]{1,0:T(8,128)(2,1)S(1)}, bf16[64,1536]{1,0:T(8,128)(2,1)S(1)}, u32[]{:S(2)}, u32[]{:S(2)}) collective-permute-start(bf16[64,1536]{1,0:T(8,128)(2,1)S(1)} %pad_maximum_fusion.9), channel_id=1, source_target_pairs={{0,16},{1,17},{2,18},{3,19},{4,20},{5,21},{6,22},{7,23},{8,9},{9,8... | collective-permute-start | bytes 589832 | tf_op jit(solution)/shard_map/s3h6/ppermute | solution.py:476
  94.0 1.4 %collective-permute-start.24 = (bf16[512,512]{1,0:T(8,128)(2,1)S(1)}, bf16[512,512]{1,0:T(8,128)(2,1)S(1)}, u32[]{:S(2)}, u32[]{:S(2)}) collective-permute-start(bf16[512,512]{1,0:T(8,128)(2,1)S(1)} %pad_maximum_fusion.3), channel_id=1, source_target_pairs={{0,2},{1,3},{2,0},{3,1},{4,6},{5,7},{6,4},{7,5},{8,24},{9,25},{10,... | collective-permute-start | bytes 1572872 | tf_op jit(solution)/shard_map/s1h7/ppermute | solution.py:476
  95.4 4.8 %collective-permute-done.26 = bf16[64,1536]{1,0:T(8,128)(2,1)S(1)} collective-permute-done((bf16[64,1536]{1,0:T(8,128)(2,1)S(1)}, bf16[64,1536]{1,0:T(8,128)(2,1)S(1)}, u32[]{:S(2)}, u32[]{:S(2)}) %collective-permute-start.26) | collective-permute-done | bytes 196640 | tf_op jit(solution)/shard_map/s3h6/ppermute | solution.py:476
  100.2 0.5 collective-permute-start.29
  100.7 3.0 %collective-permute-done.25 = bf16[128,2560]{1,0:T(8,128)(2,1)S(1)} collective-permute-done((bf16[128,2560]{1,0:T(8,128)(2,1)S(1)}, bf16[128,2560]{1,0:T(8,128)(2,1)S(1)}, u32[]{:S(2)}, u32[]{:S(2)}) %collective-permute-start.25) | collective-permute-done | bytes 655392 | tf_op jit(solution)/shard_map/s2h7/ppermute | solution.py:476
  103.8 0.5 collective-permute-start.28
  104.3 1.7 %shard_map.247 = (f32[512,2048]{1,0:T(8,128)}, f32[512,512]{1,0:T(8,128)}) custom-call(bf16[256,2560]{1,0:T(8,128)(2,1)S(1)} %pad_maximum_fusion.refs_0_), custom_call_target="tpu_custom_call" | custom-call | bytes 3932160 | tf_op jit(solution)/shard_map/pallas_call | solution.py:395
  106.7 1.5 %shard_map.248.refs_4_ = f32[2048,512]{1,0:T(8,128)} custom-call(bf16[1024,512]{1,0:T(8,128)(2,1)S(1)} %pad_maximum_fusion.1.refs_0_), custom_call_target="tpu_custom_call" | custom-call | bytes 3145728 | tf_op jit(solution)/shard_map/pallas_call | solution.py:395
  108.2 0.6 collective-permute-start.30
  108.8 1.3 %shard_map.249.refs_7_ = f32[512,1536]{1,0:T(8,128)} custom-call(bf16[260,1536]{1,0:T(8,128)(2,1)S(1)} %fusion.refs_0_.refs_3_), custom_call_target="tpu_custom_call" | custom-call | bytes 2359296 | tf_op jit(solution)/shard_map/pallas_call | solution.py:395
  110.1 0.6 collective-permute-done.30.refs_2_
  110.7 3.0 %shard_map.250 = (f32[2048,512]{1,0:T(8,128)}, f32[512,2048]{1,0:T(8,128)}, f32[512,512]{1,0:T(8,128)}, f32[512,1536]{1,0:T(8,128)}, f32[512]{0:T(512)}, /*index...) custom-call(bf16[1024,512]{1,0:T(8,128)(2,1)S(1)} %collective-permut, ...), custom_call_target="tpu_custom_call", output_to_operand_aliasing={{0}: (4, {}), {1}: (5, {}), {2}: (6, {}), {3}: (7, {})} | custom-call | bytes 9437184 | tf_op jit(solution)/shard_map/pallas_call | solution.py:395
  (71 shorter events, 3.2 us)
Async XLA Ops:
  1.6 1.5 %collective-permute-start = (bf16[96,512]{1,0:T(8,128)(2,1)S(1)}, bf16[96,512]{1,0:T(8,128)(2,1)S(1)}, u32[]{:S(2)}, u32[]{:S(2)}) collective-permute-start(bf16[96,512]{1,0:T(8,128)(2,1)S(1)} %bitcast.9), channel_id=1, source_target_pairs={{0,8},{1,9},{2,10},{3,11},{4,12},{5,13},{6,14},{7,15},{8,0},{9,1},... | collective-permute-start | bytes 294920 | tf_op jit(solution)/shard_map/ppermute | solution.py:476
  2.1 0.9 collective-permute-start.1
  3.1 0.6 copy-start.6
  3.1 0.7 copy-start.7
  17.6 10.3 %collective-permute-start.2 = (bf16[256,2560]{1,0:T(8,128)(2,1)}, bf16[256,2560]{1,0:T(8,128)(2,1)S(1)}, u32[]{:S(2)}, u32[]{:S(2)}) collective-permute-start(bf16[256,2560]{1,0:T(8,128)(2,1)} %get-tuple-element.73), channel_id=1, source_target_pairs={{0,8},{1,9},{2,10},{3,11},{4,12},{5,13},{6,14},{7,15},{8,0},{9,1},... | collective-permute-start | bytes 3932168 | tf_op jit(solution)/shard_map/s2h0/ppermute | solution.py:476
  23.5 4.4 %collective-permute-start.3 = (bf16[2,96,512]{2,1,0:T(8,128)(2,1)}, bf16[2,96,512]{2,1,0:T(8,128)(2,1)S(1)}, u32[]{:S(2)}, u32[]{:S(2)}) collective-permute-start(bf16[2,96,512]{2,1,0:T(8,128)(2,1)} %get-tuple-element.74), channel_id=1, source_target_pairs={{0,8},{1,9},{2,10},{3,11},{4,12},{5,13},{6,14},{7,15},{8,0},{9,1},... | collective-permute-start | bytes 589832 | tf_op jit(solution)/shard_map/ppermute | solution.py:476
  23.6 5.7 %collective-permute-start.4 = (bf16[2,96,512]{2,1,0:T(8,128)(2,1)}, bf16[2,96,512]{2,1,0:T(8,128)(2,1)S(1)}, u32[]{:S(2)}, u32[]{:S(2)}) collective-permute-start(bf16[2,96,512]{2,1,0:T(8,128)(2,1)} %get-tuple-element.79), channel_id=1, source_target_pairs={{8,16},{16,8},{9,17},{17,9},{10,18},{18,10},{11,19},{19,11},{12,20... | collective-permute-start | bytes 589832 | tf_op jit(solution)/shard_map/ppermute | solution.py:468
  24.5 13.4 %collective-permute-start.5 = (bf16[1024,512]{1,0:T(8,128)(2,1)}, bf16[1024,512]{1,0:T(8,128)(2,1)S(1)}, u32[]{:S(2)}, u32[]{:S(2)}) collective-permute-start(bf16[1024,512]{1,0:T(8,128)(2,1)} %get-tuple-element.85), channel_id=1, source_target_pairs={{0,8},{1,9},{2,10},{3,11},{4,12},{5,13},{6,14},{7,15},{8,0},{9,1},... | collective-permute-start | bytes 3145736 | tf_op jit(solution)/shard_map/s1h0/ppermute | solution.py:476
  27.9 1.3 %copy-start.3 = (bf16[2,96,512]{2,1,0:T(8,128)(2,1)}, bf16[2,96,512]{2,1,0:T(8,128)(2,1)S(1)}, u32[]{:S(2)}) copy-start(bf16[2,96,512]{2,1,0:T(8,128)(2,1)S(1)} %collective-permute-done.3.refs_3_) | copy-start | bytes 589828
  29.3 0.7 copy-start.4
  30.0 7.9 %copy-start.1 = (bf16[1024,512]{1,0:T(8,128)(2,1)S(1)}, bf16[1024,512]{1,0:T(8,128)(2,1)}, u32[]{:S(2)}) copy-start(bf16[1024,512]{1,0:T(8,128)(2,1)} %get-tuple-element.84) | copy-start | bytes 3145732
  33.7 6.0 %copy-start.2 = (bf16[256,1536]{1,0:T(8,128)(2,1)S(1)}, bf16[256,1536]{1,0:T(8,128)(2,1)}, u32[]{:S(2)}) copy-start(bf16[256,1536]{1,0:T(8,128)(2,1)} %get-tuple-element.88) | copy-start | bytes 2359300
  33.7 5.9 %collective-permute-start.8 = (bf16[256,1536]{1,0:T(8,128)(2,1)}, bf16[256,1536]{1,0:T(8,128)(2,1)S(1)}, u32[]{:S(2)}, u32[]{:S(2)}) collective-permute-start(bf16[256,1536]{1,0:T(8,128)(2,1)} %get-tuple-element.86), channel_id=1, source_target_pairs={{0,8},{1,9},{2,10},{3,11},{4,12},{5,13},{6,14},{7,15},{8,0},{9,1},... | collective-permute-start | bytes 2359304 | tf_op jit(solution)/shard_map/s3h0/ppermute | solution.py:476
  35.8 10.7 %collective-permute-start.7 = (bf16[128,2560]{1,0:T(8,128)(2,1)S(1)}, bf16[128,2560]{1,0:T(8,128)(2,1)S(1)}, u32[]{:S(2)}, u32[]{:S(2)}) collective-permute-start(bf16[128,2560]{1,0:T(8,128)(2,1)S(1)} %add_convert_fusion), channel_id=1, source_target_pairs={{0,1},{1,0},{2,3},{3,2},{4,5},{5,4},{6,7},{7,6},{8,10},{9,11},{10,... | collective-permute-start | bytes 1966088 | tf_op jit(solution)/shard_map/s2h1/ppermute | solution.py:476
  37.9 1.9 %copy-start.5 = (bf16[4,1536]{1,0:T(4,128)(2,1)S(1)}, bf16[4,1536]{1,0:T(4,128)(2,1)}, u32[]{:S(2)}) copy-start(bf16[4,1536]{1,0:T(4,128)(2,1)} %get-tuple-element.90) | copy-start | bytes 36868
  38.0 8.4 %copy-start = (bf16[256,2560]{1,0:T(8,128)(2,1)S(1)}, bf16[256,2560]{1,0:T(8,128)(2,1)}, u32[]{:S(2)}) copy-start(bf16[256,2560]{1,0:T(8,128)(2,1)} %get-tuple-element.72) | copy-start | bytes 3932164
  38.0 13.5 %collective-permute-start.6 = (bf16[512,512]{1,0:T(8,128)(2,1)S(1)}, bf16[512,512]{1,0:T(8,128)(2,1)S(1)}, u32[]{:S(2)}, u32[]{:S(2)}) collective-permute-start(bf16[512,512]{1,0:T(8,128)(2,1)S(1)} %add_convert_fusion.1), channel_id=1, source_target_pairs={{0,2},{1,3},{2,0},{3,1},{4,6},{5,7},{6,4},{7,5},{8,24},{9,25},{10,... | collective-permute-start | bytes 1572872 | tf_op jit(solution)/shard_map/s1h1/ppermute | solution.py:476
  39.8 13.5 %collective-permute-start.11 = (bf16[132,1536]{1,0:T(8,128)(2,1)S(1)}, bf16[132,1536]{1,0:T(8,128)(2,1)S(1)}, u32[]{:S(2)}, u32[]{:S(2)}) collective-permute-start(bf16[132,1536]{1,0:T(8,128)(2,1)S(1)} %pad_maximum_fusion.4), channel_id=1, source_target_pairs={{0,1},{1,0},{2,3},{3,2},{4,5},{5,4},{6,7},{7,6},{8,24},{9,25},{10,... | collective-permute-start | bytes 1216520 | tf_op jit(solution)/shard_map/s3h1/ppermute | solution.py:476
  46.6 8.5 %collective-permute-start.10 = (bf16[64,2560]{1,0:T(8,128)(2,1)S(1)}, bf16[64,2560]{1,0:T(8,128)(2,1)S(1)}, u32[]{:S(2)}, u32[]{:S(2)}) collective-permute-start(bf16[64,2560]{1,0:T(8,128)(2,1)S(1)} %add_convert_fusion.3), channel_id=1, source_target_pairs={{0,2},{1,3},{2,0},{3,1},{4,6},{5,7},{6,4},{7,5},{8,9},{9,8},{10,11... | collective-permute-start | bytes 983048 | tf_op jit(solution)/shard_map/s2h2/ppermute | solution.py:476
  51.6 6.4 %collective-permute-start.9 = (bf16[256,512]{1,0:T(8,128)(2,1)S(1)}, bf16[256,512]{1,0:T(8,128)(2,1)S(1)}, u32[]{:S(2)}, u32[]{:S(2)}) collective-permute-start(bf16[256,512]{1,0:T(8,128)(2,1)S(1)} %add_convert_fusion.4), channel_id=1, source_target_pairs={{0,16},{1,17},{2,18},{3,19},{4,20},{5,21},{6,22},{7,23},{8,9},{9,8... | collective-permute-start | bytes 786440 | tf_op jit(solution)/shard_map/s1h2/ppermute | solution.py:476
  53.4 7.0 %collective-permute-start.14 = (bf16[68,1536]{1,0:T(8,128)(2,1)S(1)}, bf16[68,1536]{1,0:T(8,128)(2,1)S(1)}, u32[]{:S(2)}, u32[]{:S(2)}) collective-permute-start(bf16[68,1536]{1,0:T(8,128)(2,1)S(1)} %pad_maximum_fusion.8), channel_id=1, source_target_pairs={{0,16},{1,17},{2,18},{3,19},{4,20},{5,21},{6,22},{7,23},{8,9},{9,8... | collective-permute-start | bytes 626696 | tf_op jit(solution)/shard_map/s3h2/ppermute | solution.py:476
  55.1 7.2 %collective-permute-start.13 = (bf16[32,2560]{1,0:T(8,128)(2,1)S(1)}, bf16[32,2560]{1,0:T(8,128)(2,1)S(1)}, u32[]{:S(2)}, u32[]{:S(2)}) collective-permute-start(bf16[32,2560]{1,0:T(8,128)(2,1)S(1)} %add_convert_fusion.8), channel_id=1, source_target_pairs={{0,16},{1,17},{2,18},{3,19},{4,20},{5,21},{6,22},{7,23},{8,12},{9,... | collective-permute-start | bytes 491528 | tf_op jit(solution)/shard_map/s2h3/ppermute | solution.py:476
  58.1 7.0 %collective-permute-start.12 = (bf16[128,512]{1,0:T(8,128)(2,1)S(1)}, bf16[128,512]{1,0:T(8,128)(2,1)S(1)}, u32[]{:S(2)}, u32[]{:S(2)}) collective-permute-start(bf16[128,512]{1,0:T(8,128)(2,1)S(1)} %add_convert_fusion.11), channel_id=1, source_target_pairs={{0,1},{1,0},{2,3},{3,2},{4,5},{5,4},{6,7},{7,6},{8,10},{9,11},{10,... | collective-permute-start | bytes 393224 | tf_op jit(solution)/shard_map/s1h3/ppermute | solution.py:476
  60.5 8.7 %collective-permute-start.17 = (bf16[36,1536]{1,0:T(8,128)(2,1)S(1)}, bf16[36,1536]{1,0:T(8,128)(2,1)S(1)}, u32[]{:S(2)}, u32[]{:S(2)}) collective-permute-start(bf16[36,1536]{1,0:T(8,128)(2,1)S(1)} %pad_maximum_fusion.10), channel_id=1, source_target_pairs={{0,2},{1,3},{2,0},{3,1},{4,6},{5,7},{6,4},{7,5},{8,10},{9,11},{10,... | collective-permute-start | bytes 331784 | tf_op jit(solution)/shard_map/s3h3/ppermute | solution.py:476
  62.5 7.5 %collective-permute-start.16 = (bf16[32,2560]{1,0:T(8,128)(2,1)S(1)}, bf16[32,2560]{1,0:T(8,128)(2,1)S(1)}, u32[]{:S(2)}, u32[]{:S(2)}) collective-permute-start(bf16[32,2560]{1,0:T(8,128)(2,1)S(1)} %add_convert_fusion.7), channel_id=1, source_target_pairs={{0,4},{1,5},{2,6},{3,7},{4,0},{5,1},{6,2},{7,3},{8,24},{9,25},{10,... | collective-permute-start | bytes 491528 | tf_op jit(solution)/shard_map/s2h4/ppermute | solution.py:476
  65.2 14.7 %collective-permute-start.15 = (bf16[128,512]{1,0:T(8,128)(2,1)S(1)}, bf16[128,512]{1,0:T(8,128)(2,1)S(1)}, u32[]{:S(2)}, u32[]{:S(2)}) collective-permute-start(bf16[128,512]{1,0:T(8,128)(2,1)S(1)} %add_convert_fusion.10), channel_id=1, source_target_pairs={{0,4},{1,5},{2,6},{3,7},{4,0},{5,1},{6,2},{7,3},{8,12},{9,13},{10,... | collective-permute-start | bytes 393224 | tf_op jit(solution)/shard_map/s1h4/ppermute | solution.py:476
  69.4 15.5 %collective-permute-start.19 = (bf16[36,1536]{1,0:T(8,128)(2,1)S(1)}, bf16[36,1536]{1,0:T(8,128)(2,1)S(1)}, u32[]{:S(2)}, u32[]{:S(2)}) collective-permute-start(bf16[36,1536]{1,0:T(8,128)(2,1)S(1)} %pad_maximum_fusion.11), channel_id=1, source_target_pairs={{0,4},{1,5},{2,6},{3,7},{4,0},{5,1},{6,2},{7,3},{8,12},{9,13},{10,... | collective-permute-start | bytes 331784 | tf_op jit(solution)/shard_map/s3h4/ppermute | solution.py:476
  70.0 11.3 %collective-permute-start.20 = (bf16[32,2560]{1,0:T(8,128)(2,1)S(1)}, bf16[32,2560]{1,0:T(8,128)(2,1)S(1)}, u32[]{:S(2)}, u32[]{:S(2)}) collective-permute-start(bf16[32,2560]{1,0:T(8,128)(2,1)S(1)} %add_convert_fusion.6), channel_id=1, source_target_pairs={{0,16},{1,17},{2,18},{3,19},{4,20},{5,21},{6,22},{7,23},{8,12},{9,... | collective-permute-start | bytes 491528 | tf_op jit(solution)/shard_map/s2h5/ppermute | solution.py:476
  80.0 5.1 %collective-permute-start.18 = (bf16[128,512]{1,0:T(8,128)(2,1)S(1)}, bf16[128,512]{1,0:T(8,128)(2,1)S(1)}, u32[]{:S(2)}, u32[]{:S(2)}) collective-permute-start(bf16[128,512]{1,0:T(8,128)(2,1)S(1)} %add_convert_fusion.9), channel_id=1, source_target_pairs={{0,1},{1,0},{2,3},{3,2},{4,5},{5,4},{6,7},{7,6},{8,10},{9,11},{10,... | collective-permute-start | bytes 393224 | tf_op jit(solution)/shard_map/s1h5/ppermute | solution.py:476
  81.3 9.7 %collective-permute-start.23 = (bf16[64,2560]{1,0:T(8,128)(2,1)S(1)}, bf16[64,2560]{1,0:T(8,128)(2,1)S(1)}, u32[]{:S(2)}, u32[]{:S(2)}) collective-permute-start(bf16[64,2560]{1,0:T(8,128)(2,1)S(1)} %pad_maximum_fusion.6), channel_id=1, source_target_pairs={{0,2},{1,3},{2,0},{3,1},{4,6},{5,7},{6,4},{7,5},{8,9},{9,8},{10,11... | collective-permute-start | bytes 983048 | tf_op jit(solution)/shard_map/s2h6/ppermute | solution.py:476
  84.9 7.6 %collective-permute-start.22 = (bf16[32,1536]{1,0:T(8,128)(2,1)S(1)}, bf16[32,1536]{1,0:T(8,128)(2,1)S(1)}, u32[]{:S(2)}, u32[]{:S(2)}) collective-permute-start(bf16[32,1536]{1,0:T(8,128)(2,1)S(1)} %get-tuple-element.127), channel_id=1, source_target_pairs={{0,2},{1,3},{2,0},{3,1},{4,6},{5,7},{6,4},{7,5},{8,10},{9,11},{10,... | collective-permute-start | bytes 294920 | tf_op jit(solution)/shard_map/s3h5/ppermute | solution.py:476
  85.0 8.9 %collective-permute-start.21 = (bf16[256,512]{1,0:T(8,128)(2,1)S(1)}, bf16[256,512]{1,0:T(8,128)(2,1)S(1)}, u32[]{:S(2)}, u32[]{:S(2)}) collective-permute-start(bf16[256,512]{1,0:T(8,128)(2,1)S(1)} %pad_maximum_fusion.7), channel_id=1, source_target_pairs={{0,16},{1,17},{2,18},{3,19},{4,20},{5,21},{6,22},{7,23},{8,9},{9,8... | collective-permute-start | bytes 786440 | tf_op jit(solution)/shard_map/s1h6/ppermute | solution.py:476
  91.0 12.7 %collective-permute-start.25 = (bf16[128,2560]{1,0:T(8,128)(2,1)S(1)}, bf16[128,2560]{1,0:T(8,128)(2,1)S(1)}, u32[]{:S(2)}, u32[]{:S(2)}) collective-permute-start(bf16[128,2560]{1,0:T(8,128)(2,1)S(1)} %pad_maximum_fusion.2), channel_id=1, source_target_pairs={{0,1},{1,0},{2,3},{3,2},{4,5},{5,4},{6,7},{7,6},{8,10},{9,11},{10,... | collective-permute-start | bytes 1966088 | tf_op jit(solution)/shard_map/s2h7/ppermute | solution.py:476
  92.6 7.6 %collective-permute-start.26 = (bf16[64,1536]{1,0:T(8,128)(2,1)S(1)}, bf16[64,1536]{1,0:T(8,128)(2,1)S(1)}, u32[]{:S(2)}, u32[]{:S(2)}) collective-permute-start(bf16[64,1536]{1,0:T(8,128)(2,1)S(1)} %pad_maximum_fusion.9), channel_id=1, source_target_pairs={{0,16},{1,17},{2,18},{3,19},{4,20},{5,21},{6,22},{7,23},{8,9},{9,8... | collective-permute-start | bytes 589832 | tf_op jit(solution)/shard_map/s3h6/ppermute | solution.py:476
  94.0 12.5 %collective-permute-start.24 = (bf16[512,512]{1,0:T(8,128)(2,1)S(1)}, bf16[512,512]{1,0:T(8,128)(2,1)S(1)}, u32[]{:S(2)}, u32[]{:S(2)}) collective-permute-start(bf16[512,512]{1,0:T(8,128)(2,1)S(1)} %pad_maximum_fusion.3), channel_id=1, source_target_pairs={{0,2},{1,3},{2,0},{3,1},{4,6},{5,7},{6,4},{7,5},{8,24},{9,25},{10,... | collective-permute-start | bytes 1572872 | tf_op jit(solution)/shard_map/s1h7/ppermute | solution.py:476
  100.2 7.9 %collective-permute-start.29 = (bf16[128,1536]{1,0:T(8,128)(2,1)S(1)}, bf16[128,1536]{1,0:T(8,128)(2,1)S(1)}, u32[]{:S(2)}, u32[]{:S(2)}) collective-permute-start(bf16[128,1536]{1,0:T(8,128)(2,1)S(1)} %pad_maximum_fusion.5), channel_id=1, source_target_pairs={{0,1},{1,0},{2,3},{3,2},{4,5},{5,4},{6,7},{7,6},{8,24},{9,25},{10,... | collective-permute-start | bytes 1179656 | tf_op jit(solution)/shard_map/s3h7/ppermute | solution.py:476
  103.8 6.9 %collective-permute-start.28 = (bf16[256,2560]{1,0:T(8,128)(2,1)S(1)}, bf16[256,2560]{1,0:T(8,128)(2,1)S(1)}, u32[]{:S(2)}, u32[]{:S(2)}) collective-permute-start(bf16[256,2560]{1,0:T(8,128)(2,1)S(1)} %pad_maximum_fusion.refs_0_), channel_id=1, source_target_pairs={{0,8},{1,9},{2,10},{3,11},{4,12},{5,13},{6,14},{7,15},{8,0},{9,1},... | collective-permute-start | bytes 3932168 | tf_op jit(solution)/shard_map/s2h8/ppermute | solution.py:476
  106.6 4.1 %collective-permute-start.27 = (bf16[1024,512]{1,0:T(8,128)(2,1)S(1)}, bf16[1024,512]{1,0:T(8,128)(2,1)S(1)}, u32[]{:S(2)}, u32[]{:S(2)}) collective-permute-start(bf16[1024,512]{1,0:T(8,128)(2,1)S(1)} %pad_maximum_fusion.1.refs_0_), channel_id=1, source_target_pairs={{0,8},{1,9},{2,10},{3,11},{4,12},{5,13},{6,14},{7,15},{8,0},{9,1},... | collective-permute-start | bytes 3145736 | tf_op jit(solution)/shard_map/s1h8/ppermute | solution.py:476
  108.2 2.5 %collective-permute-start.30 = (bf16[260,1536]{1,0:T(8,128)(2,1)S(1)}, bf16[260,1536]{1,0:T(8,128)(2,1)S(1)}, u32[]{:S(2)}, u32[]{:S(2)}) collective-permute-start(bf16[260,1536]{1,0:T(8,128)(2,1)S(1)} %fusion.refs_0_.refs_3_), channel_id=1, source_target_pairs={{0,8},{1,9},{2,10},{3,11},{4,12},{5,13},{6,14},{7,15},{8,0},{9,1},... | collective-permute-start | bytes 2396168 | tf_op jit(solution)/shard_map/s3h8/ppermute | solution.py:476

commit v5 on v4

--- a/solution.py
+++ b/solution.py
@@ -183,8 +183,8 @@
     branch = jnp.zeros((rows, width), f32)
     dc = jnp.zeros((rows, width), f32)
     b1_row = as_row(b1)
-    for part in range(hidden // width):
-        cols = slice(part * width, (part + 1) * width)
+    for start in range(0, hidden, 1024):
+        cols = slice(start, start + 1024)
         u = dot_nn(c_low, w1[:, cols]) + b1_row[:, cols]
         cdf = 0.5 + 0.5 * lax.erf(u * SQRT_HALF)
         slope = cdf + u * (jnp.exp(u * u * -0.5) * PHI_SCALE)
@@ -194,7 +194,10 @@
         dh = dot_nt(cot_low, w2[cols, :])
         du_low = (dh * slope).astype(bf16)
         du_ref[:, cols] = du_low
-        small_out[4 + part : 5 + part, :] = jnp.sum(du_low.astype(f32), axis=0, keepdims=True)
+        sums = jnp.sum(du_low.astype(f32), axis=0, keepdims=True)
+        for row in range(sums.shape[1] // width):
+            place = 4 + start // width + row
+            small_out[place : place + 1, :] = sums[:, row * width : (row + 1) * width]
         dc = dc + dot_nt(du_low, w1[:, cols])
     mixed_out[...] = (x1 + branch + as_row(b2)).astype(bf16)
     cot_wide = cot_low.astype(f32)

time: 114 us -> 114 us (level)
  no operation moved by 1% of the time
where the time goes in v5:
time: 114 us; the launch traced here: 113 us
  starting transfers between devices  45.9 us (40%)
  waiting for transfers between devices  36.5 us (32%)
  Pallas kernels  24.7 us (22%)
  other arithmetic  3.83 us (3%)
  local copies, waits for them, and re-layouts  1.41 us (1%)
    ppermute x29, starting transfers between devices, exchange(): return lax.ppermute(value, ('lat', 'items'), pairs)  44.4 us
    ppermute x29, waiting for transfers between devices, exchange(): return lax.ppermute(value, ('lat', 'items'), pairs)  36.5 us
    pallas_call x2, Pallas kernels, on_device(): pl.pallas_call(kernel, out_shape=[jax.ShapeDtypeStruct(shape, dtype) for...  17.2 us
    pallas_call x4, Pallas kernels, spread(): pl.pallas_call(functools.partial(spread_kernel, axes, shards, streams, bo...  7.51 us
  transfers between devices with their start and end apart: 31, of which 14 were waited for; matrix products, arithmetic and copies ran while one was open for 3% of the time, Pallas kernels for 7%

profile of v5, /device:TPU:0, one launch (start us, length us, event | category | flops | bytes accessed | tf_op | source)
XLA Modules:
  0.0 113.5 jit_solution(11707595229275687937)
XLA Ops:
  0.7 1.0 broadcast_select_fusion
  1.6 0.5 collective-permute-start
  2.1 0.7 collective-permute-start.1
  3.1 0.6 copy-done.6
  3.8 13.4 %shard_map.245 = (bf16[192,512]{1,0:T(8,128)(2,1)}, bf16[192,512]{1,0:T(8,128)(2,1)}, f32[192,512]{1,0:T(8,128)}, f32[8,512]{1,0:T(8,128)}, bf16[1024,512]{1,0:T...) custom-call(bf16[192,512]{1,0:T(8,128)(2,1)} %bitcast.6, ...), custom_call_target="tpu_custom_call" | custom-call | flops 2818572288 | bytes 13791232 | tf_op jit(solution)/shard_map/pallas_call | solution.py:420
  17.2 5.9 %collective-permute-start.2 = (bf16[256,2560]{1,0:T(8,128)(2,1)}, bf16[256,2560]{1,0:T(8,128)(2,1)S(1)}, u32[]{:S(2)}, u32[]{:S(2)}) collective-permute-start(bf16[256,2560]{1,0:T(8,128)(2,1)} %get-tuple-element.73), channel_id=1, source_target_pairs={{0,8},{1,9},{2,10},{3,11},{4,12},{5,13},{6,14},{7,15},{8,0},{9,1},... | collective-permute-start | bytes 3932168 | tf_op jit(solution)/shard_map/s2h0/ppermute | solution.py:479
  23.2 0.8 collective-permute-start.4
  24.0 3.5 %collective-permute-start.5 = (bf16[1024,512]{1,0:T(8,128)(2,1)}, bf16[1024,512]{1,0:T(8,128)(2,1)S(1)}, u32[]{:S(2)}, u32[]{:S(2)}) collective-permute-start(bf16[1024,512]{1,0:T(8,128)(2,1)} %get-tuple-element.85), channel_id=1, source_target_pairs={{0,8},{1,9},{2,10},{3,11},{4,12},{5,13},{6,14},{7,15},{8,0},{9,1},... | collective-permute-start | bytes 3145736 | tf_op jit(solution)/shard_map/s1h0/ppermute | solution.py:479
  27.5 1.3 %add_convert_fusion = bf16[128,2560]{1,0:T(8,128)(2,1)S(1)} fusion(bf16[256,2560]{1,0:T(8,128)(2,1)S(1)} %collective-permute-done.2, bf16[256,2560]{1,0:T(8,128)(2,1)} %get-tuple-element.72), kind=kLoop, calls=%fused_computation.1 | loop fusion | flops 1310720 | bytes 1966080 | tf_op jit(solution)/shard_map/convert_element_type | solution.py:520
  28.9 0.7 copy-done.4
  29.5 3.8 %shard_map.246 = (bf16[256,1536]{1,0:T(8,128)(2,1)}, bf16[256,1536]{1,0:T(8,128)(2,1)}, bf16[192,512]{1,0:T(8,128)(2,1)}, bf16[4,1536]{1,0:T(4,128)(2,1)}) custom-call(bf16[192,512]{1,0:T(8,128)(2,1)} %get-tuple-element.76.refs_0_, f32[192,512]{1,0:T(8,128)} %get-tuple-element.77.refs_1_, f32[192,512]{1,0:T(8,128)} %get-tuple-element.78.refs_2_, ...), custom_call_target="tpu_custom_call" | custom-call | flops 603979776 | bytes 5534720 | tf_op jit(solution)/shard_map/pallas_call | solution.py:420
  33.3 2.0 %collective-permute-start.8 = (bf16[256,1536]{1,0:T(8,128)(2,1)}, bf16[256,1536]{1,0:T(8,128)(2,1)S(1)}, u32[]{:S(2)}, u32[]{:S(2)}) collective-permute-start(bf16[256,1536]{1,0:T(8,128)(2,1)} %get-tuple-element.86), channel_id=1, source_target_pairs={{0,8},{1,9},{2,10},{3,11},{4,12},{5,13},{6,14},{7,15},{8,0},{9,1},... | collective-permute-start | bytes 2359304 | tf_op jit(solution)/shard_map/s3h0/ppermute | solution.py:479
  35.3 2.1 %collective-permute-start.7 = (bf16[128,2560]{1,0:T(8,128)(2,1)S(1)}, bf16[128,2560]{1,0:T(8,128)(2,1)S(1)}, u32[]{:S(2)}, u32[]{:S(2)}) collective-permute-start(bf16[128,2560]{1,0:T(8,128)(2,1)S(1)} %add_convert_fusion), channel_id=1, source_target_pairs={{0,1},{1,0},{2,3},{3,2},{4,5},{5,4},{6,7},{7,6},{8,10},{9,11},{10,... | collective-permute-start | bytes 1966088 | tf_op jit(solution)/shard_map/s2h1/ppermute | solution.py:479
  37.6 1.6 %collective-permute-start.6 = (bf16[512,512]{1,0:T(8,128)(2,1)S(1)}, bf16[512,512]{1,0:T(8,128)(2,1)S(1)}, u32[]{:S(2)}, u32[]{:S(2)}) collective-permute-start(bf16[512,512]{1,0:T(8,128)(2,1)S(1)} %add_convert_fusion.1), channel_id=1, source_target_pairs={{0,2},{1,3},{2,0},{3,1},{4,6},{5,7},{6,4},{7,5},{8,24},{9,25},{10,... | collective-permute-start | bytes 1572872 | tf_op jit(solution)/shard_map/s1h1/ppermute | solution.py:479
  39.4 0.6 collective-permute-start.11
  40.0 6.0 %collective-permute-done.7 = bf16[128,2560]{1,0:T(8,128)(2,1)S(1)} collective-permute-done((bf16[128,2560]{1,0:T(8,128)(2,1)S(1)}, bf16[128,2560]{1,0:T(8,128)(2,1)S(1)}, u32[]{:S(2)}, u32[]{:S(2)}) %collective-permute-start.7) | collective-permute-done | bytes 655392 | tf_op jit(solution)/shard_map/s2h1/ppermute | solution.py:479
  46.1 2.1 %collective-permute-start.10 = (bf16[64,2560]{1,0:T(8,128)(2,1)S(1)}, bf16[64,2560]{1,0:T(8,128)(2,1)S(1)}, u32[]{:S(2)}, u32[]{:S(2)}) collective-permute-start(bf16[64,2560]{1,0:T(8,128)(2,1)S(1)} %add_convert_fusion.3), channel_id=1, source_target_pairs={{0,2},{1,3},{2,0},{3,1},{4,6},{5,7},{6,4},{7,5},{8,9},{9,8},{10,11... | collective-permute-start | bytes 983048 | tf_op jit(solution)/shard_map/s2h2/ppermute | solution.py:479
  48.3 2.8 %collective-permute-done.6 = bf16[512,512]{1,0:T(8,128)(2,1)S(1)} collective-permute-done((bf16[512,512]{1,0:T(8,128)(2,1)S(1)}, bf16[512,512]{1,0:T(8,128)(2,1)S(1)}, u32[]{:S(2)}, u32[]{:S(2)}) %collective-permute-start.6) | collective-permute-done | bytes 524320 | tf_op jit(solution)/shard_map/s1h1/ppermute | solution.py:479
  51.2 1.7 %collective-permute-start.9 = (bf16[256,512]{1,0:T(8,128)(2,1)S(1)}, bf16[256,512]{1,0:T(8,128)(2,1)S(1)}, u32[]{:S(2)}, u32[]{:S(2)}) collective-permute-start(bf16[256,512]{1,0:T(8,128)(2,1)S(1)} %add_convert_fusion.4), channel_id=1, source_target_pairs={{0,16},{1,17},{2,18},{3,19},{4,20},{5,21},{6,22},{7,23},{8,9},{9,8... | collective-permute-start | bytes 786440 | tf_op jit(solution)/shard_map/s1h2/ppermute | solution.py:479
  53.0 0.5 collective-permute-start.14
  53.5 1.1 collective-permute-done.10
  54.7 1.7 %collective-permute-start.13 = (bf16[32,2560]{1,0:T(8,128)(2,1)S(1)}, bf16[32,2560]{1,0:T(8,128)(2,1)S(1)}, u32[]{:S(2)}, u32[]{:S(2)}) collective-permute-start(bf16[32,2560]{1,0:T(8,128)(2,1)S(1)} %add_convert_fusion.8), channel_id=1, source_target_pairs={{0,16},{1,17},{2,18},{3,19},{4,20},{5,21},{6,22},{7,23},{8,12},{9,... | collective-permute-start | bytes 491528 | tf_op jit(solution)/shard_map/s2h3/ppermute | solution.py:479
  56.4 1.3 %collective-permute-done.9 = bf16[256,512]{1,0:T(8,128)(2,1)S(1)} collective-permute-done((bf16[256,512]{1,0:T(8,128)(2,1)S(1)}, bf16[256,512]{1,0:T(8,128)(2,1)S(1)}, u32[]{:S(2)}, u32[]{:S(2)}) %collective-permute-start.9) | collective-permute-done | bytes 262176 | tf_op jit(solution)/shard_map/s1h2/ppermute | solution.py:479
  57.7 1.5 %collective-permute-start.12 = (bf16[128,512]{1,0:T(8,128)(2,1)S(1)}, bf16[128,512]{1,0:T(8,128)(2,1)S(1)}, u32[]{:S(2)}, u32[]{:S(2)}) collective-permute-start(bf16[128,512]{1,0:T(8,128)(2,1)S(1)} %add_convert_fusion.11), channel_id=1, source_target_pairs={{0,1},{1,0},{2,3},{3,2},{4,5},{5,4},{6,7},{7,6},{8,10},{9,11},{10,... | collective-permute-start | bytes 393224 | tf_op jit(solution)/shard_map/s1h3/ppermute | solution.py:479
  59.2 0.8 collective-permute-done.14
  60.1 1.8 %collective-permute-start.17 = (bf16[36,1536]{1,0:T(8,128)(2,1)S(1)}, bf16[36,1536]{1,0:T(8,128)(2,1)S(1)}, u32[]{:S(2)}, u32[]{:S(2)}) collective-permute-start(bf16[36,1536]{1,0:T(8,128)(2,1)S(1)} %pad_maximum_fusion.10), channel_id=1, source_target_pairs={{0,2},{1,3},{2,0},{3,1},{4,6},{5,7},{6,4},{7,5},{8,10},{9,11},{10,... | collective-permute-start | bytes 331784 | tf_op jit(solution)/shard_map/s3h3/ppermute | solution.py:479
  62.0 2.7 %collective-permute-start.16 = (bf16[32,2560]{1,0:T(8,128)(2,1)S(1)}, bf16[32,2560]{1,0:T(8,128)(2,1)S(1)}, u32[]{:S(2)}, u32[]{:S(2)}) collective-permute-start(bf16[32,2560]{1,0:T(8,128)(2,1)S(1)} %add_convert_fusion.7), channel_id=1, source_target_pairs={{0,4},{1,5},{2,6},{3,7},{4,0},{5,1},{6,2},{7,3},{8,24},{9,25},{10,... | collective-permute-start | bytes 491528 | tf_op jit(solution)/shard_map/s2h4/ppermute | solution.py:479
  64.8 1.7 %collective-permute-start.15 = (bf16[128,512]{1,0:T(8,128)(2,1)S(1)}, bf16[128,512]{1,0:T(8,128)(2,1)S(1)}, u32[]{:S(2)}, u32[]{:S(2)}) collective-permute-start(bf16[128,512]{1,0:T(8,128)(2,1)S(1)} %add_convert_fusion.10), channel_id=1, source_target_pairs={{0,4},{1,5},{2,6},{3,7},{4,0},{5,1},{6,2},{7,3},{8,12},{9,13},{10,... | collective-permute-start | bytes 393224 | tf_op jit(solution)/shard_map/s1h4/ppermute | solution.py:479
  66.5 2.3 %collective-permute-done.17 = bf16[36,1536]{1,0:T(8,128)(2,1)S(1)} collective-permute-done((bf16[36,1536]{1,0:T(8,128)(2,1)S(1)}, bf16[36,1536]{1,0:T(8,128)(2,1)S(1)}, u32[]{:S(2)}, u32[]{:S(2)}) %collective-permute-start.17) | collective-permute-done | bytes 110624 | tf_op jit(solution)/shard_map/s3h3/ppermute | solution.py:479
  69.5 1.6 %collective-permute-start.20 = (bf16[32,2560]{1,0:T(8,128)(2,1)S(1)}, bf16[32,2560]{1,0:T(8,128)(2,1)S(1)}, u32[]{:S(2)}, u32[]{:S(2)}) collective-permute-start(bf16[32,2560]{1,0:T(8,128)(2,1)S(1)} %add_convert_fusion.6), channel_id=1, source_target_pairs={{0,16},{1,17},{2,18},{3,19},{4,20},{5,21},{6,22},{7,23},{8,12},{9,... | collective-permute-start | bytes 491528 | tf_op jit(solution)/shard_map/s2h5/ppermute | solution.py:479
  71.2 8.3 %collective-permute-done.15 = bf16[128,512]{1,0:T(8,128)(2,1)S(1)} collective-permute-done((bf16[128,512]{1,0:T(8,128)(2,1)S(1)}, bf16[128,512]{1,0:T(8,128)(2,1)S(1)}, u32[]{:S(2)}, u32[]{:S(2)}) %collective-permute-start.15) | collective-permute-done | bytes 131104 | tf_op jit(solution)/shard_map/s1h4/ppermute | solution.py:479
  79.5 1.3 %collective-permute-start.18 = (bf16[128,512]{1,0:T(8,128)(2,1)S(1)}, bf16[128,512]{1,0:T(8,128)(2,1)S(1)}, u32[]{:S(2)}, u32[]{:S(2)}) collective-permute-start(bf16[128,512]{1,0:T(8,128)(2,1)S(1)} %add_convert_fusion.9), channel_id=1, source_target_pairs={{0,1},{1,0},{2,3},{3,2},{4,5},{5,4},{6,7},{7,6},{8,10},{9,11},{10,... | collective-permute-start | bytes 393224 | tf_op jit(solution)/shard_map/s1h5/ppermute | solution.py:479
  80.9 3.6 %collective-permute-start.23 = (bf16[64,2560]{1,0:T(8,128)(2,1)S(1)}, bf16[64,2560]{1,0:T(8,128)(2,1)S(1)}, u32[]{:S(2)}, u32[]{:S(2)}) collective-permute-start(bf16[64,2560]{1,0:T(8,128)(2,1)S(1)} %pad_maximum_fusion.6), channel_id=1, source_target_pairs={{0,2},{1,3},{2,0},{3,1},{4,6},{5,7},{6,4},{7,5},{8,9},{9,8},{10,11... | collective-permute-start | bytes 983048 | tf_op jit(solution)/shard_map/s2h6/ppermute | solution.py:479
  84.6 1.5 %collective-permute-start.21 = (bf16[256,512]{1,0:T(8,128)(2,1)S(1)}, bf16[256,512]{1,0:T(8,128)(2,1)S(1)}, u32[]{:S(2)}, u32[]{:S(2)}) collective-permute-start(bf16[256,512]{1,0:T(8,128)(2,1)S(1)} %pad_maximum_fusion.7), channel_id=1, source_target_pairs={{0,16},{1,17},{2,18},{3,19},{4,20},{5,21},{6,22},{7,23},{8,9},{9,8... | collective-permute-start | bytes 786440 | tf_op jit(solution)/shard_map/s1h6/ppermute | solution.py:479
  86.1 4.5 %collective-permute-done.23 = bf16[64,2560]{1,0:T(8,128)(2,1)S(1)} collective-permute-done((bf16[64,2560]{1,0:T(8,128)(2,1)S(1)}, bf16[64,2560]{1,0:T(8,128)(2,1)S(1)}, u32[]{:S(2)}, u32[]{:S(2)}) %collective-permute-start.23) | collective-permute-done | bytes 327712 | tf_op jit(solution)/shard_map/s2h6/ppermute | solution.py:479
  90.6 1.5 %collective-permute-start.25 = (bf16[128,2560]{1,0:T(8,128)(2,1)S(1)}, bf16[128,2560]{1,0:T(8,128)(2,1)S(1)}, u32[]{:S(2)}, u32[]{:S(2)}) collective-permute-start(bf16[128,2560]{1,0:T(8,128)(2,1)S(1)} %pad_maximum_fusion.2), channel_id=1, source_target_pairs={{0,1},{1,0},{2,3},{3,2},{4,5},{5,4},{6,7},{7,6},{8,10},{9,11},{10,... | collective-permute-start | bytes 1966088 | tf_op jit(solution)/shard_map/s2h7/ppermute | solution.py:479
  92.1 1.4 %collective-permute-start.26 = (bf16[64,1536]{1,0:T(8,128)(2,1)S(1)}, bf16[64,1536]{1,0:T(8,128)(2,1)S(1)}, u32[]{:S(2)}, u32[]{:S(2)}) collective-permute-start(bf16[64,1536]{1,0:T(8,128)(2,1)S(1)} %pad_maximum_fusion.9), channel_id=1, source_target_pairs={{0,16},{1,17},{2,18},{3,19},{4,20},{5,21},{6,22},{7,23},{8,9},{9,8... | collective-permute-start | bytes 589832 | tf_op jit(solution)/shard_map/s3h6/ppermute | solution.py:479
  93.6 1.4 %collective-permute-start.24 = (bf16[512,512]{1,0:T(8,128)(2,1)S(1)}, bf16[512,512]{1,0:T(8,128)(2,1)S(1)}, u32[]{:S(2)}, u32[]{:S(2)}) collective-permute-start(bf16[512,512]{1,0:T(8,128)(2,1)S(1)} %pad_maximum_fusion.3), channel_id=1, source_target_pairs={{0,2},{1,3},{2,0},{3,1},{4,6},{5,7},{6,4},{7,5},{8,24},{9,25},{10,... | collective-permute-start | bytes 1572872 | tf_op jit(solution)/shard_map/s1h7/ppermute | solution.py:479
  95.0 4.8 %collective-permute-done.26 = bf16[64,1536]{1,0:T(8,128)(2,1)S(1)} collective-permute-done((bf16[64,1536]{1,0:T(8,128)(2,1)S(1)}, bf16[64,1536]{1,0:T(8,128)(2,1)S(1)}, u32[]{:S(2)}, u32[]{:S(2)}) %collective-permute-start.26) | collective-permute-done | bytes 196640 | tf_op jit(solution)/shard_map/s3h6/ppermute | solution.py:479
  99.8 0.5 collective-permute-start.29
  100.3 3.0 %collective-permute-done.25 = bf16[128,2560]{1,0:T(8,128)(2,1)S(1)} collective-permute-done((bf16[128,2560]{1,0:T(8,128)(2,1)S(1)}, bf16[128,2560]{1,0:T(8,128)(2,1)S(1)}, u32[]{:S(2)}, u32[]{:S(2)}) %collective-permute-start.25) | collective-permute-done | bytes 655392 | tf_op jit(solution)/shard_map/s2h7/ppermute | solution.py:479
  103.4 0.5 collective-permute-start.28
  103.9 1.7 %shard_map.247 = (f32[512,2048]{1,0:T(8,128)}, f32[512,512]{1,0:T(8,128)}) custom-call(bf16[256,2560]{1,0:T(8,128)(2,1)S(1)} %pad_maximum_fusion.refs_0_), custom_call_target="tpu_custom_call" | custom-call | bytes 3932160 | tf_op jit(solution)/shard_map/pallas_call | solution.py:398
  106.2 1.5 %shard_map.248.refs_4_ = f32[2048,512]{1,0:T(8,128)} custom-call(bf16[1024,512]{1,0:T(8,128)(2,1)S(1)} %pad_maximum_fusion.1.refs_0_), custom_call_target="tpu_custom_call" | custom-call | bytes 3145728 | tf_op jit(solution)/shard_map/pallas_call | solution.py:398
  107.8 0.6 collective-permute-start.30
  108.3 1.3 %shard_map.249.refs_7_ = f32[512,1536]{1,0:T(8,128)} custom-call(bf16[260,1536]{1,0:T(8,128)(2,1)S(1)} %fusion.refs_0_.refs_3_), custom_call_target="tpu_custom_call" | custom-call | bytes 2359296 | tf_op jit(solution)/shard_map/pallas_call | solution.py:398
  109.6 0.6 collective-permute-done.30.refs_2_
  110.3 3.0 %shard_map.250 = (f32[2048,512]{1,0:T(8,128)}, f32[512,2048]{1,0:T(8,128)}, f32[512,512]{1,0:T(8,128)}, f32[512,1536]{1,0:T(8,128)}, f32[512]{0:T(512)}, /*index...) custom-call(bf16[1024,512]{1,0:T(8,128)(2,1)S(1)} %collective-permut, ...), custom_call_target="tpu_custom_call", output_to_operand_aliasing={{0}: (4, {}), {1}: (5, {}), {2}: (6, {}), {3}: (7, {})} | custom-call | bytes 9437184 | tf_op jit(solution)/shard_map/pallas_call | solution.py:398
  (71 shorter events, 3.2 us)
Async XLA Ops:
  1.6 1.5 %collective-permute-start = (bf16[96,512]{1,0:T(8,128)(2,1)S(1)}, bf16[96,512]{1,0:T(8,128)(2,1)S(1)}, u32[]{:S(2)}, u32[]{:S(2)}) collective-permute-start(bf16[96,512]{1,0:T(8,128)(2,1)S(1)} %bitcast.9), channel_id=1, source_target_pairs={{0,8},{1,9},{2,10},{3,11},{4,12},{5,13},{6,14},{7,15},{8,0},{9,1},... | collective-permute-start | bytes 294920 | tf_op jit(solution)/shard_map/ppermute | solution.py:479
  2.1 0.9 collective-permute-start.1
  3.1 0.6 copy-start.6
  3.1 0.7 copy-start.7
  17.2 10.3 %collective-permute-start.2 = (bf16[256,2560]{1,0:T(8,128)(2,1)}, bf16[256,2560]{1,0:T(8,128)(2,1)S(1)}, u32[]{:S(2)}, u32[]{:S(2)}) collective-permute-start(bf16[256,2560]{1,0:T(8,128)(2,1)} %get-tuple-element.73), channel_id=1, source_target_pairs={{0,8},{1,9},{2,10},{3,11},{4,12},{5,13},{6,14},{7,15},{8,0},{9,1},... | collective-permute-start | bytes 3932168 | tf_op jit(solution)/shard_map/s2h0/ppermute | solution.py:479
  23.1 4.4 %collective-permute-start.3 = (bf16[2,96,512]{2,1,0:T(8,128)(2,1)}, bf16[2,96,512]{2,1,0:T(8,128)(2,1)S(1)}, u32[]{:S(2)}, u32[]{:S(2)}) collective-permute-start(bf16[2,96,512]{2,1,0:T(8,128)(2,1)} %get-tuple-element.74), channel_id=1, source_target_pairs={{0,8},{1,9},{2,10},{3,11},{4,12},{5,13},{6,14},{7,15},{8,0},{9,1},... | collective-permute-start | bytes 589832 | tf_op jit(solution)/shard_map/ppermute | solution.py:479
  23.2 5.7 %collective-permute-start.4 = (bf16[2,96,512]{2,1,0:T(8,128)(2,1)}, bf16[2,96,512]{2,1,0:T(8,128)(2,1)S(1)}, u32[]{:S(2)}, u32[]{:S(2)}) collective-permute-start(bf16[2,96,512]{2,1,0:T(8,128)(2,1)} %get-tuple-element.79), channel_id=1, source_target_pairs={{8,16},{16,8},{9,17},{17,9},{10,18},{18,10},{11,19},{19,11},{12,20... | collective-permute-start | bytes 589832 | tf_op jit(solution)/shard_map/ppermute | solution.py:471
  24.0 13.4 %collective-permute-start.5 = (bf16[1024,512]{1,0:T(8,128)(2,1)}, bf16[1024,512]{1,0:T(8,128)(2,1)S(1)}, u32[]{:S(2)}, u32[]{:S(2)}) collective-permute-start(bf16[1024,512]{1,0:T(8,128)(2,1)} %get-tuple-element.85), channel_id=1, source_target_pairs={{0,8},{1,9},{2,10},{3,11},{4,12},{5,13},{6,14},{7,15},{8,0},{9,1},... | collective-permute-start | bytes 3145736 | tf_op jit(solution)/shard_map/s1h0/ppermute | solution.py:479
  27.5 1.3 %copy-start.3 = (bf16[2,96,512]{2,1,0:T(8,128)(2,1)}, bf16[2,96,512]{2,1,0:T(8,128)(2,1)S(1)}, u32[]{:S(2)}) copy-start(bf16[2,96,512]{2,1,0:T(8,128)(2,1)S(1)} %collective-permute-done.3.refs_3_) | copy-start | bytes 589828
  28.8 0.7 copy-start.4
  29.5 7.9 %copy-start.1 = (bf16[1024,512]{1,0:T(8,128)(2,1)S(1)}, bf16[1024,512]{1,0:T(8,128)(2,1)}, u32[]{:S(2)}) copy-start(bf16[1024,512]{1,0:T(8,128)(2,1)} %get-tuple-element.84) | copy-start | bytes 3145732
  33.3 6.0 %copy-start.2 = (bf16[256,1536]{1,0:T(8,128)(2,1)S(1)}, bf16[256,1536]{1,0:T(8,128)(2,1)}, u32[]{:S(2)}) copy-start(bf16[256,1536]{1,0:T(8,128)(2,1)} %get-tuple-element.88) | copy-start | bytes 2359300
  33.3 5.9 %collective-permute-start.8 = (bf16[256,1536]{1,0:T(8,128)(2,1)}, bf16[256,1536]{1,0:T(8,128)(2,1)S(1)}, u32[]{:S(2)}, u32[]{:S(2)}) collective-permute-start(bf16[256,1536]{1,0:T(8,128)(2,1)} %get-tuple-element.86), channel_id=1, source_target_pairs={{0,8},{1,9},{2,10},{3,11},{4,12},{5,13},{6,14},{7,15},{8,0},{9,1},... | collective-permute-start | bytes 2359304 | tf_op jit(solution)/shard_map/s3h0/ppermute | solution.py:479
  35.3 10.7 %collective-permute-start.7 = (bf16[128,2560]{1,0:T(8,128)(2,1)S(1)}, bf16[128,2560]{1,0:T(8,128)(2,1)S(1)}, u32[]{:S(2)}, u32[]{:S(2)}) collective-permute-start(bf16[128,2560]{1,0:T(8,128)(2,1)S(1)} %add_convert_fusion), channel_id=1, source_target_pairs={{0,1},{1,0},{2,3},{3,2},{4,5},{5,4},{6,7},{7,6},{8,10},{9,11},{10,... | collective-permute-start | bytes 1966088 | tf_op jit(solution)/shard_map/s2h1/ppermute | solution.py:479
  37.5 1.9 %copy-start.5 = (bf16[4,1536]{1,0:T(4,128)(2,1)S(1)}, bf16[4,1536]{1,0:T(4,128)(2,1)}, u32[]{:S(2)}) copy-start(bf16[4,1536]{1,0:T(4,128)(2,1)} %get-tuple-element.90) | copy-start | bytes 36868
  37.6 8.4 %copy-start = (bf16[256,2560]{1,0:T(8,128)(2,1)S(1)}, bf16[256,2560]{1,0:T(8,128)(2,1)}, u32[]{:S(2)}) copy-start(bf16[256,2560]{1,0:T(8,128)(2,1)} %get-tuple-element.72) | copy-start | bytes 3932164
  37.6 13.5 %collective-permute-start.6 = (bf16[512,512]{1,0:T(8,128)(2,1)S(1)}, bf16[512,512]{1,0:T(8,128)(2,1)S(1)}, u32[]{:S(2)}, u32[]{:S(2)}) collective-permute-start(bf16[512,512]{1,0:T(8,128)(2,1)S(1)} %add_convert_fusion.1), channel_id=1, source_target_pairs={{0,2},{1,3},{2,0},{3,1},{4,6},{5,7},{6,4},{7,5},{8,24},{9,25},{10,... | collective-permute-start | bytes 1572872 | tf_op jit(solution)/shard_map/s1h1/ppermute | solution.py:479
  39.4 13.5 %collective-permute-start.11 = (bf16[132,1536]{1,0:T(8,128)(2,1)S(1)}, bf16[132,1536]{1,0:T(8,128)(2,1)S(1)}, u32[]{:S(2)}, u32[]{:S(2)}) collective-permute-start(bf16[132,1536]{1,0:T(8,128)(2,1)S(1)} %pad_maximum_fusion.4), channel_id=1, source_target_pairs={{0,1},{1,0},{2,3},{3,2},{4,5},{5,4},{6,7},{7,6},{8,24},{9,25},{10,... | collective-permute-start | bytes 1216520 | tf_op jit(solution)/shard_map/s3h1/ppermute | solution.py:479
  46.1 8.5 %collective-permute-start.10 = (bf16[64,2560]{1,0:T(8,128)(2,1)S(1)}, bf16[64,2560]{1,0:T(8,128)(2,1)S(1)}, u32[]{:S(2)}, u32[]{:S(2)}) collective-permute-start(bf16[64,2560]{1,0:T(8,128)(2,1)S(1)} %add_convert_fusion.3), channel_id=1, source_target_pairs={{0,2},{1,3},{2,0},{3,1},{4,6},{5,7},{6,4},{7,5},{8,9},{9,8},{10,11... | collective-permute-start | bytes 983048 | tf_op jit(solution)/shard_map/s2h2/ppermute | solution.py:479
  51.2 6.4 %collective-permute-start.9 = (bf16[256,512]{1,0:T(8,128)(2,1)S(1)}, bf16[256,512]{1,0:T(8,128)(2,1)S(1)}, u32[]{:S(2)}, u32[]{:S(2)}) collective-permute-start(bf16[256,512]{1,0:T(8,128)(2,1)S(1)} %add_convert_fusion.4), channel_id=1, source_target_pairs={{0,16},{1,17},{2,18},{3,19},{4,20},{5,21},{6,22},{7,23},{8,9},{9,8... | collective-permute-start | bytes 786440 | tf_op jit(solution)/shard_map/s1h2/ppermute | solution.py:479
  53.0 7.0 %collective-permute-start.14 = (bf16[68,1536]{1,0:T(8,128)(2,1)S(1)}, bf16[68,1536]{1,0:T(8,128)(2,1)S(1)}, u32[]{:S(2)}, u32[]{:S(2)}) collective-permute-start(bf16[68,1536]{1,0:T(8,128)(2,1)S(1)} %pad_maximum_fusion.8), channel_id=1, source_target_pairs={{0,16},{1,17},{2,18},{3,19},{4,20},{5,21},{6,22},{7,23},{8,9},{9,8... | collective-permute-start | bytes 626696 | tf_op jit(solution)/shard_map/s3h2/ppermute | solution.py:479
  54.7 7.2 %collective-permute-start.13 = (bf16[32,2560]{1,0:T(8,128)(2,1)S(1)}, bf16[32,2560]{1,0:T(8,128)(2,1)S(1)}, u32[]{:S(2)}, u32[]{:S(2)}) collective-permute-start(bf16[32,2560]{1,0:T(8,128)(2,1)S(1)} %add_convert_fusion.8), channel_id=1, source_target_pairs={{0,16},{1,17},{2,18},{3,19},{4,20},{5,21},{6,22},{7,23},{8,12},{9,... | collective-permute-start | bytes 491528 | tf_op jit(solution)/shard_map/s2h3/ppermute | solution.py:479
  57.7 7.0 %collective-permute-start.12 = (bf16[128,512]{1,0:T(8,128)(2,1)S(1)}, bf16[128,512]{1,0:T(8,128)(2,1)S(1)}, u32[]{:S(2)}, u32[]{:S(2)}) collective-permute-start(bf16[128,512]{1,0:T(8,128)(2,1)S(1)} %add_convert_fusion.11), channel_id=1, source_target_pairs={{0,1},{1,0},{2,3},{3,2},{4,5},{5,4},{6,7},{7,6},{8,10},{9,11},{10,... | collective-permute-start | bytes 393224 | tf_op jit(solution)/shard_map/s1h3/ppermute | solution.py:479
  60.1 8.7 %collective-permute-start.17 = (bf16[36,1536]{1,0:T(8,128)(2,1)S(1)}, bf16[36,1536]{1,0:T(8,128)(2,1)S(1)}, u32[]{:S(2)}, u32[]{:S(2)}) collective-permute-start(bf16[36,1536]{1,0:T(8,128)(2,1)S(1)} %pad_maximum_fusion.10), channel_id=1, source_target_pairs={{0,2},{1,3},{2,0},{3,1},{4,6},{5,7},{6,4},{7,5},{8,10},{9,11},{10,... | collective-permute-start | bytes 331784 | tf_op jit(solution)/shard_map/s3h3/ppermute | solution.py:479
  62.0 7.5 %collective-permute-start.16 = (bf16[32,2560]{1,0:T(8,128)(2,1)S(1)}, bf16[32,2560]{1,0:T(8,128)(2,1)S(1)}, u32[]{:S(2)}, u32[]{:S(2)}) collective-permute-start(bf16[32,2560]{1,0:T(8,128)(2,1)S(1)} %add_convert_fusion.7), channel_id=1, source_target_pairs={{0,4},{1,5},{2,6},{3,7},{4,0},{5,1},{6,2},{7,3},{8,24},{9,25},{10,... | collective-permute-start | bytes 491528 | tf_op jit(solution)/shard_map/s2h4/ppermute | solution.py:479
  64.8 14.7 %collective-permute-start.15 = (bf16[128,512]{1,0:T(8,128)(2,1)S(1)}, bf16[128,512]{1,0:T(8,128)(2,1)S(1)}, u32[]{:S(2)}, u32[]{:S(2)}) collective-permute-start(bf16[128,512]{1,0:T(8,128)(2,1)S(1)} %add_convert_fusion.10), channel_id=1, source_target_pairs={{0,4},{1,5},{2,6},{3,7},{4,0},{5,1},{6,2},{7,3},{8,12},{9,13},{10,... | collective-permute-start | bytes 393224 | tf_op jit(solution)/shard_map/s1h4/ppermute | solution.py:479
  68.9 15.5 %collective-permute-start.19 = (bf16[36,1536]{1,0:T(8,128)(2,1)S(1)}, bf16[36,1536]{1,0:T(8,128)(2,1)S(1)}, u32[]{:S(2)}, u32[]{:S(2)}) collective-permute-start(bf16[36,1536]{1,0:T(8,128)(2,1)S(1)} %pad_maximum_fusion.11), channel_id=1, source_target_pairs={{0,4},{1,5},{2,6},{3,7},{4,0},{5,1},{6,2},{7,3},{8,12},{9,13},{10,... | collective-permute-start | bytes 331784 | tf_op jit(solution)/shard_map/s3h4/ppermute | solution.py:479
  69.5 11.3 %collective-permute-start.20 = (bf16[32,2560]{1,0:T(8,128)(2,1)S(1)}, bf16[32,2560]{1,0:T(8,128)(2,1)S(1)}, u32[]{:S(2)}, u32[]{:S(2)}) collective-permute-start(bf16[32,2560]{1,0:T(8,128)(2,1)S(1)} %add_convert_fusion.6), channel_id=1, source_target_pairs={{0,16},{1,17},{2,18},{3,19},{4,20},{5,21},{6,22},{7,23},{8,12},{9,... | collective-permute-start | bytes 491528 | tf_op jit(solution)/shard_map/s2h5/ppermute | solution.py:479
  79.5 5.1 %collective-permute-start.18 = (bf16[128,512]{1,0:T(8,128)(2,1)S(1)}, bf16[128,512]{1,0:T(8,128)(2,1)S(1)}, u32[]{:S(2)}, u32[]{:S(2)}) collective-permute-start(bf16[128,512]{1,0:T(8,128)(2,1)S(1)} %add_convert_fusion.9), channel_id=1, source_target_pairs={{0,1},{1,0},{2,3},{3,2},{4,5},{5,4},{6,7},{7,6},{8,10},{9,11},{10,... | collective-permute-start | bytes 393224 | tf_op jit(solution)/shard_map/s1h5/ppermute | solution.py:479
  80.9 9.7 %collective-permute-start.23 = (bf16[64,2560]{1,0:T(8,128)(2,1)S(1)}, bf16[64,2560]{1,0:T(8,128)(2,1)S(1)}, u32[]{:S(2)}, u32[]{:S(2)}) collective-permute-start(bf16[64,2560]{1,0:T(8,128)(2,1)S(1)} %pad_maximum_fusion.6), channel_id=1, source_target_pairs={{0,2},{1,3},{2,0},{3,1},{4,6},{5,7},{6,4},{7,5},{8,9},{9,8},{10,11... | collective-permute-start | bytes 983048 | tf_op jit(solution)/shard_map/s2h6/ppermute | solution.py:479
  84.5 7.6 %collective-permute-start.22 = (bf16[32,1536]{1,0:T(8,128)(2,1)S(1)}, bf16[32,1536]{1,0:T(8,128)(2,1)S(1)}, u32[]{:S(2)}, u32[]{:S(2)}) collective-permute-start(bf16[32,1536]{1,0:T(8,128)(2,1)S(1)} %get-tuple-element.127), channel_id=1, source_target_pairs={{0,2},{1,3},{2,0},{3,1},{4,6},{5,7},{6,4},{7,5},{8,10},{9,11},{10,... | collective-permute-start | bytes 294920 | tf_op jit(solution)/shard_map/s3h5/ppermute | solution.py:479
  84.6 8.9 %collective-permute-start.21 = (bf16[256,512]{1,0:T(8,128)(2,1)S(1)}, bf16[256,512]{1,0:T(8,128)(2,1)S(1)}, u32[]{:S(2)}, u32[]{:S(2)}) collective-permute-start(bf16[256,512]{1,0:T(8,128)(2,1)S(1)} %pad_maximum_fusion.7), channel_id=1, source_target_pairs={{0,16},{1,17},{2,18},{3,19},{4,20},{5,21},{6,22},{7,23},{8,9},{9,8... | collective-permute-start | bytes 786440 | tf_op jit(solution)/shard_map/s1h6/ppermute | solution.py:479
  90.6 12.7 %collective-permute-start.25 = (bf16[128,2560]{1,0:T(8,128)(2,1)S(1)}, bf16[128,2560]{1,0:T(8,128)(2,1)S(1)}, u32[]{:S(2)}, u32[]{:S(2)}) collective-permute-start(bf16[128,2560]{1,0:T(8,128)(2,1)S(1)} %pad_maximum_fusion.2), channel_id=1, source_target_pairs={{0,1},{1,0},{2,3},{3,2},{4,5},{5,4},{6,7},{7,6},{8,10},{9,11},{10,... | collective-permute-start | bytes 1966088 | tf_op jit(solution)/shard_map/s2h7/ppermute | solution.py:479
  92.1 7.6 %collective-permute-start.26 = (bf16[64,1536]{1,0:T(8,128)(2,1)S(1)}, bf16[64,1536]{1,0:T(8,128)(2,1)S(1)}, u32[]{:S(2)}, u32[]{:S(2)}) collective-permute-start(bf16[64,1536]{1,0:T(8,128)(2,1)S(1)} %pad_maximum_fusion.9), channel_id=1, source_target_pairs={{0,16},{1,17},{2,18},{3,19},{4,20},{5,21},{6,22},{7,23},{8,9},{9,8... | collective-permute-start | bytes 589832 | tf_op jit(solution)/shard_map/s3h6/ppermute | solution.py:479
  93.6 12.5 %collective-permute-start.24 = (bf16[512,512]{1,0:T(8,128)(2,1)S(1)}, bf16[512,512]{1,0:T(8,128)(2,1)S(1)}, u32[]{:S(2)}, u32[]{:S(2)}) collective-permute-start(bf16[512,512]{1,0:T(8,128)(2,1)S(1)} %pad_maximum_fusion.3), channel_id=1, source_target_pairs={{0,2},{1,3},{2,0},{3,1},{4,6},{5,7},{6,4},{7,5},{8,24},{9,25},{10,... | collective-permute-start | bytes 1572872 | tf_op jit(solution)/shard_map/s1h7/ppermute | solution.py:479
  99.8 7.9 %collective-permute-start.29 = (bf16[128,1536]{1,0:T(8,128)(2,1)S(1)}, bf16[128,1536]{1,0:T(8,128)(2,1)S(1)}, u32[]{:S(2)}, u32[]{:S(2)}) collective-permute-start(bf16[128,1536]{1,0:T(8,128)(2,1)S(1)} %pad_maximum_fusion.5), channel_id=1, source_target_pairs={{0,1},{1,0},{2,3},{3,2},{4,5},{5,4},{6,7},{7,6},{8,24},{9,25},{10,... | collective-permute-start | bytes 1179656 | tf_op jit(solution)/shard_map/s3h7/ppermute | solution.py:479
  103.4 6.9 %collective-permute-start.28 = (bf16[256,2560]{1,0:T(8,128)(2,1)S(1)}, bf16[256,2560]{1,0:T(8,128)(2,1)S(1)}, u32[]{:S(2)}, u32[]{:S(2)}) collective-permute-start(bf16[256,2560]{1,0:T(8,128)(2,1)S(1)} %pad_maximum_fusion.refs_0_), channel_id=1, source_target_pairs={{0,8},{1,9},{2,10},{3,11},{4,12},{5,13},{6,14},{7,15},{8,0},{9,1},... | collective-permute-start | bytes 3932168 | tf_op jit(solution)/shard_map/s2h8/ppermute | solution.py:479
  106.1 4.1 %collective-permute-start.27 = (bf16[1024,512]{1,0:T(8,128)(2,1)S(1)}, bf16[1024,512]{1,0:T(8,128)(2,1)S(1)}, u32[]{:S(2)}, u32[]{:S(2)}) collective-permute-start(bf16[1024,512]{1,0:T(8,128)(2,1)S(1)} %pad_maximum_fusion.1.refs_0_), channel_id=1, source_target_pairs={{0,8},{1,9},{2,10},{3,11},{4,12},{5,13},{6,14},{7,15},{8,0},{9,1},... | collective-permute-start | bytes 3145736 | tf_op jit(solution)/shard_map/s1h8/ppermute | solution.py:479
  107.8 2.5 %collective-permute-start.30 = (bf16[260,1536]{1,0:T(8,128)(2,1)S(1)}, bf16[260,1536]{1,0:T(8,128)(2,1)S(1)}, u32[]{:S(2)}, u32[]{:S(2)}) collective-permute-start(bf16[260,1536]{1,0:T(8,128)(2,1)S(1)} %fusion.refs_0_.refs_3_), channel_id=1, source_target_pairs={{0,8},{1,9},{2,10},{3,11},{4,12},{5,13},{6,14},{7,15},{8,0},{9,1},... | collective-permute-start | bytes 2396168 | tf_op jit(solution)/shard_map/s3h8/ppermute | solution.py:479

commit v6 on v5

--- a/solution.py
+++ b/solution.py
@@ -17,7 +17,7 @@
 SQRT_HALF = 0.5**0.5
 PHI_SCALE = (2.0 * math.pi) ** (-0.5)
 NEGATIVE = -1e30
-CUT = 1024
+CUT = 2048
 PACE = 2
 ORDERS = (("zxyw", "xyzw"), ("yzxw", "zywx"), ("yxzw", "xyzw"))
 ORDER = (2, 3, 1, 3, 2, 1, 3, 2, 1, 3, 2, 1, 3, 2, 1, 2, 3, 1, 2, 3, 1, 3, 2, 1, 3, 2, 1, 3)
@@ -183,8 +183,8 @@
     branch = jnp.zeros((rows, width), f32)
     dc = jnp.zeros((rows, width), f32)
     b1_row = as_row(b1)
-    for start in range(0, hidden, 1024):
-        cols = slice(start, start + 1024)
+    for start in range(0, hidden, 2048):
+        cols = slice(start, start + 2048)
         u = dot_nn(c_low, w1[:, cols]) + b1_row[:, cols]
         cdf = 0.5 + 0.5 * lax.erf(u * SQRT_HALF)
         slope = cdf + u * (jnp.exp(u * u * -0.5) * PHI_SCALE)

time: 114 us -> 114 us (level)
  no operation moved by 1% of the time
where the time goes in v6:
time: 114 us
  starting transfers between devices  46 us (40%)
  waiting for transfers between devices  36.4 us (32%)
  Pallas kernels  24.7 us (22%)
  other arithmetic  3.83 us (3%)
  local copies, waits for them, and re-layouts  1.41 us (1%)
    ppermute x29, starting transfers between devices, exchange(): return lax.ppermute(value, ('lat', 'items'), pairs)  44.5 us
    ppermute x29, waiting for transfers between devices, exchange(): return lax.ppermute(value, ('lat', 'items'), pairs)  36.4 us
    pallas_call x2, Pallas kernels, on_device(): pl.pallas_call(kernel, out_shape=[jax.ShapeDtypeStruct(shape, dtype) for...  17.2 us
    pallas_call x4, Pallas kernels, spread(): pl.pallas_call(functools.partial(spread_kernel, axes, shards, streams, bo...  7.51 us
  transfers between devices with their start and end apart: 31, of which 14 were waited for; matrix products, arithmetic and copies ran while one was open for 3% of the time, Pallas kernels for 7%

profile of v6, /device:TPU:0, one launch (start us, length us, event | category | flops | bytes accessed | tf_op | source)
XLA Modules:
  0.0 113.6 jit_solution(18043304639733574503)
XLA Ops:
  0.7 1.0 broadcast_select_fusion
  1.6 0.5 collective-permute-start
  2.1 0.7 collective-permute-start.1
  3.1 0.6 copy-done.6
  3.8 13.5 %shard_map.245 = (bf16[192,512]{1,0:T(8,128)(2,1)}, bf16[192,512]{1,0:T(8,128)(2,1)}, f32[192,512]{1,0:T(8,128)}, f32[8,512]{1,0:T(8,128)}, bf16[1024,512]{1,0:T...) custom-call(bf16[192,512]{1,0:T(8,128)(2,1)} %bitcast.6, ...), custom_call_target="tpu_custom_call" | custom-call | flops 2818572288 | bytes 13791232 | tf_op jit(solution)/shard_map/pallas_call | solution.py:420
  17.2 5.9 %collective-permute-start.2 = (bf16[256,2560]{1,0:T(8,128)(2,1)}, bf16[256,2560]{1,0:T(8,128)(2,1)S(1)}, u32[]{:S(2)}, u32[]{:S(2)}) collective-permute-start(bf16[256,2560]{1,0:T(8,128)(2,1)} %get-tuple-element.73), channel_id=1, source_target_pairs={{0,8},{1,9},{2,10},{3,11},{4,12},{5,13},{6,14},{7,15},{8,0},{9,1},... | collective-permute-start | bytes 3932168 | tf_op jit(solution)/shard_map/s2h0/ppermute | solution.py:479
  23.2 0.8 collective-permute-start.4
  24.1 3.5 %collective-permute-start.5 = (bf16[1024,512]{1,0:T(8,128)(2,1)}, bf16[1024,512]{1,0:T(8,128)(2,1)S(1)}, u32[]{:S(2)}, u32[]{:S(2)}) collective-permute-start(bf16[1024,512]{1,0:T(8,128)(2,1)} %get-tuple-element.85), channel_id=1, source_target_pairs={{0,8},{1,9},{2,10},{3,11},{4,12},{5,13},{6,14},{7,15},{8,0},{9,1},... | collective-permute-start | bytes 3145736 | tf_op jit(solution)/shard_map/s1h0/ppermute | solution.py:479
  27.6 1.3 %add_convert_fusion = bf16[128,2560]{1,0:T(8,128)(2,1)S(1)} fusion(bf16[256,2560]{1,0:T(8,128)(2,1)S(1)} %collective-permute-done.2, bf16[256,2560]{1,0:T(8,128)(2,1)} %get-tuple-element.72), kind=kLoop, calls=%fused_computation.1 | loop fusion | flops 1310720 | bytes 1966080 | tf_op jit(solution)/shard_map/convert_element_type | solution.py:520
  28.9 0.7 copy-done.4
  29.6 3.8 %shard_map.246 = (bf16[256,1536]{1,0:T(8,128)(2,1)}, bf16[256,1536]{1,0:T(8,128)(2,1)}, bf16[192,512]{1,0:T(8,128)(2,1)}, bf16[4,1536]{1,0:T(4,128)(2,1)}) custom-call(bf16[192,512]{1,0:T(8,128)(2,1)} %get-tuple-element.76.refs_0_, f32[192,512]{1,0:T(8,128)} %get-tuple-element.77.refs_1_, f32[192,512]{1,0:T(8,128)} %get-tuple-element.78.refs_2_, ...), custom_call_target="tpu_custom_call" | custom-call | flops 603979776 | bytes 5534720 | tf_op jit(solution)/shard_map/pallas_call | solution.py:420
  33.4 2.0 %collective-permute-start.8 = (bf16[256,1536]{1,0:T(8,128)(2,1)}, bf16[256,1536]{1,0:T(8,128)(2,1)S(1)}, u32[]{:S(2)}, u32[]{:S(2)}) collective-permute-start(bf16[256,1536]{1,0:T(8,128)(2,1)} %get-tuple-element.86), channel_id=1, source_target_pairs={{0,8},{1,9},{2,10},{3,11},{4,12},{5,13},{6,14},{7,15},{8,0},{9,1},... | collective-permute-start | bytes 2359304 | tf_op jit(solution)/shard_map/s3h0/ppermute | solution.py:479
  35.4 2.1 %collective-permute-start.7 = (bf16[128,2560]{1,0:T(8,128)(2,1)S(1)}, bf16[128,2560]{1,0:T(8,128)(2,1)S(1)}, u32[]{:S(2)}, u32[]{:S(2)}) collective-permute-start(bf16[128,2560]{1,0:T(8,128)(2,1)S(1)} %add_convert_fusion), channel_id=1, source_target_pairs={{0,1},{1,0},{2,3},{3,2},{4,5},{5,4},{6,7},{7,6},{8,10},{9,11},{10,... | collective-permute-start | bytes 1966088 | tf_op jit(solution)/shard_map/s2h1/ppermute | solution.py:479
  37.7 1.7 %collective-permute-start.6 = (bf16[512,512]{1,0:T(8,128)(2,1)S(1)}, bf16[512,512]{1,0:T(8,128)(2,1)S(1)}, u32[]{:S(2)}, u32[]{:S(2)}) collective-permute-start(bf16[512,512]{1,0:T(8,128)(2,1)S(1)} %add_convert_fusion.1), channel_id=1, source_target_pairs={{0,2},{1,3},{2,0},{3,1},{4,6},{5,7},{6,4},{7,5},{8,24},{9,25},{10,... | collective-permute-start | bytes 1572872 | tf_op jit(solution)/shard_map/s1h1/ppermute | solution.py:479
  39.5 0.6 collective-permute-start.11
  40.0 6.0 %collective-permute-done.7 = bf16[128,2560]{1,0:T(8,128)(2,1)S(1)} collective-permute-done((bf16[128,2560]{1,0:T(8,128)(2,1)S(1)}, bf16[128,2560]{1,0:T(8,128)(2,1)S(1)}, u32[]{:S(2)}, u32[]{:S(2)}) %collective-permute-start.7) | collective-permute-done | bytes 655392 | tf_op jit(solution)/shard_map/s2h1/ppermute | solution.py:479
  46.2 2.2 %collective-permute-start.10 = (bf16[64,2560]{1,0:T(8,128)(2,1)S(1)}, bf16[64,2560]{1,0:T(8,128)(2,1)S(1)}, u32[]{:S(2)}, u32[]{:S(2)}) collective-permute-start(bf16[64,2560]{1,0:T(8,128)(2,1)S(1)} %add_convert_fusion.3), channel_id=1, source_target_pairs={{0,2},{1,3},{2,0},{3,1},{4,6},{5,7},{6,4},{7,5},{8,9},{9,8},{10,11... | collective-permute-start | bytes 983048 | tf_op jit(solution)/shard_map/s2h2/ppermute | solution.py:479
  48.4 2.8 %collective-permute-done.6 = bf16[512,512]{1,0:T(8,128)(2,1)S(1)} collective-permute-done((bf16[512,512]{1,0:T(8,128)(2,1)S(1)}, bf16[512,512]{1,0:T(8,128)(2,1)S(1)}, u32[]{:S(2)}, u32[]{:S(2)}) %collective-permute-start.6) | collective-permute-done | bytes 524320 | tf_op jit(solution)/shard_map/s1h1/ppermute | solution.py:479
  51.3 1.7 %collective-permute-start.9 = (bf16[256,512]{1,0:T(8,128)(2,1)S(1)}, bf16[256,512]{1,0:T(8,128)(2,1)S(1)}, u32[]{:S(2)}, u32[]{:S(2)}) collective-permute-start(bf16[256,512]{1,0:T(8,128)(2,1)S(1)} %add_convert_fusion.4), channel_id=1, source_target_pairs={{0,16},{1,17},{2,18},{3,19},{4,20},{5,21},{6,22},{7,23},{8,9},{9,8... | collective-permute-start | bytes 786440 | tf_op jit(solution)/shard_map/s1h2/ppermute | solution.py:479
  53.0 0.5 collective-permute-start.14
  53.5 1.1 collective-permute-done.10
  54.7 1.7 %collective-permute-start.13 = (bf16[32,2560]{1,0:T(8,128)(2,1)S(1)}, bf16[32,2560]{1,0:T(8,128)(2,1)S(1)}, u32[]{:S(2)}, u32[]{:S(2)}) collective-permute-start(bf16[32,2560]{1,0:T(8,128)(2,1)S(1)} %add_convert_fusion.8), channel_id=1, source_target_pairs={{0,16},{1,17},{2,18},{3,19},{4,20},{5,21},{6,22},{7,23},{8,12},{9,... | collective-permute-start | bytes 491528 | tf_op jit(solution)/shard_map/s2h3/ppermute | solution.py:479
  56.4 1.3 %collective-permute-done.9 = bf16[256,512]{1,0:T(8,128)(2,1)S(1)} collective-permute-done((bf16[256,512]{1,0:T(8,128)(2,1)S(1)}, bf16[256,512]{1,0:T(8,128)(2,1)S(1)}, u32[]{:S(2)}, u32[]{:S(2)}) %collective-permute-start.9) | collective-permute-done | bytes 262176 | tf_op jit(solution)/shard_map/s1h2/ppermute | solution.py:479
  57.8 1.5 %collective-permute-start.12 = (bf16[128,512]{1,0:T(8,128)(2,1)S(1)}, bf16[128,512]{1,0:T(8,128)(2,1)S(1)}, u32[]{:S(2)}, u32[]{:S(2)}) collective-permute-start(bf16[128,512]{1,0:T(8,128)(2,1)S(1)} %add_convert_fusion.11), channel_id=1, source_target_pairs={{0,1},{1,0},{2,3},{3,2},{4,5},{5,4},{6,7},{7,6},{8,10},{9,11},{10,... | collective-permute-start | bytes 393224 | tf_op jit(solution)/shard_map/s1h3/ppermute | solution.py:479
  59.3 0.8 collective-permute-done.14
  60.2 1.8 %collective-permute-start.17 = (bf16[36,1536]{1,0:T(8,128)(2,1)S(1)}, bf16[36,1536]{1,0:T(8,128)(2,1)S(1)}, u32[]{:S(2)}, u32[]{:S(2)}) collective-permute-start(bf16[36,1536]{1,0:T(8,128)(2,1)S(1)} %pad_maximum_fusion.10), channel_id=1, source_target_pairs={{0,2},{1,3},{2,0},{3,1},{4,6},{5,7},{6,4},{7,5},{8,10},{9,11},{10,... | collective-permute-start | bytes 331784 | tf_op jit(solution)/shard_map/s3h3/ppermute | solution.py:479
  62.1 2.7 %collective-permute-start.16 = (bf16[32,2560]{1,0:T(8,128)(2,1)S(1)}, bf16[32,2560]{1,0:T(8,128)(2,1)S(1)}, u32[]{:S(2)}, u32[]{:S(2)}) collective-permute-start(bf16[32,2560]{1,0:T(8,128)(2,1)S(1)} %add_convert_fusion.7), channel_id=1, source_target_pairs={{0,4},{1,5},{2,6},{3,7},{4,0},{5,1},{6,2},{7,3},{8,24},{9,25},{10,... | collective-permute-start | bytes 491528 | tf_op jit(solution)/shard_map/s2h4/ppermute | solution.py:479
  64.8 1.7 %collective-permute-start.15 = (bf16[128,512]{1,0:T(8,128)(2,1)S(1)}, bf16[128,512]{1,0:T(8,128)(2,1)S(1)}, u32[]{:S(2)}, u32[]{:S(2)}) collective-permute-start(bf16[128,512]{1,0:T(8,128)(2,1)S(1)} %add_convert_fusion.10), channel_id=1, source_target_pairs={{0,4},{1,5},{2,6},{3,7},{4,0},{5,1},{6,2},{7,3},{8,12},{9,13},{10,... | collective-permute-start | bytes 393224 | tf_op jit(solution)/shard_map/s1h4/ppermute | solution.py:479
  66.6 2.2 %collective-permute-done.17 = bf16[36,1536]{1,0:T(8,128)(2,1)S(1)} collective-permute-done((bf16[36,1536]{1,0:T(8,128)(2,1)S(1)}, bf16[36,1536]{1,0:T(8,128)(2,1)S(1)}, u32[]{:S(2)}, u32[]{:S(2)}) %collective-permute-start.17) | collective-permute-done | bytes 110624 | tf_op jit(solution)/shard_map/s3h3/ppermute | solution.py:479
  69.6 1.6 %collective-permute-start.20 = (bf16[32,2560]{1,0:T(8,128)(2,1)S(1)}, bf16[32,2560]{1,0:T(8,128)(2,1)S(1)}, u32[]{:S(2)}, u32[]{:S(2)}) collective-permute-start(bf16[32,2560]{1,0:T(8,128)(2,1)S(1)} %add_convert_fusion.6), channel_id=1, source_target_pairs={{0,16},{1,17},{2,18},{3,19},{4,20},{5,21},{6,22},{7,23},{8,12},{9,... | collective-permute-start | bytes 491528 | tf_op jit(solution)/shard_map/s2h5/ppermute | solution.py:479
  71.2 8.4 %collective-permute-done.15 = bf16[128,512]{1,0:T(8,128)(2,1)S(1)} collective-permute-done((bf16[128,512]{1,0:T(8,128)(2,1)S(1)}, bf16[128,512]{1,0:T(8,128)(2,1)S(1)}, u32[]{:S(2)}, u32[]{:S(2)}) %collective-permute-start.15) | collective-permute-done | bytes 131104 | tf_op jit(solution)/shard_map/s1h4/ppermute | solution.py:479
  79.6 1.4 %collective-permute-start.18 = (bf16[128,512]{1,0:T(8,128)(2,1)S(1)}, bf16[128,512]{1,0:T(8,128)(2,1)S(1)}, u32[]{:S(2)}, u32[]{:S(2)}) collective-permute-start(bf16[128,512]{1,0:T(8,128)(2,1)S(1)} %add_convert_fusion.9), channel_id=1, source_target_pairs={{0,1},{1,0},{2,3},{3,2},{4,5},{5,4},{6,7},{7,6},{8,10},{9,11},{10,... | collective-permute-start | bytes 393224 | tf_op jit(solution)/shard_map/s1h5/ppermute | solution.py:479
  81.0 3.5 %collective-permute-start.23 = (bf16[64,2560]{1,0:T(8,128)(2,1)S(1)}, bf16[64,2560]{1,0:T(8,128)(2,1)S(1)}, u32[]{:S(2)}, u32[]{:S(2)}) collective-permute-start(bf16[64,2560]{1,0:T(8,128)(2,1)S(1)} %pad_maximum_fusion.6), channel_id=1, source_target_pairs={{0,2},{1,3},{2,0},{3,1},{4,6},{5,7},{6,4},{7,5},{8,9},{9,8},{10,11... | collective-permute-start | bytes 983048 | tf_op jit(solution)/shard_map/s2h6/ppermute | solution.py:479
  84.7 1.5 %collective-permute-start.21 = (bf16[256,512]{1,0:T(8,128)(2,1)S(1)}, bf16[256,512]{1,0:T(8,128)(2,1)S(1)}, u32[]{:S(2)}, u32[]{:S(2)}) collective-permute-start(bf16[256,512]{1,0:T(8,128)(2,1)S(1)} %pad_maximum_fusion.7), channel_id=1, source_target_pairs={{0,16},{1,17},{2,18},{3,19},{4,20},{5,21},{6,22},{7,23},{8,9},{9,8... | collective-permute-start | bytes 786440 | tf_op jit(solution)/shard_map/s1h6/ppermute | solution.py:479
  86.2 4.5 %collective-permute-done.23 = bf16[64,2560]{1,0:T(8,128)(2,1)S(1)} collective-permute-done((bf16[64,2560]{1,0:T(8,128)(2,1)S(1)}, bf16[64,2560]{1,0:T(8,128)(2,1)S(1)}, u32[]{:S(2)}, u32[]{:S(2)}) %collective-permute-start.23) | collective-permute-done | bytes 327712 | tf_op jit(solution)/shard_map/s2h6/ppermute | solution.py:479
  90.7 1.5 %collective-permute-start.25 = (bf16[128,2560]{1,0:T(8,128)(2,1)S(1)}, bf16[128,2560]{1,0:T(8,128)(2,1)S(1)}, u32[]{:S(2)}, u32[]{:S(2)}) collective-permute-start(bf16[128,2560]{1,0:T(8,128)(2,1)S(1)} %pad_maximum_fusion.2), channel_id=1, source_target_pairs={{0,1},{1,0},{2,3},{3,2},{4,5},{5,4},{6,7},{7,6},{8,10},{9,11},{10,... | collective-permute-start | bytes 1966088 | tf_op jit(solution)/shard_map/s2h7/ppermute | solution.py:479
  92.2 1.4 %collective-permute-start.26 = (bf16[64,1536]{1,0:T(8,128)(2,1)S(1)}, bf16[64,1536]{1,0:T(8,128)(2,1)S(1)}, u32[]{:S(2)}, u32[]{:S(2)}) collective-permute-start(bf16[64,1536]{1,0:T(8,128)(2,1)S(1)} %pad_maximum_fusion.9), channel_id=1, source_target_pairs={{0,16},{1,17},{2,18},{3,19},{4,20},{5,21},{6,22},{7,23},{8,9},{9,8... | collective-permute-start | bytes 589832 | tf_op jit(solution)/shard_map/s3h6/ppermute | solution.py:479
  93.6 1.4 %collective-permute-start.24 = (bf16[512,512]{1,0:T(8,128)(2,1)S(1)}, bf16[512,512]{1,0:T(8,128)(2,1)S(1)}, u32[]{:S(2)}, u32[]{:S(2)}) collective-permute-start(bf16[512,512]{1,0:T(8,128)(2,1)S(1)} %pad_maximum_fusion.3), channel_id=1, source_target_pairs={{0,2},{1,3},{2,0},{3,1},{4,6},{5,7},{6,4},{7,5},{8,24},{9,25},{10,... | collective-permute-start | bytes 1572872 | tf_op jit(solution)/shard_map/s1h7/ppermute | solution.py:479
  95.0 4.8 %collective-permute-done.26 = bf16[64,1536]{1,0:T(8,128)(2,1)S(1)} collective-permute-done((bf16[64,1536]{1,0:T(8,128)(2,1)S(1)}, bf16[64,1536]{1,0:T(8,128)(2,1)S(1)}, u32[]{:S(2)}, u32[]{:S(2)}) %collective-permute-start.26) | collective-permute-done | bytes 196640 | tf_op jit(solution)/shard_map/s3h6/ppermute | solution.py:479
  99.9 0.5 collective-permute-start.29
  100.4 3.0 %collective-permute-done.25 = bf16[128,2560]{1,0:T(8,128)(2,1)S(1)} collective-permute-done((bf16[128,2560]{1,0:T(8,128)(2,1)S(1)}, bf16[128,2560]{1,0:T(8,128)(2,1)S(1)}, u32[]{:S(2)}, u32[]{:S(2)}) %collective-permute-start.25) | collective-permute-done | bytes 655392 | tf_op jit(solution)/shard_map/s2h7/ppermute | solution.py:479
  103.4 0.6 collective-permute-start.28
  104.0 1.7 %shard_map.247 = (f32[512,2048]{1,0:T(8,128)}, f32[512,512]{1,0:T(8,128)}) custom-call(bf16[256,2560]{1,0:T(8,128)(2,1)S(1)} %pad_maximum_fusion.refs_0_), custom_call_target="tpu_custom_call" | custom-call | bytes 3932160 | tf_op jit(solution)/shard_map/pallas_call | solution.py:398
  106.3 1.5 %shard_map.248.refs_4_ = f32[2048,512]{1,0:T(8,128)} custom-call(bf16[1024,512]{1,0:T(8,128)(2,1)S(1)} %pad_maximum_fusion.1.refs_0_), custom_call_target="tpu_custom_call" | custom-call | bytes 3145728 | tf_op jit(solution)/shard_map/pallas_call | solution.py:398
  107.9 0.6 collective-permute-start.30
  108.4 1.3 %shard_map.249.refs_7_ = f32[512,1536]{1,0:T(8,128)} custom-call(bf16[260,1536]{1,0:T(8,128)(2,1)S(1)} %fusion.refs_0_.refs_3_), custom_call_target="tpu_custom_call" | custom-call | bytes 2359296 | tf_op jit(solution)/shard_map/pallas_call | solution.py:398
  109.7 0.6 collective-permute-done.30.refs_2_
  110.4 3.0 %shard_map.250 = (f32[2048,512]{1,0:T(8,128)}, f32[512,2048]{1,0:T(8,128)}, f32[512,512]{1,0:T(8,128)}, f32[512,1536]{1,0:T(8,128)}, f32[512]{0:T(512)}, /*index...) custom-call(bf16[1024,512]{1,0:T(8,128)(2,1)S(1)} %collective-permut, ...), custom_call_target="tpu_custom_call", output_to_operand_aliasing={{0}: (4, {}), {1}: (5, {}), {2}: (6, {}), {3}: (7, {})} | custom-call | bytes 9437184 | tf_op jit(solution)/shard_map/pallas_call | solution.py:398
  (71 shorter events, 3.3 us)
Async XLA Ops:
  1.6 1.5 %collective-permute-start = (bf16[96,512]{1,0:T(8,128)(2,1)S(1)}, bf16[96,512]{1,0:T(8,128)(2,1)S(1)}, u32[]{:S(2)}, u32[]{:S(2)}) collective-permute-start(bf16[96,512]{1,0:T(8,128)(2,1)S(1)} %bitcast.9), channel_id=1, source_target_pairs={{0,8},{1,9},{2,10},{3,11},{4,12},{5,13},{6,14},{7,15},{8,0},{9,1},... | collective-permute-start | bytes 294920 | tf_op jit(solution)/shard_map/ppermute | solution.py:479
  2.1 0.9 collective-permute-start.1
  3.1 0.6 copy-start.6
  3.1 0.7 copy-start.7
  17.2 10.3 %collective-permute-start.2 = (bf16[256,2560]{1,0:T(8,128)(2,1)}, bf16[256,2560]{1,0:T(8,128)(2,1)S(1)}, u32[]{:S(2)}, u32[]{:S(2)}) collective-permute-start(bf16[256,2560]{1,0:T(8,128)(2,1)} %get-tuple-element.73), channel_id=1, source_target_pairs={{0,8},{1,9},{2,10},{3,11},{4,12},{5,13},{6,14},{7,15},{8,0},{9,1},... | collective-permute-start | bytes 3932168 | tf_op jit(solution)/shard_map/s2h0/ppermute | solution.py:479
  23.2 4.4 %collective-permute-start.3 = (bf16[2,96,512]{2,1,0:T(8,128)(2,1)}, bf16[2,96,512]{2,1,0:T(8,128)(2,1)S(1)}, u32[]{:S(2)}, u32[]{:S(2)}) collective-permute-start(bf16[2,96,512]{2,1,0:T(8,128)(2,1)} %get-tuple-element.74), channel_id=1, source_target_pairs={{0,8},{1,9},{2,10},{3,11},{4,12},{5,13},{6,14},{7,15},{8,0},{9,1},... | collective-permute-start | bytes 589832 | tf_op jit(solution)/shard_map/ppermute | solution.py:479
  23.2 5.6 %collective-permute-start.4 = (bf16[2,96,512]{2,1,0:T(8,128)(2,1)}, bf16[2,96,512]{2,1,0:T(8,128)(2,1)S(1)}, u32[]{:S(2)}, u32[]{:S(2)}) collective-permute-start(bf16[2,96,512]{2,1,0:T(8,128)(2,1)} %get-tuple-element.79), channel_id=1, source_target_pairs={{8,16},{16,8},{9,17},{17,9},{10,18},{18,10},{11,19},{19,11},{12,20... | collective-permute-start | bytes 589832 | tf_op jit(solution)/shard_map/ppermute | solution.py:471
  24.1 13.4 %collective-permute-start.5 = (bf16[1024,512]{1,0:T(8,128)(2,1)}, bf16[1024,512]{1,0:T(8,128)(2,1)S(1)}, u32[]{:S(2)}, u32[]{:S(2)}) collective-permute-start(bf16[1024,512]{1,0:T(8,128)(2,1)} %get-tuple-element.85), channel_id=1, source_target_pairs={{0,8},{1,9},{2,10},{3,11},{4,12},{5,13},{6,14},{7,15},{8,0},{9,1},... | collective-permute-start | bytes 3145736 | tf_op jit(solution)/shard_map/s1h0/ppermute | solution.py:479
  27.6 1.3 %copy-start.3 = (bf16[2,96,512]{2,1,0:T(8,128)(2,1)}, bf16[2,96,512]{2,1,0:T(8,128)(2,1)S(1)}, u32[]{:S(2)}) copy-start(bf16[2,96,512]{2,1,0:T(8,128)(2,1)S(1)} %collective-permute-done.3.refs_3_) | copy-start | bytes 589828
  28.9 0.7 copy-start.4
  29.6 8.0 %copy-start.1 = (bf16[1024,512]{1,0:T(8,128)(2,1)S(1)}, bf16[1024,512]{1,0:T(8,128)(2,1)}, u32[]{:S(2)}) copy-start(bf16[1024,512]{1,0:T(8,128)(2,1)} %get-tuple-element.84) | copy-start | bytes 3145732
  33.3 6.0 %copy-start.2 = (bf16[256,1536]{1,0:T(8,128)(2,1)S(1)}, bf16[256,1536]{1,0:T(8,128)(2,1)}, u32[]{:S(2)}) copy-start(bf16[256,1536]{1,0:T(8,128)(2,1)} %get-tuple-element.88) | copy-start | bytes 2359300
  33.4 6.0 %collective-permute-start.8 = (bf16[256,1536]{1,0:T(8,128)(2,1)}, bf16[256,1536]{1,0:T(8,128)(2,1)S(1)}, u32[]{:S(2)}, u32[]{:S(2)}) collective-permute-start(bf16[256,1536]{1,0:T(8,128)(2,1)} %get-tuple-element.86), channel_id=1, source_target_pairs={{0,8},{1,9},{2,10},{3,11},{4,12},{5,13},{6,14},{7,15},{8,0},{9,1},... | collective-permute-start | bytes 2359304 | tf_op jit(solution)/shard_map/s3h0/ppermute | solution.py:479
  35.4 10.7 %collective-permute-start.7 = (bf16[128,2560]{1,0:T(8,128)(2,1)S(1)}, bf16[128,2560]{1,0:T(8,128)(2,1)S(1)}, u32[]{:S(2)}, u32[]{:S(2)}) collective-permute-start(bf16[128,2560]{1,0:T(8,128)(2,1)S(1)} %add_convert_fusion), channel_id=1, source_target_pairs={{0,1},{1,0},{2,3},{3,2},{4,5},{5,4},{6,7},{7,6},{8,10},{9,11},{10,... | collective-permute-start | bytes 1966088 | tf_op jit(solution)/shard_map/s2h1/ppermute | solution.py:479
  37.5 1.9 %copy-start.5 = (bf16[4,1536]{1,0:T(4,128)(2,1)S(1)}, bf16[4,1536]{1,0:T(4,128)(2,1)}, u32[]{:S(2)}) copy-start(bf16[4,1536]{1,0:T(4,128)(2,1)} %get-tuple-element.90) | copy-start | bytes 36868
  37.7 8.4 %copy-start = (bf16[256,2560]{1,0:T(8,128)(2,1)S(1)}, bf16[256,2560]{1,0:T(8,128)(2,1)}, u32[]{:S(2)}) copy-start(bf16[256,2560]{1,0:T(8,128)(2,1)} %get-tuple-element.72) | copy-start | bytes 3932164
  37.7 13.5 %collective-permute-start.6 = (bf16[512,512]{1,0:T(8,128)(2,1)S(1)}, bf16[512,512]{1,0:T(8,128)(2,1)S(1)}, u32[]{:S(2)}, u32[]{:S(2)}) collective-permute-start(bf16[512,512]{1,0:T(8,128)(2,1)S(1)} %add_convert_fusion.1), channel_id=1, source_target_pairs={{0,2},{1,3},{2,0},{3,1},{4,6},{5,7},{6,4},{7,5},{8,24},{9,25},{10,... | collective-permute-start | bytes 1572872 | tf_op jit(solution)/shard_map/s1h1/ppermute | solution.py:479
  39.5 13.4 %collective-permute-start.11 = (bf16[132,1536]{1,0:T(8,128)(2,1)S(1)}, bf16[132,1536]{1,0:T(8,128)(2,1)S(1)}, u32[]{:S(2)}, u32[]{:S(2)}) collective-permute-start(bf16[132,1536]{1,0:T(8,128)(2,1)S(1)} %pad_maximum_fusion.4), channel_id=1, source_target_pairs={{0,1},{1,0},{2,3},{3,2},{4,5},{5,4},{6,7},{7,6},{8,24},{9,25},{10,... | collective-permute-start | bytes 1216520 | tf_op jit(solution)/shard_map/s3h1/ppermute | solution.py:479
  46.2 8.5 %collective-permute-start.10 = (bf16[64,2560]{1,0:T(8,128)(2,1)S(1)}, bf16[64,2560]{1,0:T(8,128)(2,1)S(1)}, u32[]{:S(2)}, u32[]{:S(2)}) collective-permute-start(bf16[64,2560]{1,0:T(8,128)(2,1)S(1)} %add_convert_fusion.3), channel_id=1, source_target_pairs={{0,2},{1,3},{2,0},{3,1},{4,6},{5,7},{6,4},{7,5},{8,9},{9,8},{10,11... | collective-permute-start | bytes 983048 | tf_op jit(solution)/shard_map/s2h2/ppermute | solution.py:479
  51.3 6.4 %collective-permute-start.9 = (bf16[256,512]{1,0:T(8,128)(2,1)S(1)}, bf16[256,512]{1,0:T(8,128)(2,1)S(1)}, u32[]{:S(2)}, u32[]{:S(2)}) collective-permute-start(bf16[256,512]{1,0:T(8,128)(2,1)S(1)} %add_convert_fusion.4), channel_id=1, source_target_pairs={{0,16},{1,17},{2,18},{3,19},{4,20},{5,21},{6,22},{7,23},{8,9},{9,8... | collective-permute-start | bytes 786440 | tf_op jit(solution)/shard_map/s1h2/ppermute | solution.py:479
  53.0 7.0 %collective-permute-start.14 = (bf16[68,1536]{1,0:T(8,128)(2,1)S(1)}, bf16[68,1536]{1,0:T(8,128)(2,1)S(1)}, u32[]{:S(2)}, u32[]{:S(2)}) collective-permute-start(bf16[68,1536]{1,0:T(8,128)(2,1)S(1)} %pad_maximum_fusion.8), channel_id=1, source_target_pairs={{0,16},{1,17},{2,18},{3,19},{4,20},{5,21},{6,22},{7,23},{8,9},{9,8... | collective-permute-start | bytes 626696 | tf_op jit(solution)/shard_map/s3h2/ppermute | solution.py:479
  54.7 7.2 %collective-permute-start.13 = (bf16[32,2560]{1,0:T(8,128)(2,1)S(1)}, bf16[32,2560]{1,0:T(8,128)(2,1)S(1)}, u32[]{:S(2)}, u32[]{:S(2)}) collective-permute-start(bf16[32,2560]{1,0:T(8,128)(2,1)S(1)} %add_convert_fusion.8), channel_id=1, source_target_pairs={{0,16},{1,17},{2,18},{3,19},{4,20},{5,21},{6,22},{7,23},{8,12},{9,... | collective-permute-start | bytes 491528 | tf_op jit(solution)/shard_map/s2h3/ppermute | solution.py:479
  57.8 7.0 %collective-permute-start.12 = (bf16[128,512]{1,0:T(8,128)(2,1)S(1)}, bf16[128,512]{1,0:T(8,128)(2,1)S(1)}, u32[]{:S(2)}, u32[]{:S(2)}) collective-permute-start(bf16[128,512]{1,0:T(8,128)(2,1)S(1)} %add_convert_fusion.11), channel_id=1, source_target_pairs={{0,1},{1,0},{2,3},{3,2},{4,5},{5,4},{6,7},{7,6},{8,10},{9,11},{10,... | collective-permute-start | bytes 393224 | tf_op jit(solution)/shard_map/s1h3/ppermute | solution.py:479
  60.2 8.7 %collective-permute-start.17 = (bf16[36,1536]{1,0:T(8,128)(2,1)S(1)}, bf16[36,1536]{1,0:T(8,128)(2,1)S(1)}, u32[]{:S(2)}, u32[]{:S(2)}) collective-permute-start(bf16[36,1536]{1,0:T(8,128)(2,1)S(1)} %pad_maximum_fusion.10), channel_id=1, source_target_pairs={{0,2},{1,3},{2,0},{3,1},{4,6},{5,7},{6,4},{7,5},{8,10},{9,11},{10,... | collective-permute-start | bytes 331784 | tf_op jit(solution)/shard_map/s3h3/ppermute | solution.py:479
  62.1 7.5 %collective-permute-start.16 = (bf16[32,2560]{1,0:T(8,128)(2,1)S(1)}, bf16[32,2560]{1,0:T(8,128)(2,1)S(1)}, u32[]{:S(2)}, u32[]{:S(2)}) collective-permute-start(bf16[32,2560]{1,0:T(8,128)(2,1)S(1)} %add_convert_fusion.7), channel_id=1, source_target_pairs={{0,4},{1,5},{2,6},{3,7},{4,0},{5,1},{6,2},{7,3},{8,24},{9,25},{10,... | collective-permute-start | bytes 491528 | tf_op jit(solution)/shard_map/s2h4/ppermute | solution.py:479
  64.8 14.7 %collective-permute-start.15 = (bf16[128,512]{1,0:T(8,128)(2,1)S(1)}, bf16[128,512]{1,0:T(8,128)(2,1)S(1)}, u32[]{:S(2)}, u32[]{:S(2)}) collective-permute-start(bf16[128,512]{1,0:T(8,128)(2,1)S(1)} %add_convert_fusion.10), channel_id=1, source_target_pairs={{0,4},{1,5},{2,6},{3,7},{4,0},{5,1},{6,2},{7,3},{8,12},{9,13},{10,... | collective-permute-start | bytes 393224 | tf_op jit(solution)/shard_map/s1h4/ppermute | solution.py:479
  68.9 15.6 %collective-permute-start.19 = (bf16[36,1536]{1,0:T(8,128)(2,1)S(1)}, bf16[36,1536]{1,0:T(8,128)(2,1)S(1)}, u32[]{:S(2)}, u32[]{:S(2)}) collective-permute-start(bf16[36,1536]{1,0:T(8,128)(2,1)S(1)} %pad_maximum_fusion.11), channel_id=1, source_target_pairs={{0,4},{1,5},{2,6},{3,7},{4,0},{5,1},{6,2},{7,3},{8,12},{9,13},{10,... | collective-permute-start | bytes 331784 | tf_op jit(solution)/shard_map/s3h4/ppermute | solution.py:479
  69.6 11.3 %collective-permute-start.20 = (bf16[32,2560]{1,0:T(8,128)(2,1)S(1)}, bf16[32,2560]{1,0:T(8,128)(2,1)S(1)}, u32[]{:S(2)}, u32[]{:S(2)}) collective-permute-start(bf16[32,2560]{1,0:T(8,128)(2,1)S(1)} %add_convert_fusion.6), channel_id=1, source_target_pairs={{0,16},{1,17},{2,18},{3,19},{4,20},{5,21},{6,22},{7,23},{8,12},{9,... | collective-permute-start | bytes 491528 | tf_op jit(solution)/shard_map/s2h5/ppermute | solution.py:479
  79.6 5.1 %collective-permute-start.18 = (bf16[128,512]{1,0:T(8,128)(2,1)S(1)}, bf16[128,512]{1,0:T(8,128)(2,1)S(1)}, u32[]{:S(2)}, u32[]{:S(2)}) collective-permute-start(bf16[128,512]{1,0:T(8,128)(2,1)S(1)} %add_convert_fusion.9), channel_id=1, source_target_pairs={{0,1},{1,0},{2,3},{3,2},{4,5},{5,4},{6,7},{7,6},{8,10},{9,11},{10,... | collective-permute-start | bytes 393224 | tf_op jit(solution)/shard_map/s1h5/ppermute | solution.py:479
  81.0 9.6 %collective-permute-start.23 = (bf16[64,2560]{1,0:T(8,128)(2,1)S(1)}, bf16[64,2560]{1,0:T(8,128)(2,1)S(1)}, u32[]{:S(2)}, u32[]{:S(2)}) collective-permute-start(bf16[64,2560]{1,0:T(8,128)(2,1)S(1)} %pad_maximum_fusion.6), channel_id=1, source_target_pairs={{0,2},{1,3},{2,0},{3,1},{4,6},{5,7},{6,4},{7,5},{8,9},{9,8},{10,11... | collective-permute-start | bytes 983048 | tf_op jit(solution)/shard_map/s2h6/ppermute | solution.py:479
  84.6 7.6 %collective-permute-start.22 = (bf16[32,1536]{1,0:T(8,128)(2,1)S(1)}, bf16[32,1536]{1,0:T(8,128)(2,1)S(1)}, u32[]{:S(2)}, u32[]{:S(2)}) collective-permute-start(bf16[32,1536]{1,0:T(8,128)(2,1)S(1)} %get-tuple-element.127), channel_id=1, source_target_pairs={{0,2},{1,3},{2,0},{3,1},{4,6},{5,7},{6,4},{7,5},{8,10},{9,11},{10,... | collective-permute-start | bytes 294920 | tf_op jit(solution)/shard_map/s3h5/ppermute | solution.py:479
  84.7 8.9 %collective-permute-start.21 = (bf16[256,512]{1,0:T(8,128)(2,1)S(1)}, bf16[256,512]{1,0:T(8,128)(2,1)S(1)}, u32[]{:S(2)}, u32[]{:S(2)}) collective-permute-start(bf16[256,512]{1,0:T(8,128)(2,1)S(1)} %pad_maximum_fusion.7), channel_id=1, source_target_pairs={{0,16},{1,17},{2,18},{3,19},{4,20},{5,21},{6,22},{7,23},{8,9},{9,8... | collective-permute-start | bytes 786440 | tf_op jit(solution)/shard_map/s1h6/ppermute | solution.py:479
  90.7 12.7 %collective-permute-start.25 = (bf16[128,2560]{1,0:T(8,128)(2,1)S(1)}, bf16[128,2560]{1,0:T(8,128)(2,1)S(1)}, u32[]{:S(2)}, u32[]{:S(2)}) collective-permute-start(bf16[128,2560]{1,0:T(8,128)(2,1)S(1)} %pad_maximum_fusion.2), channel_id=1, source_target_pairs={{0,1},{1,0},{2,3},{3,2},{4,5},{5,4},{6,7},{7,6},{8,10},{9,11},{10,... | collective-permute-start | bytes 1966088 | tf_op jit(solution)/shard_map/s2h7/ppermute | solution.py:479
  92.2 7.6 %collective-permute-start.26 = (bf16[64,1536]{1,0:T(8,128)(2,1)S(1)}, bf16[64,1536]{1,0:T(8,128)(2,1)S(1)}, u32[]{:S(2)}, u32[]{:S(2)}) collective-permute-start(bf16[64,1536]{1,0:T(8,128)(2,1)S(1)} %pad_maximum_fusion.9), channel_id=1, source_target_pairs={{0,16},{1,17},{2,18},{3,19},{4,20},{5,21},{6,22},{7,23},{8,9},{9,8... | collective-permute-start | bytes 589832 | tf_op jit(solution)/shard_map/s3h6/ppermute | solution.py:479
  93.6 12.5 %collective-permute-start.24 = (bf16[512,512]{1,0:T(8,128)(2,1)S(1)}, bf16[512,512]{1,0:T(8,128)(2,1)S(1)}, u32[]{:S(2)}, u32[]{:S(2)}) collective-permute-start(bf16[512,512]{1,0:T(8,128)(2,1)S(1)} %pad_maximum_fusion.3), channel_id=1, source_target_pairs={{0,2},{1,3},{2,0},{3,1},{4,6},{5,7},{6,4},{7,5},{8,24},{9,25},{10,... | collective-permute-start | bytes 1572872 | tf_op jit(solution)/shard_map/s1h7/ppermute | solution.py:479
  99.9 7.9 %collective-permute-start.29 = (bf16[128,1536]{1,0:T(8,128)(2,1)S(1)}, bf16[128,1536]{1,0:T(8,128)(2,1)S(1)}, u32[]{:S(2)}, u32[]{:S(2)}) collective-permute-start(bf16[128,1536]{1,0:T(8,128)(2,1)S(1)} %pad_maximum_fusion.5), channel_id=1, source_target_pairs={{0,1},{1,0},{2,3},{3,2},{4,5},{5,4},{6,7},{7,6},{8,24},{9,25},{10,... | collective-permute-start | bytes 1179656 | tf_op jit(solution)/shard_map/s3h7/ppermute | solution.py:479
  103.4 6.9 %collective-permute-start.28 = (bf16[256,2560]{1,0:T(8,128)(2,1)S(1)}, bf16[256,2560]{1,0:T(8,128)(2,1)S(1)}, u32[]{:S(2)}, u32[]{:S(2)}) collective-permute-start(bf16[256,2560]{1,0:T(8,128)(2,1)S(1)} %pad_maximum_fusion.refs_0_), channel_id=1, source_target_pairs={{0,8},{1,9},{2,10},{3,11},{4,12},{5,13},{6,14},{7,15},{8,0},{9,1},... | collective-permute-start | bytes 3932168 | tf_op jit(solution)/shard_map/s2h8/ppermute | solution.py:479
  106.2 4.1 %collective-permute-start.27 = (bf16[1024,512]{1,0:T(8,128)(2,1)S(1)}, bf16[1024,512]{1,0:T(8,128)(2,1)S(1)}, u32[]{:S(2)}, u32[]{:S(2)}) collective-permute-start(bf16[1024,512]{1,0:T(8,128)(2,1)S(1)} %pad_maximum_fusion.1.refs_0_), channel_id=1, source_target_pairs={{0,8},{1,9},{2,10},{3,11},{4,12},{5,13},{6,14},{7,15},{8,0},{9,1},... | collective-permute-start | bytes 3145736 | tf_op jit(solution)/shard_map/s1h8/ppermute | solution.py:479
  107.9 2.5 %collective-permute-start.30 = (bf16[260,1536]{1,0:T(8,128)(2,1)S(1)}, bf16[260,1536]{1,0:T(8,128)(2,1)S(1)}, u32[]{:S(2)}, u32[]{:S(2)}) collective-permute-start(bf16[260,1536]{1,0:T(8,128)(2,1)S(1)} %fusion.refs_0_.refs_3_), channel_id=1, source_target_pairs={{0,8},{1,9},{2,10},{3,11},{4,12},{5,13},{6,14},{7,15},{8,0},{9,1},... | collective-permute-start | bytes 2396168 | tf_op jit(solution)/shard_map/s3h8/ppermute | solution.py:479
